TPU v7x, 256 devices: a whole 4x4x8 slice. The times are simulated.
256 devices in a mesh: lat: 8 (over z), lon: 32 (over x, y, core).
Axes of the slice: x: 4, y: 4, z: 8, core: 2. Of those that a mesh axis runs over, the one named last changes fastest.
Arguments:
- displacement: float32 [3, 32, 128, 512], P(None, 'lat', 'lon'), may hold values from -0.12 to 0.12
- velocity: float32 [3, 32, 128, 512], P(None, 'lat', 'lon'), may hold values from -6 to 6
- acceleration: float32 [3, 32, 128, 512], P(None, 'lat', 'lon'), may hold values from -6 to 6
- potential: float32 [32, 128, 512], P('lat', 'lon'), may hold values from -0.6 to 0.6
- memory_vars: bfloat16 [3, 5, 5, 8, 5, 32, 5, 128], P(None, None, None, 'lat', None, 'lon'), may hold values from -0.59765625 to 0.59765625
- materials: int32 [8, 32, 128], P('lat', 'lon'), may hold values from 0 to 7
- shell_flags: int32 [8, 32, 128], P('lat', 'lon'), may hold values from 0 to 1, as said below
- moduli: float32 [8, 6, 6], replicated, as said below
- densities: float32 [8], replicated, may hold values from 1.5 to 4.5
- decay: float32 [3], replicated, may hold values from 0.3 to 0.95
- strength: float32 [3], replicated, may hold values from 0.1 to 0.5
Outputs:
- disp_new: float32 [3, 32, 128, 512], P(None, 'lat', 'lon')
- vel_new: float32 [3, 32, 128, 512], P(None, 'lat', 'lon')
- acc_new: float32 [3, 32, 128, 512], P(None, 'lat', 'lon')
- phi_new: float32 [32, 128, 512], P('lat', 'lon')
- memory_new: bfloat16 [3, 5, 5, 8, 5, 32, 5, 128], P(None, None, None, 'lat', None, 'lon')
Inputs may be any that keep to these rules, and one draw needn't show every extreme that they name: `shell_flags`: in every radial column of elements the flagged ones are the outermost ones along the radius, at least one. `moduli`: each material's table is symmetric, each diagonal entry larger than the sum of magnitudes of the rest of its row.
All inputs are finite; a program needn't handle non-finite values.
Results may differ from a plain program's by a relative error of at most 0.0013.
Values sent between devices are 32-bit elements; how exact they have to be, the bound alone decides.
No kernel may reach another device: no remote copies, remote signals or barrier semaphores. Data moves between devices by JAX's collectives and lax.ppermute only.
A program may use at most 128 MiB of HBM per device.

v0:
```python
import jax
import jax.numpy as jnp
import numpy as np
from jax import lax
from jax.sharding import PartitionSpec as P

ITERS = 3


time_step = 0.1
shell_stretch = 3.0
grav_coef = 1.0
highest = lax.Precision.HIGHEST


def shifted(array, axis, by):
    devices = lax.axis_size(axis)
    pairs = [(i, i + by) for i in range(devices) if 0 <= i + by < devices]
    return lax.ppermute(array, axis, pairs)


def from_behind(array, axis, by):
    devices = lax.axis_size(axis)
    return lax.ppermute(array, axis, [(i, (i + by) % devices) for i in range(devices)])


def gll_tables():
    points = np.array([-1.0, -np.sqrt(3.0 / 7.0), 0.0, np.sqrt(3.0 / 7.0), 1.0])
    weights = np.array([0.1, 49.0 / 90.0, 32.0 / 45.0, 49.0 / 90.0, 0.1])
    differ = points[:, None] - points[None, :] + np.eye(5)
    factors = np.prod(differ, axis=1)
    deriv_mat = factors[:, None] / factors[None, :] / differ * (1.0 - np.eye(5))
    deriv_mat = deriv_mat - np.eye(5) * np.sum(deriv_mat, axis=1)[:, None]
    cube = weights[:, None, None] * weights[None, :, None] * weights[None, None, :] * 0.125
    weight_cube = cube.reshape(1, 5, 1, 5, 1, 5, 1)
    return (
        jnp.asarray(deriv_mat, jnp.float32),
        jnp.asarray(deriv_mat.T, jnp.float32),
        jnp.asarray((deriv_mat**2).T, jnp.float32),
        jnp.asarray(weight_cube, jnp.float32),
    )


def contract(field_vals, matrix, direction):
    if direction == 0:
        return jnp.einsum("pa,caxbydz->cpxbydz", matrix, field_vals, precision=highest)
    if direction == 1:
        return jnp.einsum("pb,caxbydz->caxpydz", matrix, field_vals, precision=highest)
    return jnp.einsum("pd,caxbydz->caxbypz", matrix, field_vals, precision=highest)


def spread(values):
    return values[None, None, :, None, :, None, :]


def split_axis(array, dim_pos, elem_count):
    pieces = [
        lax.slice_in_dim(array, start, start + 4 * (elem_count - 1) + 1, 4, dim_pos)
        for start in range(5)
    ]
    return jnp.stack(pieces, dim_pos)


def to_elements(extended):
    values = split_axis(extended, 1, (extended.shape[1] - 1) // 4)
    values = split_axis(values, 3, (extended.shape[2] - 1) // 4)
    return split_axis(values, 5, (extended.shape[3] - 1) // 4)


def merge_axis(values, dim_pos):
    leading = lax.slice_in_dim(values, 0, 4, 1, dim_pos)
    trailing = jnp.concatenate(
        [
            jnp.zeros_like(lax.slice_in_dim(values, 0, 3, 1, dim_pos)),
            lax.slice_in_dim(values, 4, 5, 1, dim_pos),
        ],
        dim_pos,
    )

    def alternate(block):
        block = jnp.swapaxes(block, dim_pos, dim_pos + 1)
        block_shape = block.shape
        return block.reshape(
            block_shape[:dim_pos] + (block_shape[dim_pos] * 4,) + block_shape[dim_pos + 2 :]
        )

    widths_end = [(0, 0)] * (values.ndim - 1)
    widths_front = [(0, 0)] * (values.ndim - 1)
    widths_end[dim_pos] = (0, 1)
    widths_front[dim_pos] = (1, 0)
    return jnp.pad(alternate(leading), widths_end) + jnp.pad(alternate(trailing), widths_front)


def to_points(values):
    values = merge_axis(values, 5)
    values = merge_axis(values, 3)
    return merge_axis(values, 1)


def grad_three(values, z_scale, tables):
    return (
        2.0 * contract(values, tables[0], 0),
        2.0 * contract(values, tables[0], 1),
        z_scale * contract(values, tables[0], 2),
    )


def div_three(flux_x, flux_y, flux_z, z_scale, tables):
    return (
        2.0 * contract(flux_x, tables[1], 0)
        + 2.0 * contract(flux_y, tables[1], 1)
        + z_scale * contract(flux_z, tables[1], 2)
    )


def shell_geometry(shell_flags):
    stretch = 1.0 + (shell_stretch - 1.0) * spread(shell_flags.astype(jnp.float32))
    return (stretch, 2.0 / stretch)


def poisson_elements(values, shell_flags, tables):
    stretch, z_scale = shell_geometry(shell_flags)
    volume = tables[3] * stretch
    grad_x, grad_y, grad_z = grad_three(values, z_scale, tables)
    return div_three(volume * grad_x, volume * grad_y, volume * grad_z, z_scale, tables)


def density_lookup(materials, densities):
    onehot = (materials[..., None] == jnp.arange(densities.shape[0], dtype=jnp.int32)).astype(
        jnp.float32
    )
    return (onehot, jnp.einsum("xyzm,m->xyz", onehot, densities, precision=highest))


def first_block(
    extended, materials, shell_flags, memory_vars, moduli, densities, decay, strength, tables
):
    values = to_elements(extended)
    displaced = values[0:3]
    potential_vals = values[3:4]
    onehot, density = density_lookup(materials, densities)
    stiffness = jnp.einsum("xyzm,mkl->klxyz", onehot, moduli, precision=highest)
    weight_cube = tables[3]
    grad_x, grad_y, grad_z = grad_three(displaced, 2.0, tables)
    strain = jnp.stack(
        [
            grad_x[0],
            grad_y[1],
            grad_z[2],
            grad_y[0] + grad_x[1],
            grad_z[0] + grad_x[2],
            grad_z[1] + grad_y[2],
        ]
    )
    elastic = jnp.einsum("klxyz,laxbydz->kaxbydz", stiffness, strain, precision=highest)
    pressure = (elastic[0] + elastic[1] + elastic[2]) / 3.0
    deviator = jnp.stack(
        [elastic[0] - pressure, elastic[1] - pressure, elastic[3], elastic[4], elastic[5]]
    )
    decay_rate = decay.reshape(-1, 1, 1, 1, 1, 1, 1, 1)
    gain_rate = strength.reshape(-1, 1, 1, 1, 1, 1, 1, 1)
    memory_new = (
        decay_rate * memory_vars.astype(jnp.float32)
        + (1.0 - decay_rate) * gain_rate * deviator[None]
    ).astype(jnp.bfloat16)
    memory_new = lax.optimization_barrier(memory_new)
    relaxed = jnp.sum(memory_new.astype(jnp.float32), 0)
    stress = [
        elastic[0] - relaxed[0],
        elastic[1] - relaxed[1],
        elastic[2] + relaxed[0] + relaxed[1],
        elastic[3] - relaxed[2],
        elastic[4] - relaxed[3],
        elastic[5] - relaxed[4],
    ]
    flux_x = weight_cube * jnp.stack([stress[0], stress[3], stress[4]])
    flux_y = weight_cube * jnp.stack([stress[3], stress[1], stress[5]])
    flux_z = weight_cube * jnp.stack([stress[4], stress[5], stress[2]])
    elastic_force = div_three(flux_x, flux_y, flux_z, 2.0, tables)
    mass_vals = weight_cube * spread(density)
    carried = weight_cube * spread(density * (1.0 - shell_flags.astype(jnp.float32))) * displaced
    source = -grav_coef * div_three(carried[0:1], carried[1:2], carried[2:3], 2.0, tables)
    stretch, z_scale = shell_geometry(shell_flags)
    volume = weight_cube * stretch
    precond = (
        4.0 * contract(volume, tables[2], 0)
        + 4.0 * contract(volume, tables[2], 1)
        + z_scale * z_scale * contract(volume, tables[2], 2)
    )
    poisson_vals = poisson_elements(potential_vals, shell_flags, tables)
    joined = jnp.concatenate([elastic_force, source, mass_vals, precond, poisson_vals], 0)
    return (to_points(joined), memory_new)


def gravity_block(extended, materials, shell_flags, densities, tables):
    values = to_elements(extended)
    onehot, density = density_lookup(materials, densities)
    stretch, z_scale = shell_geometry(shell_flags)
    grad_x, grad_y, grad_z = grad_three(values, z_scale, tables)
    coefficient = -tables[3] * spread(density)
    return to_points(
        jnp.concatenate([coefficient * grad_x, coefficient * grad_y, coefficient * grad_z], 0)
    )


def extend(fields):
    upper_plane = shifted(fields[:, :1], "lat", -1)
    extended = jnp.concatenate([fields, upper_plane], 1)
    side_plane = from_behind(extended[:, :, :1], "lon", -1)
    extended = jnp.concatenate([extended, side_plane], 2)
    return jnp.pad(extended, ((0, 0), (0, 0), (0, 0), (0, 1)))


def assemble(contrib):
    trimmed = contrib[..., :-1]
    carried_lon = from_behind(trimmed[:, :, -1:], "lon", 1)
    main_part = trimmed[:, :, :-1]
    main_part = jnp.concatenate([main_part[:, :, :1] + carried_lon, main_part[:, :, 1:]], 2)
    carried_lat = shifted(main_part[:, -1:], "lat", 1)
    row_part = main_part[:, :-1]
    return jnp.concatenate([row_part[:, :1] + carried_lat, row_part[:, 1:]], 1)


def precond_inner(residual, precond_res):
    return lax.psum(jnp.sum(residual * precond_res), ("lat", "lon"))


def per_device(
    displacement,
    velocity,
    acceleration,
    potential,
    memory_vars,
    materials,
    shell_flags,
    moduli,
    densities,
    decay,
    strength,
):
    tables = gll_tables()
    disp_new = displacement + time_step * velocity + 0.5 * time_step * time_step * acceleration
    extended = extend(jnp.concatenate([disp_new, potential[None]], 0))
    contrib, memory_new = first_block(
        extended, materials, shell_flags, memory_vars, moduli, densities, decay, strength, tables
    )
    assembled = assemble(contrib)
    phi_now = potential
    source = assembled[3]
    kpotential = assembled[6]
    precond = assembled[5]
    residual = source - kpotential
    precond_res = residual / precond
    rz_now = precond_inner(residual, precond_res)
    search_dir = precond_res
    for step in range(ITERS):
        values = to_elements(extend(search_dir[None]))
        image_dir = assemble(to_points(poisson_elements(values, shell_flags, tables)))[0]
        step_len = rz_now / lax.psum(jnp.sum(search_dir * image_dir), ("lat", "lon"))
        phi_now = phi_now + step_len * search_dir
        residual = residual - step_len * image_dir
        if step + 1 < ITERS:
            precond_res = residual / precond
            rz_next = precond_inner(residual, precond_res)
            search_dir = precond_res + rz_next / rz_now * search_dir
            rz_now = rz_next
    gravity = assemble(
        gravity_block(extend(phi_now[None]), materials, shell_flags, densities, tables)
    )
    elastic_force = assembled[0:3]
    mass_diag = assembled[4]
    acc_new = (gravity - elastic_force) / mass_diag[None]
    vel_new = velocity + 0.5 * time_step * (acceleration + acc_new)
    return (disp_new, vel_new, acc_new, phi_now, memory_new)


def solution(mesh):
    placed = (
        P(None, "lat", "lon", None),
        P(None, "lat", "lon", None),
        P(None, "lat", "lon", None),
        P("lat", "lon", None),
        P(None, None, None, "lat", None, "lon", None, None),
        P("lat", "lon", None),
        P("lat", "lon", None),
        P(),
        P(),
        P(),
        P(),
    )
    return jax.shard_map(
        per_device,
        mesh=mesh,
        in_specs=placed,
        out_specs=(
            P(None, "lat", "lon", None),
            P(None, "lat", "lon", None),
            P(None, "lat", "lon", None),
            P("lat", "lon", None),
            P(None, None, None, "lat", None, "lon", None, None),
        ),
        check_vma=False,
    )
```

profile of v0, /device:TPU:96, one launch (start us, length us, event | category | flops | bytes accessed | tf_op | source)
XLA Modules:
  0.0 652.8 jit_solution(13842447045403322362)
XLA Ops:
  33.6 7.3 %copy.1900 = f32[6,5,5,5,128]{0,3,2,1,4:T(8,128)} copy(f32[6,5,5,5,128]{4,1,3,2,0:T(8,128)S(1)} %bitcast.815) | data formatting | bytes 768000 | tf_op jit(solution)/shard_map/reshape.28
  40.9 23.4 %convolution_bitcast_fusion = f32[1,1,128,5,5,5,6]{6,5,4,3,2,1,0:T(8,128)} fusion(f32[6,5,5,5,128]{0,3,2,1,4:T(8,128)} %copy.1900, f32[6,6,128,1,1]{1,0,4,3,2:T(8,128)S(1)} %copy.2027), kind=kOutput, calls=%fused_computation | convolution fusion | flops 6912000 | bytes 786432 | tf_op jit(solution)/shard_map/klxyz,laxbydz->kaxbydz/dot_general | solution.py:155
  64.3 19.5 %copy.1903 = f32[1,1,128,5,5,5,6]{2,1,5,4,0,3,6:T(1,128)S(1)} copy(f32[1,1,128,5,5,5,6]{6,5,4,3,2,1,0:T(8,128)} %convolution_bitcast_fusion) | data formatting | bytes 768000 | tf_op jit(solution)/shard_map/klxyz,laxbydz->kaxbydz/dot_general | solution.py:155
  91.3 6.3 copy.2036
  97.5 11.2 %reshape.498 = f32[7,5,1,5,1,512]{5,1,3,0,4,2:T(8,128)S(1)} reshape(f32[7,5,1,5,1,128,4]{6,5,1,3,0,4,2:T(8,128)} %copy.2036) | data formatting | bytes 716800 | tf_op jit(solution)/shard_map/reshape | solution.py:83
  108.8 6.3 copy.2037
  115.0 11.2 %reshape.499 = f32[7,5,1,5,1,512]{5,1,3,0,4,2:T(8,128)S(1)} reshape(f32[7,5,1,5,1,128,4]{6,5,1,3,0,4,2:T(8,128)} %copy.2037) | data formatting | bytes 716800 | tf_op jit(solution)/shard_map/reshape | solution.py:83
  127.3 7.5 %collective-permute-done.2 = f32[7,5,1,512]{3,1,2,0:T(8,128)S(1)} collective-permute-done((f32[7,5,1,512]{3,1,2,0:T(8,128)S(1)}, f32[7,5,1,512]{3,1,2,0:T(8,128)S(1)}, u32[]{:S(2)}, u32[]{:S(2)}) %collective-permute-start.2) | collective-permute-done | bytes 71712 | tf_op jit(solution)/shard_map/ppermute | solution.py:24
  134.9 5.0 collective-permute-start.3
  143.9 5.2 collective-permute-done.4
  159.4 6.4 collective-permute-done.6
  172.1 73.2 %all-reduce.50 = (f32[]{:T(128)}, f32[]{:T(128)}) all-reduce(f32[]{:T(128)} %get-tuple-element.71, f32[]{:T(128)} %get-tuple-element.70), channel_id=1, replica_groups=mesh['lat'=8,'lon'=32] {'lat','lon'}, use_global_device_ids=true, to_apply=%region_2.3 | all-reduce | flops 2 | bytes 16 | tf_op jit(solution)/shard_map/psum | solution.py:225
  247.3 73.5 %psum.44 = f32[]{:T(128)} all-reduce(f32[]{:T(128)} %get-tuple-element.80), channel_id=1, replica_groups=mesh['lat'=8,'lon'=32] {'lat','lon'}, use_global_device_ids=true, to_apply=%region_6.7 | all-reduce | flops 1 | bytes 8 | tf_op jit(solution)/shard_map/psum | solution.py:225
  324.1 4.8 collective-permute-done.8
  341.6 5.4 collective-permute-done.10
  353.3 72.4 %psum.45 = f32[]{:T(128)} all-reduce(f32[]{:T(128)} %get-tuple-element.78), channel_id=1, replica_groups=mesh['lat'=8,'lon'=32] {'lat','lon'}, use_global_device_ids=true, to_apply=%region_8.9 | all-reduce | flops 1 | bytes 8 | tf_op jit(solution)/shard_map/psum | solution.py:259
  427.7 73.4 %psum.46 = f32[]{:T(128)} all-reduce(f32[]{:T(128)} %get-tuple-element.76), channel_id=1, replica_groups=mesh['lat'=8,'lon'=32] {'lat','lon'}, use_global_device_ids=true, to_apply=%region_10.11 | all-reduce | flops 1 | bytes 8 | tf_op jit(solution)/shard_map/psum | solution.py:225
  504.4 4.8 collective-permute-done.12
  521.4 5.4 collective-permute-done.14
  533.0 72.4 %psum.47 = f32[]{:T(128)} all-reduce(f32[]{:T(128)} %fusion.133), channel_id=1, replica_groups=mesh['lat'=8,'lon'=32] {'lat','lon'}, use_global_device_ids=true, to_apply=%region_12.13 | all-reduce | flops 1 | bytes 8 | tf_op jit(solution)/shard_map/psum | solution.py:259
  608.8 4.8 collective-permute-done.16
  623.6 5.5 reshape.507
  632.3 5.5 reshape.506
  639.4 5.8 collective-permute-done.18
  (350 shorter events, 126.8 us)
Async XLA Ops:
  0.6 15.6 %copy-start = (f32[8,6,6]{2,0,1:T(8,128)S(1)}, f32[8,6,6]{2,0,1:T(8,128)}, u32[]{:S(2)}) copy-start(f32[8,6,6]{2,0,1:T(8,128)} %param.22) | copy-start | bytes 3460
  0.6 15.6 %copy-start.18 = (s32[1,1,128]{2,1,0:T(1,128)S(1)}, s32[1,1,128]{2,1,0:T(1,128)}, u32[]{:S(2)}) copy-start(s32[1,1,128]{2,1,0:T(1,128)} %param.20) | copy-start | bytes 1540
  2.7 8.9 %collective-permute-start = (f32[4,1,4,512]{3,0,2,1:T(4,128)S(1)}, f32[4,1,4,512]{3,0,2,1:T(4,128)S(1)}, u32[]{:S(2)}, u32[]{:S(2)}) collective-permute-start(f32[4,1,4,512]{3,0,2,1:T(4,128)S(1)} %pad_maximum_fusion.5), channel_id=1, source_target_pairs={{32,0},{64,32},{96,64},{128,96},{160,128},{192,160},{224,192},{33,... | collective-permute-start | bytes 98312 | tf_op jit(solution)/shard_map/ppermute | solution.py:19
  11.6 6.3 collective-permute-start.1
  127.0 7.8 %collective-permute-start.2 = (f32[7,5,1,512]{3,1,2,0:T(8,128)S(1)}, f32[7,5,1,512]{3,1,2,0:T(8,128)S(1)}, u32[]{:S(2)}, u32[]{:S(2)}) collective-permute-start(f32[7,5,1,512]{3,1,2,0:T(8,128)S(1)} %pad_add_fusion.3), channel_id=1, source_target_pairs={{0,1},{1,2},{2,3},{3,4},{4,5},{5,6},{6,7},{7,8},{8,9},{9,10},{10,1... | collective-permute-start | bytes 215048 | tf_op jit(solution)/shard_map/ppermute | solution.py:24
  134.9 6.8 %collective-permute-start.3 = (f32[7,1,4,512]{3,1,2,0:T(1,128)S(1)}, f32[7,1,4,512]{3,1,2,0:T(1,128)S(1)}, u32[]{:S(2)}, u32[]{:S(2)}) collective-permute-start(f32[7,1,4,512]{3,1,2,0:T(1,128)S(1)} %pad_maximum_fusion.2), channel_id=1, source_target_pairs={{0,32},{32,64},{64,96},{96,128},{128,160},{160,192},{192,224},{1,3... | collective-permute-start | bytes 172040 | tf_op jit(solution)/shard_map/ppermute | solution.py:19
  142.0 7.1 %collective-permute-start.4 = (f32[1,1,4,512]{3,1,2,0:T(1,128)S(1)}, f32[1,1,4,512]{3,1,2,0:T(1,128)S(1)}, u32[]{:S(2)}, u32[]{:S(2)}) collective-permute-start(f32[1,1,4,512]{3,1,2,0:T(1,128)S(1)} %slice.874), channel_id=1, source_target_pairs={{32,0},{64,32},{96,64},{128,96},{160,128},{192,160},{224,192},{33,... | collective-permute-start | bytes 24584 | tf_op jit(solution)/shard_map/ppermute | solution.py:19
  149.1 1.5 collective-permute-start.5
  159.3 6.6 %collective-permute-start.6 = (f32[1,5,1,512]{3,1,2,0:T(8,128)S(1)}, f32[1,5,1,512]{3,1,2,0:T(8,128)S(1)}, u32[]{:S(2)}, u32[]{:S(2)}) collective-permute-start(f32[1,5,1,512]{3,1,2,0:T(8,128)S(1)} %pad_add_fusion.16), channel_id=1, source_target_pairs={{0,1},{1,2},{2,3},{3,4},{4,5},{5,6},{6,7},{7,8},{8,9},{9,10},{10,1... | collective-permute-start | bytes 30728 | tf_op jit(solution)/shard_map/ppermute | solution.py:24
  165.9 5.5 collective-permute-start.7
  322.2 6.8 %collective-permute-start.8 = (f32[1,1,4,512]{3,1,2,0:T(1,128)S(1)}, f32[1,1,4,512]{3,1,2,0:T(1,128)S(1)}, u32[]{:S(2)}, u32[]{:S(2)}) collective-permute-start(f32[1,1,4,512]{3,1,2,0:T(1,128)S(1)} %slice.891), channel_id=1, source_target_pairs={{32,0},{64,32},{96,64},{128,96},{160,128},{192,160},{224,192},{33,... | collective-permute-start | bytes 24584 | tf_op jit(solution)/shard_map/ppermute | solution.py:19
  328.9 2.4 collective-permute-start.9
  340.5 6.6 %collective-permute-start.10 = (f32[1,5,1,512]{3,1,2,0:T(8,128)S(1)}, f32[1,5,1,512]{3,1,2,0:T(8,128)S(1)}, u32[]{:S(2)}, u32[]{:S(2)}) collective-permute-start(f32[1,5,1,512]{3,1,2,0:T(8,128)S(1)} %pad_add_fusion.15), channel_id=1, source_target_pairs={{0,1},{1,2},{2,3},{3,4},{4,5},{5,6},{6,7},{7,8},{8,9},{9,10},{10,1... | collective-permute-start | bytes 30728 | tf_op jit(solution)/shard_map/ppermute | solution.py:24
  347.1 5.5 collective-permute-start.11
  502.5 6.8 %collective-permute-start.12 = (f32[1,1,4,512]{3,1,2,0:T(1,128)S(1)}, f32[1,1,4,512]{3,1,2,0:T(1,128)S(1)}, u32[]{:S(2)}, u32[]{:S(2)}) collective-permute-start(f32[1,1,4,512]{3,1,2,0:T(1,128)S(1)} %slice.908), channel_id=1, source_target_pairs={{32,0},{64,32},{96,64},{128,96},{160,128},{192,160},{224,192},{33,... | collective-permute-start | bytes 24584 | tf_op jit(solution)/shard_map/ppermute | solution.py:19
  509.3 1.8 collective-permute-start.13
  518.8 88.1 %copy-start.10 = (f32[4,4,512]{2,1,0:T(4,128)S(1)}, f32[4,4,512]{2,1,0:T(4,128)}, u32[]{:S(2)}) copy-start(f32[4,4,512]{2,1,0:T(4,128)} %param.18) | copy-start | bytes 98308
  520.1 100.0 %copy-start.15 = (f32[5,5,5]{1,2,0:T(8,128)S(1)}, f32[5,5,5]{1,2,0:T(8,128)}, u32[]{:S(2)}) copy-start(f32[5,5,5]{1,2,0:T(8,128)} %constant.155) | copy-start | bytes 1504
  520.2 6.6 %collective-permute-start.14 = (f32[1,5,1,512]{3,1,2,0:T(8,128)S(1)}, f32[1,5,1,512]{3,1,2,0:T(8,128)S(1)}, u32[]{:S(2)}, u32[]{:S(2)}) collective-permute-start(f32[1,5,1,512]{3,1,2,0:T(8,128)S(1)} %pad_add_fusion.14), channel_id=1, source_target_pairs={{0,1},{1,2},{2,3},{3,4},{4,5},{5,6},{6,7},{7,8},{8,9},{9,10},{10,1... | collective-permute-start | bytes 30728 | tf_op jit(solution)/shard_map/ppermute | solution.py:24
  526.8 5.5 collective-permute-start.15
  606.9 6.8 %collective-permute-start.16 = (f32[1,1,4,512]{3,1,2,0:T(1,128)S(1)}, f32[1,1,4,512]{3,1,2,0:T(1,128)S(1)}, u32[]{:S(2)}, u32[]{:S(2)}) collective-permute-start(f32[1,1,4,512]{3,1,2,0:T(1,128)S(1)} %slice.925), channel_id=1, source_target_pairs={{32,0},{64,32},{96,64},{128,96},{160,128},{192,160},{224,192},{33,... | collective-permute-start | bytes 24584 | tf_op jit(solution)/shard_map/ppermute | solution.py:19
  613.6 1.9 collective-permute-start.17
  638.3 6.9 %collective-permute-start.18 = (f32[3,5,1,512]{3,1,2,0:T(8,128)S(1)}, f32[3,5,1,512]{3,1,2,0:T(8,128)S(1)}, u32[]{:S(2)}, u32[]{:S(2)}) collective-permute-start(f32[3,5,1,512]{3,1,2,0:T(8,128)S(1)} %pad_add_fusion.6), channel_id=1, source_target_pairs={{0,1},{1,2},{2,3},{3,4},{4,5},{5,6},{6,7},{7,8},{8,9},{9,10},{10,1... | collective-permute-start | bytes 92168 | tf_op jit(solution)/shard_map/ppermute | solution.py:24
  645.2 5.7 collective-permute-start.19
  (15 other events, 71.0 us)
where the time goes:
time: 664 us; the launch traced here: 653 us
  blocking collectives  365 us (55%)
  local copies, waits for them, and re-layouts  123 us (19%)
  waiting for transfers between devices  68.3 us (10%)
  matrix products  37 us (6%)
  starting transfers between devices  36.6 us (6%)
  other arithmetic  13.4 us (2%)
  between operations  9.69 us (1%)
    psum x3, blocking collectives, precond_inner(): return lax.psum(jnp.sum(residual * precond_res), ('lat', 'lon'))  220 us
    psum x2, blocking collectives, per_device(): lax.psum(jnp.sum(search_dir * image_dir), ('lat', 'lon'))  145 us
    reshape x20, local copies, waits for them, and re-layouts, alternate(): block.reshape(block_shape[:dim_pos] + (block_shape[dim_pos] * 4,) + block...  62.5 us
    ppermute x10, waiting for transfers between devices, from_behind(): lax.ppermute(array, axis, [(i, (i + by) % devices) for i in range(devices)])  37.5 us
    ppermute x10, waiting for transfers between devices, shifted(): return lax.ppermute(array, axis, pairs)  30.8 us
    ppermute x10, starting transfers between devices, shifted(): return lax.ppermute(array, axis, pairs)  26.4 us
    slice x26, local copies, waits for them, and re-layouts, split_axis(): lax.slice_in_dim(array, start, start + 4 * (elem_count - 1) + 1, 4, dim_pos)  26.3 us
    dot_general x1, matrix products, first_block(): jnp.einsum('klxyz,laxbydz->kaxbydz', stiffness, strain, precision=highest)  23.4 us
  transfers between devices with their start and end apart: 20, of which 19 were waited for; matrix products, arithmetic and copies ran while one was open for 1% of the time, Pallas kernels for 0%

commit v1 on v0

v1 whole, which is shorter than its diff:
```python
import functools

import jax
import jax.numpy as jnp
import numpy as np
from jax import lax
from jax.experimental import pallas as pl
from jax.experimental.pallas import tpu as pltpu
from jax.sharding import PartitionSpec as P

TIME_STEP = 0.1
F32 = jnp.float32
BF16 = jnp.bfloat16
LAT, LON = 8, 32
AXES = ("lat", "lon")
VMEM = pl.BlockSpec(memory_space=pltpu.VMEM)
SMEM = pl.BlockSpec(memory_space=pltpu.SMEM)


def gll():
    points = np.array([-1.0, -np.sqrt(3.0 / 7.0), 0.0, np.sqrt(3.0 / 7.0), 1.0])
    weights = np.array([0.1, 49.0 / 90.0, 32.0 / 45.0, 49.0 / 90.0, 0.1])
    differ = points[:, None] - points[None, :] + np.eye(5)
    factors = np.prod(differ, axis=1)
    deriv = factors[:, None] / factors[None, :] / differ * (1.0 - np.eye(5))
    deriv = deriv - np.eye(5) * np.sum(deriv, axis=1)[:, None]
    return deriv, weights


DERIV, WEIGHTS = gll()
W = [float(v) for v in WEIGHTS]
M_POISSON = (DERIV.T @ np.diag(WEIGHTS) @ DERIV).tolist()
M_SOURCE = (np.diag(WEIGHTS) @ DERIV).T.tolist()
M_GRAVITY = (np.diag(WEIGHTS) @ DERIV).tolist()


def lanes(shape):
    return lax.broadcasted_iota(jnp.int32, shape, len(shape) - 1)


def sublanes(shape):
    return lax.broadcasted_iota(jnp.int32, shape, len(shape) - 2)


def by_index(index, values):
    out = jnp.full(index.shape, float(values[-1]), F32)
    for pos in range(len(values) - 2, -1, -1):
        out = jnp.where(index == pos, float(values[pos]), out)
    return out


def column(values, rows=4, width=512):
    return by_index(sublanes((rows, width)), list(values))


def row_of(array, pos, rows=4):
    return jnp.broadcast_to(array[pos : pos + 1], (rows, array.shape[1]))


def radial(field, matrix):
    lane = lanes((4, 512))
    node = lane & 3
    own, before = None, None
    for shift in range(-4, 5):
        moved = field if shift == 0 else pltpu.roll(field, (-shift) % 512, 1)
        if shift > -4:
            factors = [
                matrix[c][c + shift] if 0 <= c + shift <= 4 else 0.0 for c in range(4)
            ]
            table = by_index(node, factors)
            if shift > 0:
                table = jnp.where(lane < 512 - shift, table, 0.0)
            own = table * moved if own is None else own + table * moved
        if shift <= 0:
            term = float(matrix[4][4 + shift]) * moved
            before = term if before is None else before + term
    return own, before


def mix(matrix_row, arrays):
    total = None
    for factor, array in zip(matrix_row, arrays):
        term = float(factor) * array
        total = term if total is None else total + term
    return total


def lat_part(fields, above, below, matrix, own_row, back_row):
    out = []
    for i in range(4):
        value = own_row * mix(matrix[i], fields + [above])
        if i == 0:
            value = value + back_row * (float(matrix[4][4]) * fields[0] + below)
        out.append(value)
    return out


def lon_part(fields, above, below, matrix, own_col, back_col):
    columns = [column([matrix[b][p] for b in range(4)]) for p in range(5)]
    first = column([1.0, 0.0, 0.0, 0.0])
    out = []
    for i in range(4):
        value = columns[4] * row_of(above, i)
        for p in range(4):
            value = value + columns[p] * row_of(fields[i], p)
        edge = float(matrix[4][4]) * fields[i][0:1] + below[i : i + 1]
        kind = min(i, 1)
        value = own_col[kind] * value + first * (back_col[kind] * edge)
        out.append(W[i] * value)
    return out


def radial_part(fields, matrix, own, before):
    out = []
    for i in range(4):
        first, second = radial(fields[i], matrix)
        kind = min(i, 1)
        out.append(W[i] * (own[kind] * first + before[kind] * second))
    return out


def partial_lat(fields, matrix):
    return mix(matrix[4][:4], fields)


def partial_lon(field, matrix):
    weighted = column(matrix[4][:4]) * field
    return jnp.sum(weighted, axis=0, keepdims=True)


def messages(fields, up_lat, down_lat, up_lon, down_lon):
    up_lat[0:4, :] = partial_lat(fields, M_POISSON)
    up_lat[4:8, :] = partial_lat(fields, M_GRAVITY)
    down_lat[0:4, :] = fields[0]
    for i in range(4):
        up_lon[i : i + 1, :] = partial_lon(fields[i], M_POISSON)
        up_lon[4 + i : 5 + i, :] = partial_lon(fields[i], M_GRAVITY)
        down_lon[i : i + 1, :] = fields[i][0:1]


def has_next():
    return jnp.where(lax.axis_index("lat") < LAT - 1, 1.0, 0.0).astype(F32)


def has_before():
    return jnp.where(lax.axis_index("lat") > 0, 1.0, 0.0).astype(F32)


def start_kernel(disp, vel, acc, phi, mat, flag, disp_new, up_lat, down_lat, up_lon, down_lon, code):
    u = []
    for comp in range(3):
        planes = []
        for i in range(4):
            value = (
                disp[comp, i]
                + TIME_STEP * vel[comp, i]
                + 0.5 * TIME_STEP * TIME_STEP * acc[comp, i]
            )
            disp_new[comp, i] = value
            planes.append(value)
        u.append(planes)
    potential = [phi[i] for i in range(4)]
    kind = (1 + mat[0] + 8 * flag[0]).astype(F32).astype(BF16)
    spread = (
        lax.broadcasted_iota(jnp.int32, (128, 512), 1) // 4
        == lax.broadcasted_iota(jnp.int32, (128, 512), 0)
    )
    spread = jnp.where(spread, 1.0, 0.0).astype(BF16)
    kinds = jnp.dot(jnp.broadcast_to(kind, (16, 128)), spread, preferred_element_type=F32)
    kinds = kinds[0:8]
    code[...] = kinds
    up_lat[0:4, :] = partial_lat(u[0], M_SOURCE)
    up_lat[4:8, :] = partial_lat(potential, M_POISSON)
    up_lat[8:12, :] = partial_lat(potential, M_GRAVITY)
    up_lat[12:16, :] = kinds[0:4]
    up_lon[12:16, :] = kinds[0:4]
    for comp in range(3):
        down_lat[4 * comp : 4 * comp + 4, :] = u[comp][0]
        for i in range(4):
            row = 4 * comp + i
            down_lon[row : row + 1, :] = u[comp][i][0:1]
    down_lat[12:16, :] = potential[0]
    for i in range(4):
        up_lon[i : i + 1, :] = partial_lon(u[1][i], M_SOURCE)
        up_lon[4 + i : 5 + i, :] = partial_lon(potential[i], M_POISSON)
        up_lon[8 + i : 9 + i, :] = partial_lon(potential[i], M_GRAVITY)
        down_lon[12 + i : 13 + i, :] = potential[i][0:1]


def lat_rows(factor):
    cols, first = column(W[:4]), column([W[0], 0.0, 0.0, 0.0])
    own = cols * row_of(factor, 0) + first * row_of(factor, 2)
    back = cols * row_of(factor, 1) + first * row_of(factor, 3)
    return own, back


def lon_cols(factor):
    own = (factor[0:1] + factor[1:2], factor[0:1])
    back = (factor[2:3] + factor[3:4], factor[2:3])
    return own, back


def residual_kernel(
    disp_new, phi, own_code, lat_below, lat_above, lon_below, lon_above, diag_code, dens,
    coef, rho_coef, precond_out, w0_out, up_lat, down_lat, up_lon, down_lon,
):
    following, before = has_next(), has_before()
    codes = jnp.concatenate(
        [
            own_code[0:1, :],
            before * lat_below[12:13, :],
            lon_below[12:13, :],
            before * diag_code[0:1, :],
        ],
        0,
    )
    flagged = codes > 8.5
    material = jnp.where(flagged, codes - 9.0, codes - 1.0)
    valid = codes > 0.5
    rho = jnp.zeros((4, 512), F32)
    for m in range(8):
        rho = jnp.where(jnp.abs(material - m) < 0.5, dens[m], rho)
    rho = jnp.where(valid, rho, 0.0)
    stretch = jnp.where(valid, jnp.where(flagged, 3.0, 1.0), 0.0)
    inverse = jnp.where(valid, jnp.where(flagged, 1.0 / 3.0, 1.0), 0.0)
    rho_in = jnp.where(flagged, 0.0, rho)
    lane = lanes((4, 512))
    node = lane & 3
    joint = jnp.logical_and(node == 0, lane >= 4)
    weight = by_index(node, W[:4])

    def earlier(factor):
        return jnp.where(joint, pltpu.roll(factor, 4, 1), 0.0)

    def weighted(factor):
        return weight * factor + W[4] * earlier(factor)

    s_points = 0.5 * weighted(stretch)
    s_own, s_back = lat_rows(s_points)
    s_col, s_col_back = lon_cols(s_points)
    i_own, i_back = lat_rows(0.5 * inverse)
    j_own, j_back = lat_rows(0.5 * earlier(inverse))
    i_both, j_both = (i_own + i_back, i_own), (j_own + j_back, j_own)
    coef[0:4, :] = s_own
    coef[4:8, :] = s_back
    coef[8:12, :] = i_both[0]
    coef[12:16, :] = i_both[1]
    coef[16:20, :] = j_both[0]
    coef[20:24, :] = j_both[1]
    coef[24:25, :] = s_col[0]
    coef[25:26, :] = s_col[1]
    coef[26:27, :] = s_col_back[0]
    coef[27:28, :] = s_col_back[1]
    r_points = 0.25 * weighted(rho)
    r_own, r_back = lat_rows(r_points)
    r_col, r_col_back = lon_cols(r_points)
    scaled = 0.25 * rho * inverse
    g_own, g_back = lat_rows(scaled)
    h_own, h_back = lat_rows(earlier(scaled))
    rho_coef[0:4, :] = r_own
    rho_coef[4:8, :] = r_back
    rho_coef[8:12, :] = g_own + g_back
    rho_coef[12:16, :] = g_own
    rho_coef[16:20, :] = h_own + h_back
    rho_coef[20:24, :] = h_own
    rho_coef[24:25, :] = r_col[0]
    rho_coef[25:26, :] = r_col[1]
    rho_coef[26:27, :] = r_col_back[0]
    rho_coef[27:28, :] = r_col_back[1]
    q_points = 0.25 * weighted(rho_in)
    q_own, q_back = lat_rows(q_points)
    q_col, q_col_back = lon_cols(q_points)
    t_own, t_back = lat_rows(0.25 * rho_in)
    v_own, v_back = lat_rows(0.25 * earlier(rho_in))

    u = [[disp_new[comp, i] for i in range(4)] for comp in range(3)]
    potential = [phi[i] for i in range(4)]
    source_x = lat_part(
        u[0], following * lat_above[0:4, :], lat_below[0:4, :], M_SOURCE, q_own, q_back
    )
    source_y = lon_part(
        u[1], lon_above[4:8, :], lon_below[0:4, :], M_SOURCE, q_col, q_col_back
    )
    source_z = radial_part(u[2], M_SOURCE, (t_own + t_back, t_own), (v_own + v_back, v_own))
    image_x = lat_part(
        potential, following * lat_above[12:16, :], lat_below[4:8, :], M_POISSON, s_own, s_back
    )
    image_y = lon_part(
        potential, lon_above[12:16, :], lon_below[4:8, :], M_POISSON, s_col, s_col_back
    )
    image_z = radial_part(potential, M_POISSON, i_both, j_both)
    diag = [M_POISSON[a][a] for a in range(5)]
    diag_node = by_index(node, diag[:4])
    diag_col = column(diag[:4])
    first = column([1.0, 0.0, 0.0, 0.0])
    w0 = []
    for i in range(4):
        kind = min(i, 1)
        precond = diag[i] * s_own
        if i == 0:
            precond = precond + diag[4] * s_back
        precond = precond + W[i] * (
            diag_col * s_col[kind]
            + first * (diag[4] * s_col_back[kind])
            + i_both[kind] * diag_node
            + diag[4] * j_both[kind]
        )
        precond_out[i] = precond
        source = -(source_x[i] + source_y[i] + source_z[i])
        image = image_x[i] + image_y[i] + image_z[i]
        value = (source - image) / precond
        w0_out[i] = value
        w0.append(value)
    messages(w0, up_lat, down_lat, up_lon, down_lon)
    for comp in range(3):
        down_lat[4 + comp : 5 + comp, :] = lon_above[4 * comp : 4 * comp + 1, :]
    down_lat[7:8, :] = jnp.zeros((1, 512), F32)


def poisson(fields, coef, lat_below, lat_above, lon_below, lon_above):
    following = has_next()
    s_col = (coef[24:25, :], coef[25:26, :])
    s_col_back = (coef[26:27, :], coef[27:28, :])
    x = lat_part(
        fields, following * lat_above[0:4, :], lat_below[0:4, :], M_POISSON, coef[0:4, :], coef[4:8, :]
    )
    y = lon_part(fields, lon_above[0:4, :], lon_below[0:4, :], M_POISSON, s_col, s_col_back)
    z = radial_part(
        fields, M_POISSON, (coef[8:12, :], coef[12:16, :]), (coef[16:20, :], coef[20:24, :])
    )
    return [x[i] + y[i] + z[i] for i in range(4)]


def next_kernel(
    last, field, coef, precond, lat_below, lat_above, lon_below, lon_above, *rest
):
    if last:
        lat_force, lon_force, out, up_lat, down_lat, up_lon, down_lon = rest
    else:
        out, up_lat, down_lat, up_lon, down_lon = rest
    fields = [field[i] for i in range(4)]
    image = poisson(fields, coef, lat_below, lat_above, lon_below, lon_above)
    result = []
    for i in range(4):
        value = image[i] / precond[i] - fields[i]
        out[i] = value
        result.append(value)
    messages(result, up_lat, down_lat, up_lon, down_lon)
    down_lat[4:8, :] = jnp.zeros((4, 512), F32)
    down_lon[4:8, :] = jnp.zeros((4, 512), F32)
    if last:
        up_lat[8:24, :] = lat_force[...]
        up_lon[8:24, :] = lon_force[...]


def moment_kernel(w0, w1, w2, coef, precond, lat_below, lat_above, lon_below, lon_above, out):
    fields = [w2[i] for i in range(4)]
    image = poisson(fields, coef, lat_below, lat_above, lon_below, lon_above)
    sums = [None] * 6
    for i in range(4):
        m = precond[i]
        a, b, c = w0[i], w1[i], w2[i]
        ma, mb, mc = m * a, m * b, m * c
        terms = [a * ma, b * ma, b * mb, c * mb, c * mc, c * (image[i] - mc)]
        for k in range(6):
            sums[k] = terms[k] if sums[k] is None else sums[k] + terms[k]
    lane = lanes((1, 128))
    line = jnp.zeros((1, 128), F32)
    for k in range(6):
        total = jnp.sum(jnp.sum(sums[k], axis=0, keepdims=True), axis=1, keepdims=True)
        line = jnp.where(lane == k, total, line)
    out[...] = jnp.broadcast_to(line, out.shape)


def cg_coefficients(mu):
    zero = jnp.zeros_like(mu[0])

    def inner(a):
        total = zero
        for i in range(len(a)):
            for j in range(len(a)):
                total = total + a[i] * a[j] * mu[i + j]
        return total

    def energy(a):
        total = zero
        for i in range(len(a)):
            for j in range(len(a)):
                total = total + a[i] * a[j] * (mu[i + j + 1] + mu[i + j])
        return total

    def ratio(a, b):
        return jnp.where(b == 0.0, 0.0, a / jnp.where(b == 0.0, 1.0, b))

    y = [zero, zero, zero]
    z = [zero + 1.0]
    search = [zero + 1.0]
    rz = mu[0]
    for step in range(3):
        length = ratio(rz, energy(search))
        for i in range(len(search)):
            y[i] = y[i] + length * search[i]
        if step < 2:
            grown = [zero] * (len(search) + 1)
            for i in range(len(search)):
                grown[i] = grown[i] + search[i]
                grown[i + 1] = grown[i + 1] + search[i]
            z = z + [zero]
            z = [z[i] - length * grown[i] for i in range(len(z))]
            rz_next = inner(z)
            beta = ratio(rz_next, rz)
            padded = search + [zero]
            search = [z[i] + beta * padded[i] for i in range(len(z))]
            rz = rz_next
    return y


def final_kernel(
    moments, phi, w0, w1, w2, rho_coef, own_force, corner,
    ma, mb, mc, md, na, nb, nc, nd, fa, fb, fc, fd, ga, gb, gc, gd,
    vel, acc, phi_new, acc_new, vel_new,
):
    total = jnp.sum(moments[...], axis=0, keepdims=True)
    lane = lanes((1, 128))
    mu = [
        jnp.broadcast_to(
            jnp.sum(jnp.where(lane == k, total, 0.0), axis=1, keepdims=True), (1, 128)
        )
        for k in range(6)
    ]
    y = cg_coefficients(mu)
    y = [jnp.concatenate([v] * 4, 1) for v in y]

    def combined(first, one, two, three):
        return first + y[0] * one + y[1] * two + y[2] * three

    potential = []
    for i in range(4):
        value = combined(phi[i], w0[i], w1[i], w2[i])
        phi_new[i] = value
        potential.append(value)
    following, before = has_next(), has_before()
    lat_below = combined(ma[8:12, :], mb[4:8, :], mc[4:8, :], md[4:8, :])
    lat_above = following * combined(na[12:16, :], nb[0:4, :], nc[0:4, :], nd[0:4, :])
    lon_below = combined(fa[8:12, :], fb[4:8, :], fc[4:8, :], fd[4:8, :])
    lon_above = combined(ga[12:16, :], gb[0:4, :], gc[0:4, :], gd[0:4, :])
    r_own, r_back = rho_coef[0:4, :], rho_coef[4:8, :]
    r_col = (rho_coef[24:25, :], rho_coef[25:26, :])
    r_col_back = (rho_coef[26:27, :], rho_coef[27:28, :])
    x = lat_part(potential, lat_above, lat_below, M_GRAVITY, r_own, r_back)
    y_part = lon_part(potential, lon_above, lon_below, M_GRAVITY, r_col, r_col_back)
    z = radial_part(
        potential,
        M_GRAVITY,
        (rho_coef[8:12, :], rho_coef[12:16, :]),
        (rho_coef[16:20, :], rho_coef[20:24, :]),
    )
    cols = column(W[:4])
    first = column([1.0, 0.0, 0.0, 0.0])
    gravity = (x, y_part, z)
    for i in range(4):
        mass = r_own + r_back if i == 0 else r_own
        mass = 0.5 * W[i] * mass
        for comp in range(3):
            force = own_force[comp, i]
            force = force + first * fd[8 + 5 * comp + i : 9 + 5 * comp + i, :]
            if i == 0:
                edge = md[8 + 4 * comp : 12 + 4 * comp, :]
                edge = edge + first * corner[comp : comp + 1, :]
                force = force + before * edge
            value = (-gravity[comp][i] - force) / mass
            acc_new[comp, i] = value
            vel_new[comp, i] = vel[comp, i] + 0.5 * TIME_STEP * (acc[comp, i] + value)


def split3(value):
    high = value.astype(BF16)
    rest = value - high.astype(F32)
    mid = rest.astype(BF16)
    low = (rest - mid.astype(F32)).astype(BF16)
    return high, mid, low


def elastic_kernel(
    disp, lat_above, lon_above, corner, mat, moduli, decay, strength, memory,
    memory_new, force, lat_force, lon_force, corner_force,
    points, elems, stiff, devs, old, new, flux, perm,
):
    following = has_next()
    points[...] = jnp.zeros(points.shape, F32)
    for comp in range(3):
        for a in range(4):
            base = (comp * 5 + a) * 8
            points[base : base + 4, :] = disp[comp, a]
            row = 4 * comp + a
            points[base + 4 : base + 5, :] = lon_above[row : row + 1, :]
        base = (comp * 5 + 4) * 8
        points[base : base + 4, :] = following * lat_above[4 * comp : 4 * comp + 4, :]
        points[base + 4 : base + 5, :] = following * corner[4 + comp : 5 + comp, :]
    for c in range(4):
        hit = lax.broadcasted_iota(jnp.int32, (128, 512), 1) == (
            4 * lax.broadcasted_iota(jnp.int32, (128, 512), 0) + c
        )
        perm[128 * c : 128 * c + 128, :] = jnp.where(hit, 1.0, 0.0).astype(BF16)
    parts = jnp.concatenate(split3(points[...]), 0)
    taken = lax.dot_general(
        parts, perm[...], (((1,), (1,)), ((), ())), preferred_element_type=F32
    )
    taken = taken[0:128] + taken[128:256] + taken[256:384]
    for c in range(4):
        elems[c] = taken[:, 128 * c : 128 * c + 128]
    lane = lanes((128, 128))
    elems[4] = jnp.where(lane < 127, pltpu.roll(taken[:, 0:128], 127, 1), 0.0)
    onehot = [mat[0] == m for m in range(8)]
    for k in range(6):
        for l in range(k, 6):
            value = jnp.zeros((1, 128), F32)
            for m in range(8):
                value = jnp.where(onehot[m], moduli[m, k, l], value)
            stiff[6 * k + l : 6 * k + l + 1, :] = value
    slopes = [
        by_index(sublanes((8, 128)), [2.0 * DERIV[b][p] for b in range(5)] + [0.0])
        for p in range(5)
    ]
    turned = [
        by_index(sublanes((8, 128)), [2.0 * DERIV[p][b] for b in range(5)] + [0.0])
        for p in range(5)
    ]
    weight_col = by_index(sublanes((8, 128)), W + [0.0])

    def slab(comp, a, c):
        base = (comp * 5 + a) * 8
        return elems[c, base : base + 8, :]

    def along_lon(cols, value):
        total = None
        for p in range(5):
            term = cols[p] * row_of(value, p, 8)
            total = term if total is None else total + term
        return total

    for a in range(5):
        elastic_of = []
        for c in range(5):
            dx, dy, dz = [], [], []
            for comp in range(3):
                dx.append(mix([2.0 * DERIV[a][p] for p in range(5)], [slab(comp, p, c) for p in range(5)]))
                dy.append(along_lon(slopes, slab(comp, a, c)))
                dz.append(mix([2.0 * DERIV[c][p] for p in range(5)], [slab(comp, a, p) for p in range(5)]))
            strain = [dx[0], dy[1], dz[2], dy[0] + dx[1], dz[0] + dx[2], dz[1] + dy[2]]
            elastic = []
            for k in range(6):
                total = None
                for l in range(6):
                    pos = 6 * min(k, l) + max(k, l)
                    term = stiff[pos : pos + 1, :] * strain[l]
                    total = term if total is None else total + term
                elastic.append(total)
            pressure = (elastic[0] + elastic[1] + elastic[2]) * (1.0 / 3.0)
            dev = [elastic[0] - pressure, elastic[1] - pressure, elastic[3], elastic[4], elastic[5]]
            for d in range(5):
                devs[d * 5 + c] = dev[d]
            elastic_of.append(elastic)
        relaxed = []
        for d in range(5):
            for b in range(5):
                for c in range(5):
                    row = (b * 5 + c) * 4
                    old[row : row + 3, :] = memory[d, a, b, c].astype(F32)
            sums = []
            for c in range(5):
                dev = devs[d * 5 + c]
                total = None
                for l in range(3):
                    was = old[pl.ds(4 * c + l, 8, stride=20), :]
                    rate = decay[l]
                    now = rate * was + ((1.0 - rate) * strength[l]) * dev
                    now = now.astype(BF16).astype(F32)
                    new[pl.ds(4 * c + l, 8, stride=20), :] = now
                    total = now if total is None else total + now
                sums.append(total)
            for b in range(5):
                for c in range(5):
                    row = (b * 5 + c) * 4
                    memory_new[d, a, b, c] = new[row : row + 3, :].astype(BF16)
            relaxed.append(sums)
        for c in range(5):
            e = elastic_of[c]
            r = [relaxed[d][c] for d in range(5)]
            weight = weight_col * (W[a] * W[c] / 8.0)
            stress = [e[0] - r[0], e[1] - r[1], e[2] + r[0] + r[1], e[3] - r[2], e[4] - r[3], e[5] - r[4]]
            for k in range(6):
                flux[k, a * 5 + c] = jnp.where(weight_col > 0.0, weight * stress[k], 0.0)
    flux_of = [[0, 3, 4], [3, 1, 5], [4, 5, 2]]
    for c in range(5):
        elems[c, 120:128, :] = jnp.zeros((8, 128), F32)
        for comp in range(3):
            for a in range(5):
                value = mix(
                    [2.0 * DERIV[p][a] for p in range(5)],
                    [flux[flux_of[comp][0], p * 5 + c] for p in range(5)],
                )
                value = value + along_lon(turned, flux[flux_of[comp][1], a * 5 + c])
                value = value + mix(
                    [2.0 * DERIV[p][c] for p in range(5)],
                    [flux[flux_of[comp][2], a * 5 + p] for p in range(5)],
                )
                base = (comp * 5 + a) * 8
                elems[c, base : base + 8, :] = value
    carried = jnp.where(lane > 0, pltpu.roll(elems[4], 1, 1), 0.0)
    merged = jnp.concatenate([elems[0] + carried, elems[1], elems[2], elems[3]], 1)
    parts = jnp.concatenate(split3(merged), 0)
    given = jnp.dot(parts, perm[...], preferred_element_type=F32)
    given = given[0:128] + given[128:256] + given[256:384]
    lat_force[12:16, :] = jnp.zeros((4, 512), F32)
    lon_force[15:16, :] = jnp.zeros((1, 512), F32)
    corner_force[...] = jnp.zeros((8, 512), F32)
    for comp in range(3):
        for a in range(5):
            base = (comp * 5 + a) * 8
            if a < 4:
                force[comp, a] = given[base : base + 4]
                lon_force[5 * comp + a : 5 * comp + a + 1, :] = given[base + 4 : base + 5]
            else:
                lat_force[4 * comp : 4 * comp + 4, :] = given[base : base + 4]
                lon_force[5 * comp + 4 : 5 * comp + 5, :] = given[base + 4 : base + 5]
                corner_force[comp : comp + 1, :] = given[base + 4 : base + 5]


def call(kernel, name, outs, ins, args, scratch=(), flops=1000000, moved=500000):
    return pl.pallas_call(
        kernel,
        name=name,
        out_shape=[jax.ShapeDtypeStruct(s, d) for s, d in outs],
        in_specs=ins,
        out_specs=[VMEM] * len(outs),
        scratch_shapes=list(scratch),
        compiler_params=pltpu.CompilerParams(vmem_limit_bytes=24 * 1024 * 1024),
        cost_estimate=pl.CostEstimate(flops=flops, bytes_accessed=moved, transcendentals=0),
    )(*args)


def lat_ring(array, by):
    return lax.ppermute(array, "lat", [(i, (i + by) % LAT) for i in range(LAT)])


def lon_ring(array, by):
    return lax.ppermute(array, "lon", [(i, (i + by) % LON) for i in range(LON)])


def diagonal(array):
    pairs = [
        (e * LON + f, (e + 1) % LAT * LON + (f + 1) % LON)
        for e in range(LAT)
        for f in range(LON)
    ]
    return lax.ppermute(array, AXES, pairs)


def star(up_lat, down_lat, up_lon, down_lon):
    return (lat_ring(up_lat, 1), lat_ring(down_lat, -1), lon_ring(up_lon, 1), lon_ring(down_lon, -1))


def per_device(
    displacement, velocity, acceleration, potential, memory_vars, materials, shell_flags,
    moduli, densities, decay, strength,
):
    field = ((4, 4, 512), F32)
    vector = ((3, 4, 4, 512), F32)
    r8, r16, r24, r32 = (((n, 512), F32) for n in (8, 16, 24, 32))
    disp_new, *sent, code = call(
        start_kernel, "start", [vector, r16, r16, r16, r16, r8], [VMEM] * 6,
        (displacement, velocity, acceleration, potential, materials, shell_flags),
    )
    halo_a = star(*sent)
    diag_code = diagonal(code)
    coef, rho_coef, precond, w0, *sent = call(
        residual_kernel, "residual", [r32, r32, field, field, r8, r8, r8, r8],
        [VMEM] * 8 + [SMEM],
        (disp_new, potential, code, *halo_a, diag_code, densities),
    )
    halo_b = star(*sent)
    w1, *sent = call(
        functools.partial(next_kernel, False), "second", [field, r8, r8, r8, r8], [VMEM] * 7,
        (w0, coef, precond, *halo_b),
    )
    halo_c = star(*sent)
    memory = memory_vars.reshape(3, 5, 5, 5, 5, 128).transpose(1, 2, 3, 4, 0, 5)
    memory_new, force, lat_force, lon_force, corner_force = call(
        elastic_kernel, "elastic",
        [((5, 5, 5, 5, 3, 128), BF16), vector, r16, r16, r8],
        [VMEM] * 5 + [SMEM] * 3 + [VMEM],
        (disp_new, halo_a[1], halo_a[3], halo_b[1], materials, moduli, decay, strength, memory),
        [
            pltpu.VMEM((128, 512), F32),
            pltpu.VMEM((5, 128, 128), F32),
            pltpu.VMEM((40, 128), F32),
            pltpu.VMEM((25, 8, 128), F32),
            pltpu.VMEM((160, 128), F32),
            pltpu.VMEM((160, 128), F32),
            pltpu.VMEM((6, 25, 8, 128), F32),
            pltpu.VMEM((512, 512), BF16),
        ],
        flops=20000000, moved=2000000,
    )
    w2, *sent = call(
        functools.partial(next_kernel, True), "third", [field, r24, r8, r24, r8], [VMEM] * 9,
        (w1, coef, precond, *halo_c, lat_force, lon_force),
    )
    halo_d = star(*sent)
    corner = diagonal(corner_force)
    (line,) = call(
        moment_kernel, "moments", [((LAT * LON, 128), F32)], [VMEM] * 9,
        (w0, w1, w2, coef, precond, *halo_d),
    )
    moments = lax.all_to_all(line, AXES, 0, 0, tiled=True)
    phi_new, acc_new, vel_new = call(
        final_kernel, "final", [field, vector, vector], [VMEM] * 26,
        (
            moments, potential, w0, w1, w2, rho_coef, force, corner,
            *(halo[k] for k in range(4) for halo in (halo_a, halo_b, halo_c, halo_d)),
            velocity, acceleration,
        ),
    )
    memory_new = memory_new.transpose(4, 0, 1, 2, 3, 5).reshape(memory_vars.shape)
    return (disp_new, vel_new, acc_new, phi_new, memory_new)


def solution(mesh):
    vector = P(None, "lat", "lon", None)
    scalar = P("lat", "lon", None)
    memory = P(None, None, None, "lat", None, "lon", None, None)
    return jax.shard_map(
        per_device,
        mesh=mesh,
        in_specs=(vector, vector, vector, scalar, memory, scalar, scalar, P(), P(), P(), P()),
        out_specs=(vector, vector, vector, scalar, memory),
        check_vma=False,
    )
```

time: 664 us -> 90.6 us (0.14)
  the two profiles are of different devices: /device:TPU:96 before, /device:TPU:1 now
where the time goes in v1:
time: 90.6 us; the launch traced here: 90.2 us
  starting transfers between devices  53.9 us (59%)
  waiting for transfers between devices  18.8 us (21%)
  Pallas kernels  8.98 us (10%)
  local copies, waits for them, and re-layouts  7.71 us (9%)
    ppermute x8, starting transfers between devices, lon_ring(): return lax.ppermute(array, 'lon', [(i, (i + by) % LON) for i in range(LON)])  20.2 us
    all_to_all x1, starting transfers between devices, per_device(): moments = lax.all_to_all(line, AXES, 0, 0, tiled=True)  16.3 us
    ppermute x8, starting transfers between devices, lat_ring(): return lax.ppermute(array, 'lat', [(i, (i + by) % LAT) for i in range(LAT)])  14.6 us
    ppermute x2, waiting for transfers between devices, diagonal(): return lax.ppermute(array, AXES, pairs)  11.4 us
    pallas_call x7, Pallas kernels, call(): pl.pallas_call(kernel, name=name, out_shape=[jax.ShapeDtypeStruct(s, d) f...  8.98 us
    unnamed x35, local copies, waits for them, and re-layouts  7.71 us
    all_to_all x1, waiting for transfers between devices, per_device(): moments = lax.all_to_all(line, AXES, 0, 0, tiled=True)  5.76 us
    ppermute x2, starting transfers between devices, diagonal(): return lax.ppermute(array, AXES, pairs)  2.8 us
  transfers between devices with their start and end apart: 19, of which 6 were waited for; matrix products, arithmetic and copies ran while one was open for 0% of the time, Pallas kernels for 5%

profile of v1, /device:TPU:1, one launch (start us, length us, event | category | flops | bytes accessed | tf_op | source)
XLA Modules:
  0.0 90.2 jit_solution(4975473031090253577)
XLA Ops:
  0.6 0.9 copy-done.3
  1.5 0.9 copy-done.5
  2.4 0.8 copy-done.7
  3.2 0.9 copy-done.10
  6.1 2.5 %collective-permute-start = (f32[16,512]{1,0:T(8,128)S(1)}, f32[16,512]{1,0:T(8,128)S(1)}, u32[]{:S(2)}, u32[]{:S(2)}) collective-permute-start(f32[16,512]{1,0:T(8,128)S(1)} %get-tuple-element.39), channel_id=1, source_target_pairs={{0,32},{32,64},{64,96},{96,128},{128,160},{160,192},{192,224},{224... | collective-permute-start | bytes 98312 | tf_op jit(solution)/shard_map/ppermute | solution.py:644
  8.5 3.9 %collective-permute-start.1 = (f32[16,512]{1,0:T(8,128)S(1)}, f32[16,512]{1,0:T(8,128)S(1)}, u32[]{:S(2)}, u32[]{:S(2)}) collective-permute-start(f32[16,512]{1,0:T(8,128)S(1)} %get-tuple-element.40), channel_id=1, source_target_pairs={{0,224},{32,0},{64,32},{96,64},{128,96},{160,128},{192,160},{224,1... | collective-permute-start | bytes 98312 | tf_op jit(solution)/shard_map/ppermute | solution.py:644
  12.5 2.1 %collective-permute-start.2 = (f32[16,512]{1,0:T(8,128)S(1)}, f32[16,512]{1,0:T(8,128)S(1)}, u32[]{:S(2)}, u32[]{:S(2)}) collective-permute-start(f32[16,512]{1,0:T(8,128)S(1)} %get-tuple-element.41), channel_id=1, source_target_pairs={{0,1},{1,2},{2,3},{3,4},{4,5},{5,6},{6,7},{7,8},{8,9},{9,10},{10,1... | collective-permute-start | bytes 98312 | tf_op jit(solution)/shard_map/ppermute | solution.py:648
  14.6 6.9 %collective-permute-done.4.diag_code = f32[8,512]{1,0:T(8,128)S(1)} collective-permute-done((f32[8,512]{1,0:T(8,128)S(1)}, f32[8,512]{1,0:T(8,128)S(1)}, u32[]{:S(2)}, u32[]{:S(2)}) %collective-permute-start.4) | collective-permute-done | bytes 16416 | tf_op jit(solution)/shard_map/ppermute | solution.py:657
  21.6 0.9 copy-done.1
  23.9 1.1 %residual.1 = (f32[32,512]{1,0:T(8,128)S(1)}, f32[32,512]{1,0:T(8,128)S(1)}, f32[4,4,512]{2,1,0:T(4,128)S(1)}, f32[4,4,512]{2,1,0:T(4,128)S(1)}, f32[8,512]{1,0:...) custom-call(f32[3,4,4,512]{3,2,1,0:T(4,128)S(1)} %copy-done.1, ...), custom_call_target="tpu_custom_call" | custom-call | flops 1000000 | bytes 500000 | tf_op jit(solution)/shard_map/residual/pallas_call | solution.py:631
  25.1 2.7 %collective-permute-start.6 = (f32[8,512]{1,0:T(8,128)S(1)}, f32[8,512]{1,0:T(8,128)S(1)}, u32[]{:S(2)}, u32[]{:S(2)}) collective-permute-start(f32[8,512]{1,0:T(8,128)S(1)} %get-tuple-element.47), channel_id=1, source_target_pairs={{0,224},{32,0},{64,32},{96,64},{128,96},{160,128},{192,160},{224,1... | collective-permute-start | bytes 49160 | tf_op jit(solution)/shard_map/ppermute | solution.py:644
  28.4 5.5 %collective-permute-start.8 = (f32[8,512]{1,0:T(8,128)S(1)}, f32[8,512]{1,0:T(8,128)S(1)}, u32[]{:S(2)}, u32[]{:S(2)}) collective-permute-start(f32[8,512]{1,0:T(8,128)S(1)} %get-tuple-element.49), channel_id=1, source_target_pairs={{0,31},{1,0},{2,1},{3,2},{4,3},{5,4},{6,5},{7,6},{8,7},{9,8},{10,9... | collective-permute-start | bytes 49160 | tf_op jit(solution)/shard_map/ppermute | solution.py:648
  35.0 2.7 %collective-permute-start.10 = (f32[8,512]{1,0:T(8,128)S(1)}, f32[8,512]{1,0:T(8,128)S(1)}, u32[]{:S(2)}, u32[]{:S(2)}) collective-permute-start(f32[8,512]{1,0:T(8,128)S(1)} %get-tuple-element.52), channel_id=1, source_target_pairs={{0,224},{32,0},{64,32},{96,64},{128,96},{160,128},{192,160},{224,1... | collective-permute-start | bytes 49160 | tf_op jit(solution)/shard_map/ppermute | solution.py:644
  37.7 6.2 %collective-permute-start.12 = (f32[8,512]{1,0:T(8,128)S(1)}, f32[8,512]{1,0:T(8,128)S(1)}, u32[]{:S(2)}, u32[]{:S(2)}) collective-permute-start(f32[8,512]{1,0:T(8,128)S(1)} %get-tuple-element.54), channel_id=1, source_target_pairs={{0,31},{1,0},{2,1},{3,2},{4,3},{5,4},{6,5},{7,6},{8,7},{9,8},{10,9... | collective-permute-start | bytes 49160 | tf_op jit(solution)/shard_map/ppermute | solution.py:648
  44.6 4.6 %elastic.1 = (bf16[5,5,5,5,3,128]{5,4,3,2,1,0:T(4,128)(2,1)}, f32[3,4,4,512]{3,2,1,0:T(4,128)S(1)}, f32[16,512]{1,0:T(8,128)S(1)}, f32[16,512]{1,0:T(8,128)S(1)}, f32[8,512]{1,0:T(8,128)S(1)}) custom-call(f32[3,4,4,512]{3,2,1,0:T(4,128)S(1)} %copy-done.2, f32[16,512]{1,0:T(8,128)S(1)} %collective-permute-done.1.lat_above.na, ...), custom_call_target="tpu_custom_call" | custom-call | flops 20000000 | bytes 2000000 | tf_op jit(solution)/shard_map/elastic/pallas_call | solution.py:631
  49.7 2.6 %collective-permute-start.14 = (f32[8,512]{1,0:T(8,128)S(1)}, f32[8,512]{1,0:T(8,128)S(1)}, u32[]{:S(2)}, u32[]{:S(2)}) collective-permute-start(f32[8,512]{1,0:T(8,128)S(1)} %get-tuple-element.59), channel_id=1, source_target_pairs={{0,224},{32,0},{64,32},{96,64},{128,96},{160,128},{192,160},{224,1... | collective-permute-start | bytes 49160 | tf_op jit(solution)/shard_map/ppermute | solution.py:644
  52.2 5.6 %collective-permute-start.16 = (f32[8,512]{1,0:T(8,128)S(1)}, f32[8,512]{1,0:T(8,128)S(1)}, u32[]{:S(2)}, u32[]{:S(2)}) collective-permute-start(f32[8,512]{1,0:T(8,128)S(1)} %get-tuple-element.61), channel_id=1, source_target_pairs={{0,31},{1,0},{2,1},{3,2},{4,3},{5,4},{6,5},{7,6},{8,7},{9,8},{10,9... | collective-permute-start | bytes 49160 | tf_op jit(solution)/shard_map/ppermute | solution.py:648
  57.9 0.8 collective-permute-done.16.lon_above.gd
  58.7 1.0 %moments.1 = f32[256,128]{1,0:T(8,128)} custom-call(f32[4,4,512]{2,1,0:T(4,128)S(1)} %get-tuple-element.43.field.w0, f32[4,4,512]{2,1,0:T(4,128)S(1)} %get-tuple-element.50.field.w1, f32[4,4,512]{2,1,0:T(4,128)S(1)} %get-tuple-element.57.w2, f32[32,512]{1,0:T(8,128)S(1)} %get-tuple-element.44.coef, f32[4,4,512]{2,1,0:T(4,128)S(1)} %get-tuple-element.45.precond, ...), custom_call_target="tpu_custom_call" | custom-call | flops 1000000 | bytes 500000 | tf_op jit(solution)/shard_map/moments/pallas_call | solution.py:631
  59.7 16.3 %all-to-all-start = ((f32[256,1,128]{2,1,0:T(1,128)}), f32[256,1,128]{2,1,0:T(1,128)S(1)}, u32[]{:S(2)}, u32[]{:S(2)}) async-start(f32[256,1,128]{2,1,0:T(1,128)} %bitcast.3), calls=%async_computation | async-start | bytes 262144 | tf_op jit(solution)/shard_map/all_to_all | solution.py:716
  76.0 2.8 %collective-permute-start.17 = (f32[8,512]{1,0:T(8,128)S(1)}, f32[8,512]{1,0:T(8,128)S(1)}, u32[]{:S(2)}, u32[]{:S(2)}) collective-permute-start(f32[8,512]{1,0:T(8,128)S(1)} %get-tuple-element.64), channel_id=1, source_target_pairs={{0,33},{1,34},{2,35},{3,36},{4,37},{5,38},{6,39},{7,40},{8,41},{9,... | collective-permute-start | bytes 49160 | tf_op jit(solution)/shard_map/ppermute | solution.py:657
  78.8 4.4 %collective-permute-done.17.corner = f32[8,512]{1,0:T(8,128)S(1)} collective-permute-done((f32[8,512]{1,0:T(8,128)S(1)}, f32[8,512]{1,0:T(8,128)S(1)}, u32[]{:S(2)}, u32[]{:S(2)}) %collective-permute-start.17) | collective-permute-done | bytes 16416 | tf_op jit(solution)/shard_map/ppermute | solution.py:657
  83.2 5.8 %all-to-all-done = f32[256,1,128]{2,1,0:T(1,128)S(1)} async-done(((f32[256,1,128]{2,1,0:T(1,128)}), f32[256,1,128]{2,1,0:T(1,128)S(1)}, u32[]{:S(2)}, u32[]{:S(2)}) %all-to-all-start) | async-done | bytes 131104 | tf_op jit(solution)/shard_map/all_to_all | solution.py:716
  89.0 1.1 %final.1 = (f32[4,4,512]{2,1,0:T(4,128)}, f32[3,4,4,512]{3,2,1,0:T(4,128)}, f32[3,4,4,512]{3,2,1,0:T(4,128)}) custom-call(f32[256,128]{1,0:T(8,128)S(1)} %bitcast.13, f32[4,4,512]{2,1,0:T(4,128)S(1)} %copy-done.9, f32[4,4,512]{2,1,0:T(4,128)S(1)} %get-tuple-element.43.field.w0, f32[4,4,512]{2,1,0:T(4,128)S(1)} %get-tuple-element.50.field.w1, ...), custom_call_target="tpu_custom_call" | custom-call | flops 1000000 | bytes 500000 | tf_op jit(solution)/shard_map/final/pallas_call | solution.py:631
  (56 shorter events, 6.5 us)
Async XLA Ops:
  5.4 38.6 %copy-start = (bf16[3,5,5,1,5,1,5,128]{7,0,6,5,4,3,2,1:T(4,128)(2,1)S(1)}, bf16[3,5,5,1,5,1,5,128]{7,0,6,5,4,3,2,1:T(4,128)(2,1)}, u32[]{:S(2)}) copy-start(bf16[3,5,5,1,5,1,5,128]{7,0,6,5,4,3,2,1:T(4,128)(2,1)} %param.15) | copy-start | bytes 1440004
  6.1 15.5 %collective-permute-start = (f32[16,512]{1,0:T(8,128)S(1)}, f32[16,512]{1,0:T(8,128)S(1)}, u32[]{:S(2)}, u32[]{:S(2)}) collective-permute-start(f32[16,512]{1,0:T(8,128)S(1)} %get-tuple-element.39), channel_id=1, source_target_pairs={{0,32},{32,64},{64,96},{96,128},{128,160},{160,192},{192,224},{224... | collective-permute-start | bytes 98312 | tf_op jit(solution)/shard_map/ppermute | solution.py:644
  8.5 13.0 %collective-permute-start.1 = (f32[16,512]{1,0:T(8,128)S(1)}, f32[16,512]{1,0:T(8,128)S(1)}, u32[]{:S(2)}, u32[]{:S(2)}) collective-permute-start(f32[16,512]{1,0:T(8,128)S(1)} %get-tuple-element.40), channel_id=1, source_target_pairs={{0,224},{32,0},{64,32},{96,64},{128,96},{160,128},{192,160},{224,1... | collective-permute-start | bytes 98312 | tf_op jit(solution)/shard_map/ppermute | solution.py:644
  12.5 9.1 %collective-permute-start.2 = (f32[16,512]{1,0:T(8,128)S(1)}, f32[16,512]{1,0:T(8,128)S(1)}, u32[]{:S(2)}, u32[]{:S(2)}) collective-permute-start(f32[16,512]{1,0:T(8,128)S(1)} %get-tuple-element.41), channel_id=1, source_target_pairs={{0,1},{1,2},{2,3},{3,4},{4,5},{5,6},{6,7},{7,8},{8,9},{9,10},{10,1... | collective-permute-start | bytes 98312 | tf_op jit(solution)/shard_map/ppermute | solution.py:648
  14.6 7.0 %collective-permute-start.3 = (f32[16,512]{1,0:T(8,128)S(1)}, f32[16,512]{1,0:T(8,128)S(1)}, u32[]{:S(2)}, u32[]{:S(2)}) collective-permute-start(f32[16,512]{1,0:T(8,128)S(1)} %get-tuple-element.42), channel_id=1, source_target_pairs={{0,31},{1,0},{2,1},{3,2},{4,3},{5,4},{6,5},{7,6},{8,7},{9,8},{10,9... | collective-permute-start | bytes 98312 | tf_op jit(solution)/shard_map/ppermute | solution.py:648
  14.6 6.9 %collective-permute-start.4 = (f32[8,512]{1,0:T(8,128)S(1)}, f32[8,512]{1,0:T(8,128)S(1)}, u32[]{:S(2)}, u32[]{:S(2)}) collective-permute-start(f32[8,512]{1,0:T(8,128)S(1)} %get-tuple-element.38.own_code), channel_id=1, source_target_pairs={{0,33},{1,34},{2,35},{3,36},{4,37},{5,38},{6,39},{7,40},{8,41},{9,... | collective-permute-start | bytes 49160 | tf_op jit(solution)/shard_map/ppermute | solution.py:657
  25.0 8.9 %collective-permute-start.5 = (f32[8,512]{1,0:T(8,128)S(1)}, f32[8,512]{1,0:T(8,128)S(1)}, u32[]{:S(2)}, u32[]{:S(2)}) collective-permute-start(f32[8,512]{1,0:T(8,128)S(1)} %get-tuple-element.46), channel_id=1, source_target_pairs={{0,32},{32,64},{64,96},{96,128},{128,160},{160,192},{192,224},{224... | collective-permute-start | bytes 49160 | tf_op jit(solution)/shard_map/ppermute | solution.py:644
  25.1 8.8 %collective-permute-start.6 = (f32[8,512]{1,0:T(8,128)S(1)}, f32[8,512]{1,0:T(8,128)S(1)}, u32[]{:S(2)}, u32[]{:S(2)}) collective-permute-start(f32[8,512]{1,0:T(8,128)S(1)} %get-tuple-element.47), channel_id=1, source_target_pairs={{0,224},{32,0},{64,32},{96,64},{128,96},{160,128},{192,160},{224,1... | collective-permute-start | bytes 49160 | tf_op jit(solution)/shard_map/ppermute | solution.py:644
  27.7 6.8 %collective-permute-start.7 = (f32[8,512]{1,0:T(8,128)S(1)}, f32[8,512]{1,0:T(8,128)S(1)}, u32[]{:S(2)}, u32[]{:S(2)}) collective-permute-start(f32[8,512]{1,0:T(8,128)S(1)} %get-tuple-element.48), channel_id=1, source_target_pairs={{0,1},{1,2},{2,3},{3,4},{4,5},{5,6},{6,7},{7,8},{8,9},{9,10},{10,1... | collective-permute-start | bytes 49160 | tf_op jit(solution)/shard_map/ppermute | solution.py:648
  28.4 6.3 %collective-permute-start.8 = (f32[8,512]{1,0:T(8,128)S(1)}, f32[8,512]{1,0:T(8,128)S(1)}, u32[]{:S(2)}, u32[]{:S(2)}) collective-permute-start(f32[8,512]{1,0:T(8,128)S(1)} %get-tuple-element.49), channel_id=1, source_target_pairs={{0,31},{1,0},{2,1},{3,2},{4,3},{5,4},{6,5},{7,6},{8,7},{9,8},{10,9... | collective-permute-start | bytes 49160 | tf_op jit(solution)/shard_map/ppermute | solution.py:648
  34.7 9.3 %copy-start.2 = (f32[3,4,4,512]{3,2,1,0:T(4,128)S(1)}, f32[3,4,4,512]{3,2,1,0:T(4,128)}, u32[]{:S(2)}) copy-start(f32[3,4,4,512]{3,2,1,0:T(4,128)} %get-tuple-element.74.disp_new.disp) | copy-start | bytes 294916
  34.9 14.2 %collective-permute-start.9 = (f32[8,512]{1,0:T(8,128)S(1)}, f32[8,512]{1,0:T(8,128)S(1)}, u32[]{:S(2)}, u32[]{:S(2)}) collective-permute-start(f32[8,512]{1,0:T(8,128)S(1)} %get-tuple-element.51), channel_id=1, source_target_pairs={{0,32},{32,64},{64,96},{96,128},{128,160},{160,192},{192,224},{224... | collective-permute-start | bytes 49160 | tf_op jit(solution)/shard_map/ppermute | solution.py:644
  35.0 14.1 %collective-permute-start.10 = (f32[8,512]{1,0:T(8,128)S(1)}, f32[8,512]{1,0:T(8,128)S(1)}, u32[]{:S(2)}, u32[]{:S(2)}) collective-permute-start(f32[8,512]{1,0:T(8,128)S(1)} %get-tuple-element.52), channel_id=1, source_target_pairs={{0,224},{32,0},{64,32},{96,64},{128,96},{160,128},{192,160},{224,1... | collective-permute-start | bytes 49160 | tf_op jit(solution)/shard_map/ppermute | solution.py:644
  37.7 11.5 %collective-permute-start.11 = (f32[8,512]{1,0:T(8,128)S(1)}, f32[8,512]{1,0:T(8,128)S(1)}, u32[]{:S(2)}, u32[]{:S(2)}) collective-permute-start(f32[8,512]{1,0:T(8,128)S(1)} %get-tuple-element.53), channel_id=1, source_target_pairs={{0,1},{1,2},{2,3},{3,4},{4,5},{5,6},{6,7},{7,8},{8,9},{9,10},{10,1... | collective-permute-start | bytes 49160 | tf_op jit(solution)/shard_map/ppermute | solution.py:648
  37.7 11.5 %collective-permute-start.12 = (f32[8,512]{1,0:T(8,128)S(1)}, f32[8,512]{1,0:T(8,128)S(1)}, u32[]{:S(2)}, u32[]{:S(2)}) collective-permute-start(f32[8,512]{1,0:T(8,128)S(1)} %get-tuple-element.54), channel_id=1, source_target_pairs={{0,31},{1,0},{2,1},{3,2},{4,3},{5,4},{6,5},{7,6},{8,7},{9,8},{10,9... | collective-permute-start | bytes 49160 | tf_op jit(solution)/shard_map/ppermute | solution.py:648
  49.5 9.2 %collective-permute-start.13 = (f32[24,512]{1,0:T(8,128)S(1)}, f32[24,512]{1,0:T(8,128)S(1)}, u32[]{:S(2)}, u32[]{:S(2)}) collective-permute-start(f32[24,512]{1,0:T(8,128)S(1)} %get-tuple-element.58), channel_id=1, source_target_pairs={{0,32},{32,64},{64,96},{96,128},{128,160},{160,192},{192,224},{224... | collective-permute-start | bytes 147464 | tf_op jit(solution)/shard_map/ppermute | solution.py:644
  49.6 9.1 %collective-permute-start.15 = (f32[24,512]{1,0:T(8,128)S(1)}, f32[24,512]{1,0:T(8,128)S(1)}, u32[]{:S(2)}, u32[]{:S(2)}) collective-permute-start(f32[24,512]{1,0:T(8,128)S(1)} %get-tuple-element.60), channel_id=1, source_target_pairs={{0,1},{1,2},{2,3},{3,4},{4,5},{5,6},{6,7},{7,8},{8,9},{9,10},{10,1... | collective-permute-start | bytes 147464 | tf_op jit(solution)/shard_map/ppermute | solution.py:648
  49.7 8.2 %collective-permute-start.14 = (f32[8,512]{1,0:T(8,128)S(1)}, f32[8,512]{1,0:T(8,128)S(1)}, u32[]{:S(2)}, u32[]{:S(2)}) collective-permute-start(f32[8,512]{1,0:T(8,128)S(1)} %get-tuple-element.59), channel_id=1, source_target_pairs={{0,224},{32,0},{64,32},{96,64},{128,96},{160,128},{192,160},{224,1... | collective-permute-start | bytes 49160 | tf_op jit(solution)/shard_map/ppermute | solution.py:644
  52.2 6.5 %collective-permute-start.16 = (f32[8,512]{1,0:T(8,128)S(1)}, f32[8,512]{1,0:T(8,128)S(1)}, u32[]{:S(2)}, u32[]{:S(2)}) collective-permute-start(f32[8,512]{1,0:T(8,128)S(1)} %get-tuple-element.61), channel_id=1, source_target_pairs={{0,31},{1,0},{2,1},{3,2},{4,3},{5,4},{6,5},{7,6},{8,7},{9,8},{10,9... | collective-permute-start | bytes 49160 | tf_op jit(solution)/shard_map/ppermute | solution.py:648
  59.7 29.3 %copy-start.4 = (f32[3,4,4,512]{3,2,1,0:T(4,128)S(1)}, f32[3,4,4,512]{3,2,1,0:T(4,128)}, u32[]{:S(2)}) copy-start(f32[3,4,4,512]{3,2,1,0:T(4,128)} %vel.3) | copy-start | bytes 294916
  59.7 29.3 %copy-start.6 = (f32[3,4,4,512]{3,2,1,0:T(4,128)S(1)}, f32[3,4,4,512]{3,2,1,0:T(4,128)}, u32[]{:S(2)}) copy-start(f32[3,4,4,512]{3,2,1,0:T(4,128)} %acc.3) | copy-start | bytes 294916
  59.7 29.3 %copy-start.9 = (f32[4,4,512]{2,1,0:T(4,128)S(1)}, f32[4,4,512]{2,1,0:T(4,128)}, u32[]{:S(2)}) copy-start(f32[4,4,512]{2,1,0:T(4,128)} %phi.5) | copy-start | bytes 98308
  59.7 29.3 %all-to-all-start = ((f32[256,1,128]{2,1,0:T(1,128)}), f32[256,1,128]{2,1,0:T(1,128)S(1)}, u32[]{:S(2)}, u32[]{:S(2)}) async-start(f32[256,1,128]{2,1,0:T(1,128)} %bitcast.3), calls=%async_computation | async-start | bytes 262144 | tf_op jit(solution)/shard_map/all_to_all | solution.py:716
  76.0 7.2 %collective-permute-start.17 = (f32[8,512]{1,0:T(8,128)S(1)}, f32[8,512]{1,0:T(8,128)S(1)}, u32[]{:S(2)}, u32[]{:S(2)}) collective-permute-start(f32[8,512]{1,0:T(8,128)S(1)} %get-tuple-element.64), channel_id=1, source_target_pairs={{0,33},{1,34},{2,35},{3,36},{4,37},{5,38},{6,39},{7,40},{8,41},{9,... | collective-permute-start | bytes 49160 | tf_op jit(solution)/shard_map/ppermute | solution.py:657
  (12 other events, 17.6 us)

commit v2 on v1

--- a/solution.py
+++ b/solution.py
@@ -1,5 +1,3 @@
-import functools
-
 import jax
 import jax.numpy as jnp
 import numpy as np
@@ -14,7 +12,7 @@
 LAT, LON = 8, 32
 AXES = ("lat", "lon")
 VMEM = pl.BlockSpec(memory_space=pltpu.VMEM)
-SMEM = pl.BlockSpec(memory_space=pltpu.SMEM)
+HBM = pl.BlockSpec(memory_space=pltpu.HBM)
 
 
 def gll():
@@ -128,14 +126,41 @@
     return jnp.sum(weighted, axis=0, keepdims=True)
 
 
-def messages(fields, up_lat, down_lat, up_lon, down_lon):
-    up_lat[0:4, :] = partial_lat(fields, M_POISSON)
-    up_lat[4:8, :] = partial_lat(fields, M_GRAVITY)
-    down_lat[0:4, :] = fields[0]
-    for i in range(4):
-        up_lon[i : i + 1, :] = partial_lon(fields[i], M_POISSON)
-        up_lon[4 + i : 5 + i, :] = partial_lon(fields[i], M_GRAVITY)
-        down_lon[i : i + 1, :] = fields[i][0:1]
+def even(axis):
+    return lax.rem(lax.axis_index(axis), 2) == 0
+
+
+def pick(axis, for_even, for_odd):
+    return jnp.where(even(axis), for_even, for_odd)
+
+
+def post(axis, outs, up, down):
+    for out, sent in zip(outs, (pick(axis, up, down), pick(axis, down, up))):
+        out[...] = sent[: out.shape[0]]
+
+
+def arrived(axis, first, second):
+    height = min(first.shape[0], second.shape[0])
+    first, second = first[0:height], second[0:height]
+    return pick(axis, second, first), pick(axis, first, second)
+
+
+def stack(rows, height):
+    total = sum(r.shape[0] for r in rows)
+    if total < height:
+        rows = rows + [jnp.zeros((height - total, 512), F32)]
+    return jnp.concatenate(rows, 0)
+
+
+def messages(fields, lat_out, lon_out, extra_lat=(), extra_lon=()):
+    up = [partial_lat(fields, M_POISSON), partial_lat(fields, M_GRAVITY)]
+    height = max(out.shape[0] for out in lat_out)
+    post("lat", lat_out, stack(up + list(extra_lat), height), stack([fields[0]], height))
+    up = [partial_lon(fields[i], M_POISSON) for i in range(4)]
+    up += [partial_lon(fields[i], M_GRAVITY) for i in range(4)]
+    down = [fields[i][0:1] for i in range(4)]
+    height = max(out.shape[0] for out in lon_out)
+    post("lon", lon_out, stack(up + list(extra_lon), height), stack(down, height))
 
 
 def has_next():
@@ -146,7 +171,34 @@
     return jnp.where(lax.axis_index("lat") > 0, 1.0, 0.0).astype(F32)
 
 
-def start_kernel(disp, vel, acc, phi, mat, flag, disp_new, up_lat, down_lat, up_lon, down_lon, code):
+def start_kernel(
+    disp_h, vel_h, acc_h, phi_h, mat_h, flag_h, dens_h,
+    disp_new, disp_out, phi_out, info_out, lon0, lon1,
+    disp, vel, acc, mat, flag, dens, sems,
+):
+    moves = [
+        pltpu.make_async_copy(src, dst, sems.at[n])
+        for n, (src, dst) in enumerate(
+            [
+                (mat_h, mat), (flag_h, flag), (dens_h, dens), (phi_h, phi_out),
+                (disp_h, disp), (vel_h, vel), (acc_h, acc),
+            ]
+        )
+    ]
+    for move in moves:
+        move.start()
+    for move in moves[:3]:
+        move.wait()
+    rho = jnp.zeros((1, 128), F32)
+    for m in range(8):
+        rho = jnp.where(mat[0] == m, dens[m], rho)
+    shell = 1.0 + flag[0].astype(F32)
+    info = jnp.concatenate([rho, shell, jnp.zeros((1, 256), F32)], 1)
+    info_out[...] = jnp.concatenate([rho, shell, jnp.zeros((6, 128), F32)], 0)
+    moves[3].wait()
+    potential = [phi_out[i] for i in range(4)]
+    for move in moves[4:]:
+        move.wait()
     u = []
     for comp in range(3):
         planes = []
@@ -157,34 +209,32 @@
                 + 0.5 * TIME_STEP * TIME_STEP * acc[comp, i]
             )
             disp_new[comp, i] = value
+            disp_out[comp, i] = value
             planes.append(value)
         u.append(planes)
+    up = [partial_lon(u[1][i], M_SOURCE) for i in range(4)]
+    up += [partial_lon(potential[i], M_POISSON) for i in range(4)]
+    up += [partial_lon(potential[i], M_GRAVITY) for i in range(4)]
+    down = [u[comp][i][0:1] for comp in range(3) for i in range(4)]
+    down += [potential[i][0:1] for i in range(4)]
+    post("lon", (lon0, lon1), stack(up + [info], 24), stack(down, 24))
+
+def pack_kernel(disp, phi, own_info, lon_first, lon_second, _, lat0, lat1):
+    below, above = arrived("lon", lon_first, lon_second)
     potential = [phi[i] for i in range(4)]
-    kind = (1 + mat[0] + 8 * flag[0]).astype(F32).astype(BF16)
-    spread = (
-        lax.broadcasted_iota(jnp.int32, (128, 512), 1) // 4
-        == lax.broadcasted_iota(jnp.int32, (128, 512), 0)
-    )
-    spread = jnp.where(spread, 1.0, 0.0).astype(BF16)
-    kinds = jnp.dot(jnp.broadcast_to(kind, (16, 128)), spread, preferred_element_type=F32)
-    kinds = kinds[0:8]
-    code[...] = kinds
-    up_lat[0:4, :] = partial_lat(u[0], M_SOURCE)
-    up_lat[4:8, :] = partial_lat(potential, M_POISSON)
-    up_lat[8:12, :] = partial_lat(potential, M_GRAVITY)
-    up_lat[12:16, :] = kinds[0:4]
-    up_lon[12:16, :] = kinds[0:4]
-    for comp in range(3):
-        down_lat[4 * comp : 4 * comp + 4, :] = u[comp][0]
-        for i in range(4):
-            row = 4 * comp + i
-            down_lon[row : row + 1, :] = u[comp][i][0:1]
-    down_lat[12:16, :] = potential[0]
-    for i in range(4):
-        up_lon[i : i + 1, :] = partial_lon(u[1][i], M_SOURCE)
-        up_lon[4 + i : 5 + i, :] = partial_lon(potential[i], M_POISSON)
-        up_lon[8 + i : 9 + i, :] = partial_lon(potential[i], M_GRAVITY)
-        down_lon[12 + i : 13 + i, :] = potential[i][0:1]
+    info = jnp.concatenate(
+        [own_info[0:1, :], own_info[1:2, :], jnp.zeros((1, 256), F32)], 1
+    )
+    up = [
+        partial_lat([disp[0, i] for i in range(4)], M_SOURCE),
+        partial_lat(potential, M_POISSON),
+        partial_lat(potential, M_GRAVITY),
+        info,
+        below[12:13],
+    ]
+    down = [disp[0, 0], disp[1, 0], disp[2, 0], potential[0]]
+    down += [above[4 * comp : 4 * comp + 1] for comp in range(3)]
+    post("lat", (lat0, lat1), stack(up, 24), stack(down, 24))
 
 
 def lat_rows(factor):
@@ -201,26 +251,38 @@
 
 
 def residual_kernel(
-    disp_new, phi, own_code, lat_below, lat_above, lon_below, lon_above, diag_code, dens,
-    coef, rho_coef, precond_out, w0_out, up_lat, down_lat, up_lon, down_lon,
+    disp_new, phi, own_info, lat_first, lat_second, lon_first, lon_second,
+    coef, rho_coef, precond_out, w0_out, lat0, lat1, lon0, lon1,
 ):
     following, before = has_next(), has_before()
-    codes = jnp.concatenate(
-        [
-            own_code[0:1, :],
-            before * lat_below[12:13, :],
-            lon_below[12:13, :],
-            before * diag_code[0:1, :],
-        ],
-        0,
-    )
-    flagged = codes > 8.5
-    material = jnp.where(flagged, codes - 9.0, codes - 1.0)
-    valid = codes > 0.5
-    rho = jnp.zeros((4, 512), F32)
-    for m in range(8):
-        rho = jnp.where(jnp.abs(material - m) < 0.5, dens[m], rho)
-    rho = jnp.where(valid, rho, 0.0)
+    lat_below, lat_above = arrived("lat", lat_first, lat_second)
+    lon_below, lon_above = arrived("lon", lon_first, lon_second)
+    rho, shell = (
+        jnp.concatenate(
+            [
+                own_info[n : n + 1, :],
+                before * lat_below[12:13, 128 * n : 128 * n + 128],
+                lon_below[12:13, 128 * n : 128 * n + 128],
+                before * lat_below[13:14, 128 * n : 128 * n + 128],
+            ],
+            0,
+        )
+        for n in range(2)
+    )
+    spread = (
+        lax.broadcasted_iota(jnp.int32, (128, 512), 1) // 4
+        == lax.broadcasted_iota(jnp.int32, (128, 512), 0)
+    )
+    spread = jnp.where(spread, 1.0, 0.0).astype(BF16)
+    high, mid, low = split3(rho)
+    parts = jnp.concatenate(
+        [high.astype(F32), mid.astype(F32), low.astype(F32), shell], 0
+    ).astype(BF16)
+    parts = jnp.dot(parts, spread, preferred_element_type=F32)
+    rho = parts[0:4] + parts[4:8] + parts[8:12]
+    shell = parts[12:16]
+    flagged = shell > 1.5
+    valid = shell > 0.5
     stretch = jnp.where(valid, jnp.where(flagged, 3.0, 1.0), 0.0)
     inverse = jnp.where(valid, jnp.where(flagged, 1.0 / 3.0, 1.0), 0.0)
     rho_in = jnp.where(flagged, 0.0, rho)
@@ -311,14 +373,13 @@
         value = (source - image) / precond
         w0_out[i] = value
         w0.append(value)
-    messages(w0, up_lat, down_lat, up_lon, down_lon)
-    for comp in range(3):
-        down_lat[4 + comp : 5 + comp, :] = lon_above[4 * comp : 4 * comp + 1, :]
-    down_lat[7:8, :] = jnp.zeros((1, 512), F32)
-
-
-def poisson(fields, coef, lat_below, lat_above, lon_below, lon_above):
+    messages(w0, (lat0, lat1), (lon0, lon1))
+
+
+def poisson(fields, coef, lat_first, lat_second, lon_first, lon_second):
     following = has_next()
+    lat_below, lat_above = arrived("lat", lat_first, lat_second)
+    lon_below, lon_above = arrived("lon", lon_first, lon_second)
     s_col = (coef[24:25, :], coef[25:26, :])
     s_col_back = (coef[26:27, :], coef[27:28, :])
     x = lat_part(
@@ -331,31 +392,44 @@
     return [x[i] + y[i] + z[i] for i in range(4)]
 
 
-def next_kernel(
-    last, field, coef, precond, lat_below, lat_above, lon_below, lon_above, *rest
-):
-    if last:
-        lat_force, lon_force, out, up_lat, down_lat, up_lon, down_lon = rest
-    else:
-        out, up_lat, down_lat, up_lon, down_lon = rest
+def step(field, coef, precond, halo, out):
     fields = [field[i] for i in range(4)]
-    image = poisson(fields, coef, lat_below, lat_above, lon_below, lon_above)
+    image = poisson(fields, coef, *halo)
     result = []
     for i in range(4):
         value = image[i] / precond[i] - fields[i]
         out[i] = value
         result.append(value)
-    messages(result, up_lat, down_lat, up_lon, down_lon)
-    down_lat[4:8, :] = jnp.zeros((4, 512), F32)
-    down_lon[4:8, :] = jnp.zeros((4, 512), F32)
-    if last:
-        up_lat[8:24, :] = lat_force[...]
-        up_lon[8:24, :] = lon_force[...]
-
-
-def moment_kernel(w0, w1, w2, coef, precond, lat_below, lat_above, lon_below, lon_above, out):
+    return result
+
+
+def second_kernel(
+    field, coef, precond, lat_first, lat_second, lon_first, lon_second, lon_force,
+    out, lat0, lat1, lon0, lon1,
+):
+    result = step(field, coef, precond, (lat_first, lat_second, lon_first, lon_second), out)
+    messages(result, (lat0, lat1), (lon0, lon1), (), (lon_force[...],))
+
+
+def third_kernel(
+    field, coef, precond, lat_first, lat_second, lon_first, lon_second, lat_force,
+    out, lat0, lat1, lon0, lon1,
+):
+    result = step(field, coef, precond, (lat_first, lat_second, lon_first, lon_second), out)
+    below, _ = arrived("lon", lon_first, lon_second)
+    first = column([1.0, 0.0, 0.0, 0.0])
+    edges = []
+    for comp in range(3):
+        corner = 12 + 5 * comp
+        edges.append(
+            lat_force[4 * comp : 4 * comp + 4, :] + first * below[corner : corner + 1]
+        )
+    messages(result, (lat0, lat1), (lon0, lon1), edges)
+
+
+def moment_kernel(w0, w1, w2, coef, precond, lat_first, lat_second, lon_first, lon_second, out):
     fields = [w2[i] for i in range(4)]
-    image = poisson(fields, coef, lat_below, lat_above, lon_below, lon_above)
+    image = poisson(fields, coef, lat_first, lat_second, lon_first, lon_second)
     sums = [None] * 6
     for i in range(4):
         m = precond[i]
@@ -416,8 +490,8 @@
 
 
 def final_kernel(
-    moments, phi, w0, w1, w2, rho_coef, own_force, corner,
-    ma, mb, mc, md, na, nb, nc, nd, fa, fb, fc, fd, ga, gb, gc, gd,
+    moments, phi, w0, w1, w2, rho_coef, own_force,
+    a0, a1, a2, a3, b0, b1, b2, b3, c0, c1, c2, c3, d0, d1, d2, d3,
     vel, acc, phi_new, acc_new, vel_new,
 ):
     total = jnp.sum(moments[...], axis=0, keepdims=True)
@@ -440,6 +514,14 @@
         phi_new[i] = value
         potential.append(value)
     following, before = has_next(), has_before()
+    ma, na = arrived("lat", a0, a1)
+    mb, nb = arrived("lat", b0, b1)
+    mc, nc = arrived("lat", c0, c1)
+    md, nd = arrived("lat", d0, d1)
+    fa, ga = arrived("lon", a2, a3)
+    fb, gb = arrived("lon", b2, b3)
+    fc, gc = arrived("lon", c2, c3)
+    fd, gd = arrived("lon", d2, d3)
     lat_below = combined(ma[8:12, :], mb[4:8, :], mc[4:8, :], md[4:8, :])
     lat_above = following * combined(na[12:16, :], nb[0:4, :], nc[0:4, :], nd[0:4, :])
     lon_below = combined(fa[8:12, :], fb[4:8, :], fc[4:8, :], fd[4:8, :])
@@ -463,10 +545,9 @@
         mass = 0.5 * W[i] * mass
         for comp in range(3):
             force = own_force[comp, i]
-            force = force + first * fd[8 + 5 * comp + i : 9 + 5 * comp + i, :]
+            force = force + first * fc[8 + 5 * comp + i : 9 + 5 * comp + i, :]
             if i == 0:
                 edge = md[8 + 4 * comp : 12 + 4 * comp, :]
-                edge = edge + first * corner[comp : comp + 1, :]
                 force = force + before * edge
             value = (-gravity[comp][i] - force) / mass
             acc_new[comp, i] = value
@@ -481,43 +562,82 @@
     return high, mid, low
 
 
-def elastic_kernel(
-    disp, lat_above, lon_above, corner, mat, moduli, decay, strength, memory,
-    memory_new, force, lat_force, lon_force, corner_force,
-    points, elems, stiff, devs, old, new, flux, perm,
+def prepare_kernel(
+    disp, mat_h, moduli_h, decay_h, strength_h, stiff, rates, perm, elems,
+    points, mat, moduli, decay, strength, sems,
 ):
-    following = has_next()
-    points[...] = jnp.zeros(points.shape, F32)
-    for comp in range(3):
-        for a in range(4):
-            base = (comp * 5 + a) * 8
-            points[base : base + 4, :] = disp[comp, a]
-            row = 4 * comp + a
-            points[base + 4 : base + 5, :] = lon_above[row : row + 1, :]
-        base = (comp * 5 + 4) * 8
-        points[base : base + 4, :] = following * lat_above[4 * comp : 4 * comp + 4, :]
-        points[base + 4 : base + 5, :] = following * corner[4 + comp : 5 + comp, :]
+    moves = [
+        pltpu.make_async_copy(src, dst, sems.at[n])
+        for n, (src, dst) in enumerate(
+            [(mat_h, mat), (moduli_h, moduli), (decay_h, decay), (strength_h, strength)]
+        )
+    ]
+    for move in moves:
+        move.start()
     for c in range(4):
         hit = lax.broadcasted_iota(jnp.int32, (128, 512), 1) == (
             4 * lax.broadcasted_iota(jnp.int32, (128, 512), 0) + c
         )
         perm[128 * c : 128 * c + 128, :] = jnp.where(hit, 1.0, 0.0).astype(BF16)
-    parts = jnp.concatenate(split3(points[...]), 0)
-    taken = lax.dot_general(
-        parts, perm[...], (((1,), (1,)), ((), ())), preferred_element_type=F32
-    )
-    taken = taken[0:128] + taken[128:256] + taken[256:384]
-    for c in range(4):
-        elems[c] = taken[:, 128 * c : 128 * c + 128]
-    lane = lanes((128, 128))
-    elems[4] = jnp.where(lane < 127, pltpu.roll(taken[:, 0:128], 127, 1), 0.0)
+    points[...] = jnp.zeros(points.shape, F32)
+    for comp in range(3):
+        for a in range(4):
+            base = (comp * 4 + a) * 8
+            points[base : base + 4, :] = disp[comp, a]
+    to_nodes(points[...], perm, elems)
+    for move in moves:
+        move.wait()
     onehot = [mat[0] == m for m in range(8)]
     for k in range(6):
         for l in range(k, 6):
             value = jnp.zeros((1, 128), F32)
             for m in range(8):
-                value = jnp.where(onehot[m], moduli[m, k, l], value)
+                value = jnp.where(onehot[m], moduli[k, m, l], value)
             stiff[6 * k + l : 6 * k + l + 1, :] = value
+    for l in range(3):
+        rates[l : l + 1, :] = jnp.full((1, 128), decay[l], F32)
+        rates[3 + l : 4 + l, :] = jnp.full((1, 128), (1.0 - decay[l]) * strength[l], F32)
+
+
+def to_nodes(points, perm, elems):
+    rows = points.shape[0]
+    parts = jnp.concatenate(split3(points), 0)
+    taken = lax.dot_general(
+        parts, perm[...], (((1,), (1,)), ((), ())), preferred_element_type=F32
+    )
+    taken = taken[0:rows] + taken[rows : 2 * rows] + taken[2 * rows : 3 * rows]
+    for c in range(4):
+        elems[c] = taken[:, 128 * c : 128 * c + 128]
+    lane = lanes((rows, 128))
+    elems[4] = jnp.where(lane < 127, pltpu.roll(taken[:, 0:128], 127, 1), 0.0)
+
+
+def elastic_kernel(
+    lat_first, lat_second, lon_first, lon_second, stiff, rates, perm, own, memory,
+    memory_new, force, lat_force, lon_force,
+    points, edge, elems, devs, old, new, flux,
+):
+    following = has_next()
+    _, lat_above = arrived("lat", lat_first, lat_second)
+    _, lon_above = arrived("lon", lon_first, lon_second)
+    points[...] = jnp.zeros(points.shape, F32)
+    for comp in range(3):
+        points[8 * comp : 8 * comp + 4, :] = following * lat_above[4 * comp : 4 * comp + 4]
+        points[8 * comp + 4 : 8 * comp + 5, :] = following * lat_above[16 + comp : 17 + comp]
+    points[24:36, :] = lon_above[0:12]
+    to_nodes(points[...], perm, edge)
+    fifth = sublanes((8, 128)) == 4
+    for c in range(5):
+        for comp in range(3):
+            for a in range(4):
+                base, row = (comp * 5 + a) * 8, 24 + 4 * comp + a
+                kept = own[c, (comp * 4 + a) * 8 : (comp * 4 + a) * 8 + 8, :]
+                elems[c, base : base + 8, :] = jnp.where(
+                    fifth, row_of(edge[c, 24:40, :], row - 24, 8), kept
+                )
+            base = (comp * 5 + 4) * 8
+            elems[c, base : base + 8, :] = edge[c, 8 * comp : 8 * comp + 8, :]
+    lane = lanes((128, 128))
     slopes = [
         by_index(sublanes((8, 128)), [2.0 * DERIV[b][p] for b in range(5)] + [0.0])
         for p in range(5)
@@ -573,8 +693,7 @@
                 total = None
                 for l in range(3):
                     was = old[pl.ds(4 * c + l, 8, stride=20), :]
-                    rate = decay[l]
-                    now = rate * was + ((1.0 - rate) * strength[l]) * dev
+                    now = rates[l : l + 1, :] * was + rates[3 + l : 4 + l, :] * dev
                     now = now.astype(BF16).astype(F32)
                     new[pl.ds(4 * c + l, 8, stride=20), :] = now
                     total = now if total is None else total + now
@@ -614,7 +733,6 @@
     given = given[0:128] + given[128:256] + given[256:384]
     lat_force[12:16, :] = jnp.zeros((4, 512), F32)
     lon_force[15:16, :] = jnp.zeros((1, 512), F32)
-    corner_force[...] = jnp.zeros((8, 512), F32)
     for comp in range(3):
         for a in range(5):
             base = (comp * 5 + a) * 8
@@ -624,10 +742,9 @@
             else:
                 lat_force[4 * comp : 4 * comp + 4, :] = given[base : base + 4]
                 lon_force[5 * comp + 4 : 5 * comp + 5, :] = given[base + 4 : base + 5]
-                corner_force[comp : comp + 1, :] = given[base + 4 : base + 5]
-
-
-def call(kernel, name, outs, ins, args, scratch=(), flops=1000000, moved=500000):
+
+
+def call(kernel, name, outs, ins, args, scratch=(), flops=1000000, moved=500000, vmem=24):
     return pl.pallas_call(
         kernel,
         name=name,
@@ -635,30 +752,26 @@
         in_specs=ins,
         out_specs=[VMEM] * len(outs),
         scratch_shapes=list(scratch),
-        compiler_params=pltpu.CompilerParams(vmem_limit_bytes=24 * 1024 * 1024),
+        compiler_params=pltpu.CompilerParams(vmem_limit_bytes=vmem * 1024 * 1024),
         cost_estimate=pl.CostEstimate(flops=flops, bytes_accessed=moved, transcendentals=0),
     )(*args)
 
 
-def lat_ring(array, by):
-    return lax.ppermute(array, "lat", [(i, (i + by) % LAT) for i in range(LAT)])
-
-
-def lon_ring(array, by):
-    return lax.ppermute(array, "lon", [(i, (i + by) % LON) for i in range(LON)])
-
-
-def diagonal(array):
-    pairs = [
-        (e * LON + f, (e + 1) % LAT * LON + (f + 1) % LON)
-        for e in range(LAT)
-        for f in range(LON)
-    ]
-    return lax.ppermute(array, AXES, pairs)
-
-
-def star(up_lat, down_lat, up_lon, down_lon):
-    return (lat_ring(up_lat, 1), lat_ring(down_lat, -1), lon_ring(up_lon, 1), lon_ring(down_lon, -1))
+def swap(array, axis, size, parity):
+    pairs = []
+    for i in range(parity, size, 2):
+        j = (i + 1) % size
+        pairs += [(i, j), (j, i)]
+    return lax.ppermute(array, axis, pairs)
+
+
+def swap_lat(first, second):
+    return swap(first, "lat", LAT, 0), swap(second, "lat", LAT, 1)
+
+
+def swap_lon(first, second):
+    other = swap(second, "lon", LON, 1)
+    return swap(first, "lon", LON, 0), other
 
 
 def per_device(
@@ -668,57 +781,94 @@
     field = ((4, 4, 512), F32)
     vector = ((3, 4, 4, 512), F32)
     r8, r16, r24, r32 = (((n, 512), F32) for n in (8, 16, 24, 32))
-    disp_new, *sent, code = call(
-        start_kernel, "start", [vector, r16, r16, r16, r16, r8], [VMEM] * 6,
-        (displacement, velocity, acceleration, potential, materials, shell_flags),
-    )
-    halo_a = star(*sent)
-    diag_code = diagonal(code)
+    info = ((8, 128), F32)
+    kept = pltpu.with_memory_space_constraint
+    disp_new, disp, phi, own_info, *sent = call(
+        start_kernel, "start", [vector, vector, field, info, r16, r24], [HBM] * 7,
+        [
+            kept(array, pltpu.HBM)
+            for array in (
+                displacement, velocity, acceleration, potential, materials, shell_flags, densities
+            )
+        ],
+        [
+            pltpu.VMEM((3, 4, 4, 512), F32),
+            pltpu.VMEM((3, 4, 4, 512), F32),
+            pltpu.VMEM((3, 4, 4, 512), F32),
+            pltpu.VMEM((1, 1, 128), jnp.int32),
+            pltpu.VMEM((1, 1, 128), jnp.int32),
+            pltpu.SMEM((8,), F32),
+            pltpu.SemaphoreType.DMA((7,)),
+        ],
+    )
+    lon_a = swap_lon(*sent)
+    tables = call(
+        prepare_kernel, "prepare",
+        [((40, 128), F32), info, ((512, 512), BF16), ((5, 96, 128), F32)],
+        [VMEM] + [HBM] * 4,
+        [disp]
+        + [
+            kept(array, pltpu.HBM)
+            for array in (materials, moduli.transpose(1, 0, 2), decay, strength)
+        ],
+        [
+            pltpu.VMEM((96, 512), F32),
+            pltpu.VMEM((1, 1, 128), jnp.int32),
+            pltpu.SMEM((6, 8, 6), F32),
+            pltpu.SMEM((3,), F32),
+            pltpu.SMEM((3,), F32),
+            pltpu.SemaphoreType.DMA((4,)),
+        ],
+    )
+    lat_a = call(
+        pack_kernel, "pack", [r24, r24], [VMEM] * 6,
+        (disp, phi, own_info, *lon_a, tables[1]),
+    )
+    halo_a = (*swap_lat(*lat_a), *lon_a)
     coef, rho_coef, precond, w0, *sent = call(
-        residual_kernel, "residual", [r32, r32, field, field, r8, r8, r8, r8],
-        [VMEM] * 8 + [SMEM],
-        (disp_new, potential, code, *halo_a, diag_code, densities),
-    )
-    halo_b = star(*sent)
-    w1, *sent = call(
-        functools.partial(next_kernel, False), "second", [field, r8, r8, r8, r8], [VMEM] * 7,
-        (w0, coef, precond, *halo_b),
-    )
-    halo_c = star(*sent)
+        residual_kernel, "residual", [r32, r32, field, field, r8, r8, r8, r16], [VMEM] * 7,
+        (disp, phi, own_info, *halo_a),
+    )
+    lon_b = swap_lon(*sent[2:])
+    halo_b = (*swap_lat(*sent[:2]), *lon_b)
     memory = memory_vars.reshape(3, 5, 5, 5, 5, 128).transpose(1, 2, 3, 4, 0, 5)
-    memory_new, force, lat_force, lon_force, corner_force = call(
+    memory_new, force, lat_force, lon_force = call(
         elastic_kernel, "elastic",
-        [((5, 5, 5, 5, 3, 128), BF16), vector, r16, r16, r8],
-        [VMEM] * 5 + [SMEM] * 3 + [VMEM],
-        (disp_new, halo_a[1], halo_a[3], halo_b[1], materials, moduli, decay, strength, memory),
+        [((5, 5, 5, 5, 3, 128), BF16), vector, r16, r16],
+        [VMEM] * 9,
+        (*halo_a, *tables, memory),
         [
-            pltpu.VMEM((128, 512), F32),
+            pltpu.VMEM((48, 512), F32),
+            pltpu.VMEM((5, 48, 128), F32),
             pltpu.VMEM((5, 128, 128), F32),
-            pltpu.VMEM((40, 128), F32),
             pltpu.VMEM((25, 8, 128), F32),
             pltpu.VMEM((160, 128), F32),
             pltpu.VMEM((160, 128), F32),
             pltpu.VMEM((6, 25, 8, 128), F32),
-            pltpu.VMEM((512, 512), BF16),
         ],
         flops=20000000, moved=2000000,
     )
+    w1, *sent = call(
+        second_kernel, "second", [field, r8, r8, r24, r32], [VMEM] * 8,
+        (w0, coef, precond, *halo_b, lon_force),
+    )
+    lon_c = swap_lon(*sent[2:])
+    halo_c = (*swap_lat(*sent[:2]), *lon_c)
     w2, *sent = call(
-        functools.partial(next_kernel, True), "third", [field, r24, r8, r24, r8], [VMEM] * 9,
-        (w1, coef, precond, *halo_c, lat_force, lon_force),
-    )
-    halo_d = star(*sent)
-    corner = diagonal(corner_force)
+        third_kernel, "third", [field, r24, r24, r8, r32], [VMEM] * 8,
+        (w1, coef, precond, *halo_c, lat_force),
+    )
+    lon_d = swap_lon(*sent[2:])
+    halo_d = (*swap_lat(*sent[:2]), *lon_d)
     (line,) = call(
         moment_kernel, "moments", [((LAT * LON, 128), F32)], [VMEM] * 9,
         (w0, w1, w2, coef, precond, *halo_d),
     )
     moments = lax.all_to_all(line, AXES, 0, 0, tiled=True)
     phi_new, acc_new, vel_new = call(
-        final_kernel, "final", [field, vector, vector], [VMEM] * 26,
+        final_kernel, "final", [field, vector, vector], [VMEM] * 25,
         (
-            moments, potential, w0, w1, w2, rho_coef, force, corner,
-            *(halo[k] for k in range(4) for halo in (halo_a, halo_b, halo_c, halo_d)),
+            moments, phi, w0, w1, w2, rho_coef, force, *halo_a, *halo_b, *halo_c, *halo_d,
             velocity, acceleration,
         ),
     )

time: 90.6 us -> 67.8 us (0.75)
  starting transfers between devices: 53.9 us -> 31 us
  blocking collectives: 0 us -> 22.3 us
  waiting for transfers between devices: 18.8 us -> 4.25 us
  local copies, waits for them, and re-layouts: 7.71 us -> 0.02 us
    all_to_all x0 -> x1, blocking collectives: none -> 22.3 us  [per_device(): moments = lax.all_to_all(line, AXES, 0, 0, tiled=True)]
    all_to_all x1 -> x0, starting transfers between devices: 16.3 us -> none  [per_device(): moments = lax.all_to_all(line, AXES, 0, 0, tiled=True)]
    ppermute x18 -> x16, waiting for transfers between devices: 13.1 us -> 4.25 us  [swap(): return lax.ppermute(array, axis, pairs)]
    unnamed x35 -> x6, local copies, waits for them, and re-layouts: 7.71 us -> 0.02 us
    ppermute x18 -> x16, starting transfers between devices: 37.5 us -> 31 us  [swap(): return lax.ppermute(array, axis, pairs)]
    all_to_all x1 -> x0, waiting for transfers between devices: 5.76 us -> none  [per_device(): moments = lax.all_to_all(line, AXES, 0, 0, tiled=True)]
    pallas_call x7 -> x9, Pallas kernels: 8.98 us -> 9.18 us  [call(): pl.pallas_call(kernel, name=name, out_shape=[jax.ShapeDtypeStruct(s, d) f...]
  transfers between devices with their start and end apart: 19 -> 16, of which waited for: 6 -> 4; matrix products, arithmetic and copies ran while one was open for 0% -> 0% of each run, Pallas kernels for 5% -> 7%
where the time goes in v2:
time: 67.8 us; the launch traced here: 67.5 us
  starting transfers between devices  31 us (46%)
  blocking collectives  22.3 us (33%)
  Pallas kernels  9.18 us (14%)
  waiting for transfers between devices  4.25 us (6%)
  between operations  0.78 us (1%)
    ppermute x16, starting transfers between devices, swap(): return lax.ppermute(array, axis, pairs)  31 us
    all_to_all x1, blocking collectives, per_device(): moments = lax.all_to_all(line, AXES, 0, 0, tiled=True)  22.3 us
    pallas_call x9, Pallas kernels, call(): pl.pallas_call(kernel, name=name, out_shape=[jax.ShapeDtypeStruct(s, d) f...  9.18 us
    ppermute x16, waiting for transfers between devices, swap(): return lax.ppermute(array, axis, pairs)  4.25 us
  transfers between devices with their start and end apart: 16, of which 4 were waited for; matrix products, arithmetic and copies ran while one was open for 0% of the time, Pallas kernels for 7%

profile of v2, /device:TPU:1, one launch (start us, length us, event | category | flops | bytes accessed | tf_op | source)
XLA Modules:
  0.0 67.5 jit_solution(6633630843136247167)
XLA Ops:
  0.6 1.8 %start.1 = (f32[3,4,4,512]{3,2,1,0:T(4,128)}, f32[3,4,4,512]{3,2,1,0:T(4,128)S(1)}, f32[4,4,512]{2,1,0:T(4,128)S(1)}, f32[8,128]{1,0:T(8,128)S(1)}, f32[16,512]{1,0:T(8,128)S(1)}, /*index=5*/f32[24,512]{1,0:T(8,128)S(1)}) custom-call(f32[3,4,4,512]{3,2,1,0:T(4,128)} %disp_h.1, f32[3,4,4,512]{3,2,1,0:T(4,128)} %vel.1, f32[3,4,4,512]{3,2,1,0:T(4,128)} %acc.1, ...), custom_call_target="tpu_custom_call" | custom-call | flops 1000000 | bytes 500000 | tf_op jit(solution)/shard_map/start/pallas_call | solution.py:748
  2.5 2.8 %collective-permute-start.1 = (f32[24,512]{1,0:T(8,128)S(1)}, f32[24,512]{1,0:T(8,128)S(1)}, u32[]{:S(2)}, u32[]{:S(2)}) collective-permute-start(f32[24,512]{1,0:T(8,128)S(1)} %get-tuple-element.47), channel_id=1, source_target_pairs={{1,2},{2,1},{3,4},{4,3},{5,6},{6,5},{7,8},{8,7},{9,10},{10,9},{11,... | collective-permute-start | bytes 147464 | tf_op jit(solution)/shard_map/ppermute | solution.py:765
  5.3 3.5 %collective-permute-start = (f32[16,512]{1,0:T(8,128)S(1)}, f32[16,512]{1,0:T(8,128)S(1)}, u32[]{:S(2)}, u32[]{:S(2)}) collective-permute-start(f32[16,512]{1,0:T(8,128)S(1)} %get-tuple-element.46), channel_id=1, source_target_pairs={{0,1},{1,0},{2,3},{3,2},{4,5},{5,4},{6,7},{7,6},{8,9},{9,8},{10,11... | collective-permute-start | bytes 98312 | tf_op jit(solution)/shard_map/ppermute | solution.py:765
  8.7 1.3 %prepare.1 = (f32[40,128]{1,0:T(8,128)S(1)}, f32[8,128]{1,0:T(8,128)S(1)}, bf16[512,512]{1,0:T(8,128)(2,1)S(1)}, f32[5,96,128]{2,1,0:T(8,128)S(1)}) custom-call(f32[3,4,4,512]{3,2,1,0:T(4,128)S(1)} %get-tuple-element.43.disp.disp_new, s32[1,1,128]{2,1,0:T(1,128)} %mat_h.3, f32[6,8,6]{2,1,0:T(8,128)} %bitcast.16, f32[3]{0:T(128)} %decay_h.1, f32[3]{0:T(128)} %strength_h.1), custom_call_target="tpu_custom_call" | custom-call | flops 1000000 | bytes 500000 | tf_op jit(solution)/shard_map/prepare/pallas_call | solution.py:748
  10.1 1.7 %collective-permute-start.2 = (f32[24,512]{1,0:T(8,128)S(1)}, f32[24,512]{1,0:T(8,128)S(1)}, u32[]{:S(2)}, u32[]{:S(2)}) collective-permute-start(f32[24,512]{1,0:T(8,128)S(1)} %get-tuple-element.49), channel_id=1, source_target_pairs={{0,32},{32,0},{64,96},{96,64},{128,160},{160,128},{192,224},{224,1... | collective-permute-start | bytes 147464 | tf_op jit(solution)/shard_map/ppermute | solution.py:765
  11.9 4.7 %collective-permute-start.3 = (f32[24,512]{1,0:T(8,128)S(1)}, f32[24,512]{1,0:T(8,128)S(1)}, u32[]{:S(2)}, u32[]{:S(2)}) collective-permute-start(f32[24,512]{1,0:T(8,128)S(1)} %get-tuple-element.50), channel_id=1, source_target_pairs={{32,64},{64,32},{96,128},{128,96},{160,192},{192,160},{224,0},{0,2... | collective-permute-start | bytes 147464 | tf_op jit(solution)/shard_map/ppermute | solution.py:765
  16.5 1.5 %collective-permute-done.3.lat_second.a1 = f32[24,512]{1,0:T(8,128)S(1)} collective-permute-done((f32[24,512]{1,0:T(8,128)S(1)}, f32[24,512]{1,0:T(8,128)S(1)}, u32[]{:S(2)}, u32[]{:S(2)}) %collective-permute-start.3) | collective-permute-done | bytes 49184 | tf_op jit(solution)/shard_map/ppermute | solution.py:765
  18.0 0.6 residual.1
  18.8 2.8 %collective-permute-start.5 = (f32[8,512]{1,0:T(8,128)S(1)}, f32[8,512]{1,0:T(8,128)S(1)}, u32[]{:S(2)}, u32[]{:S(2)}) collective-permute-start(f32[8,512]{1,0:T(8,128)S(1)} %get-tuple-element.55), channel_id=1, source_target_pairs={{32,64},{64,32},{96,128},{128,96},{160,192},{192,160},{224,0},{0,2... | collective-permute-start | bytes 49160 | tf_op jit(solution)/shard_map/ppermute | solution.py:765
  21.6 5.5 %collective-permute-start.6 = (f32[8,512]{1,0:T(8,128)S(1)}, f32[8,512]{1,0:T(8,128)S(1)}, u32[]{:S(2)}, u32[]{:S(2)}) collective-permute-start(f32[8,512]{1,0:T(8,128)S(1)} %get-tuple-element.56), channel_id=1, source_target_pairs={{0,1},{1,0},{2,3},{3,2},{4,5},{5,4},{6,7},{7,6},{8,9},{9,8},{10,11... | collective-permute-start | bytes 49160 | tf_op jit(solution)/shard_map/ppermute | solution.py:765
  27.1 3.3 %elastic.1 = (bf16[5,5,5,5,3,128]{5,4,3,2,1,0:T(4,128)(2,1)}, f32[3,4,4,512]{3,2,1,0:T(4,128)S(1)}, f32[16,512]{1,0:T(8,128)S(1)}, f32[16,512]{1,0:T(8,128)S(1)}) custom-call(f32[24,512]{1,0:T(8,128)S(1)} %collective-permute-done.2.lat_first.a0, f32[24,512]{1,0:T(8,128)S(1)} %collective-permute-done.3.lat_second.a1, ...), custom_call_target="tpu_custom_call" | custom-call | flops 20000000 | bytes 2000000 | tf_op jit(solution)/shard_map/elastic/pallas_call | solution.py:748
  30.9 1.6 %collective-permute-start.10 = (f32[24,512]{1,0:T(8,128)S(1)}, f32[24,512]{1,0:T(8,128)S(1)}, u32[]{:S(2)}, u32[]{:S(2)}) collective-permute-start(f32[24,512]{1,0:T(8,128)S(1)} %get-tuple-element.65), channel_id=1, source_target_pairs={{0,1},{1,0},{2,3},{3,2},{4,5},{5,4},{6,7},{7,6},{8,9},{9,8},{10,11... | collective-permute-start | bytes 147464 | tf_op jit(solution)/shard_map/ppermute | solution.py:765
  32.4 2.2 %collective-permute-start.9 = (f32[8,512]{1,0:T(8,128)S(1)}, f32[8,512]{1,0:T(8,128)S(1)}, u32[]{:S(2)}, u32[]{:S(2)}) collective-permute-start(f32[8,512]{1,0:T(8,128)S(1)} %get-tuple-element.64), channel_id=1, source_target_pairs={{32,64},{64,32},{96,128},{128,96},{160,192},{192,160},{224,0},{0,2... | collective-permute-start | bytes 49160 | tf_op jit(solution)/shard_map/ppermute | solution.py:765
  34.6 0.4 collective-permute-done.8.lat_first.c0
  35.0 1.5 %collective-permute-done.9.lat_second.c1 = f32[8,512]{1,0:T(8,128)S(1)} collective-permute-done((f32[8,512]{1,0:T(8,128)S(1)}, f32[8,512]{1,0:T(8,128)S(1)}, u32[]{:S(2)}, u32[]{:S(2)}) %collective-permute-start.9) | collective-permute-done | bytes 16416 | tf_op jit(solution)/shard_map/ppermute | solution.py:765
  36.5 0.3 third.1
  36.8 1.2 %collective-permute-start.15 = (f32[32,512]{1,0:T(8,128)S(1)}, f32[32,512]{1,0:T(8,128)S(1)}, u32[]{:S(2)}, u32[]{:S(2)}) collective-permute-start(f32[32,512]{1,0:T(8,128)S(1)} %get-tuple-element.72), channel_id=1, source_target_pairs={{1,2},{2,1},{3,4},{4,3},{5,6},{6,5},{7,8},{8,7},{9,10},{10,9},{11,... | collective-permute-start | bytes 196616 | tf_op jit(solution)/shard_map/ppermute | solution.py:765
  38.0 0.5 collective-permute-start.12
  38.5 2.2 %collective-permute-start.13 = (f32[24,512]{1,0:T(8,128)S(1)}, f32[24,512]{1,0:T(8,128)S(1)}, u32[]{:S(2)}, u32[]{:S(2)}) collective-permute-start(f32[24,512]{1,0:T(8,128)S(1)} %get-tuple-element.70), channel_id=1, source_target_pairs={{32,64},{64,32},{96,128},{128,96},{160,192},{192,160},{224,0},{0,2... | collective-permute-start | bytes 147464 | tf_op jit(solution)/shard_map/ppermute | solution.py:765
  40.7 2.2 %collective-permute-start.14 = (f32[8,512]{1,0:T(8,128)S(1)}, f32[8,512]{1,0:T(8,128)S(1)}, u32[]{:S(2)}, u32[]{:S(2)}) collective-permute-start(f32[8,512]{1,0:T(8,128)S(1)} %get-tuple-element.71), channel_id=1, source_target_pairs={{0,1},{1,0},{2,3},{3,2},{4,5},{5,4},{6,7},{7,6},{8,9},{9,8},{10,11... | collective-permute-start | bytes 49160 | tf_op jit(solution)/shard_map/ppermute | solution.py:765
  42.9 0.8 %collective-permute-done.14.lon_first.d2 = f32[8,512]{1,0:T(8,128)S(1)} collective-permute-done((f32[8,512]{1,0:T(8,128)S(1)}, f32[8,512]{1,0:T(8,128)S(1)}, u32[]{:S(2)}, u32[]{:S(2)}) %collective-permute-start.14) | collective-permute-done | bytes 16416 | tf_op jit(solution)/shard_map/ppermute | solution.py:765
  43.7 0.3 moments.1
  44.1 22.3 %all_to_all.11 = f32[256,1,128]{2,1,0:T(1,128)S(1)} all-to-all(f32[256,1,128]{2,1,0:T(1,128)S(1)} %bitcast.15), channel_id=1, replica_groups=mesh['lat'=8,'lon'=32] {'lat','lon'}, dimensions={0} | all-to-all | bytes 262144 | tf_op jit(solution)/shard_map/all_to_all | solution.py:867
  66.4 1.1 %final.1 = (f32[4,4,512]{2,1,0:T(4,128)}, f32[3,4,4,512]{3,2,1,0:T(4,128)}, f32[3,4,4,512]{3,2,1,0:T(4,128)}) custom-call(f32[256,128]{1,0:T(8,128)S(1)} %bitcast.14, f32[4,4,512]{2,1,0:T(4,128)S(1)} %get-tuple-element.44.phi, f32[4,4,512]{2,1,0:T(4,128)S(1)} %get-tuple-element.51.field.w0, f32[4,4,512]{2,1,0:T(4,128)S(1)} %get-tuple-element.62.field.w1, ...), custom_call_target="tpu_custom_call" | custom-call | flops 1000000 | bytes 500000 | tf_op jit(solution)/shard_map/final/pallas_call | solution.py:748
  (24 shorter events, 0.6 us)
Async XLA Ops:
  0.6 26.5 %copy-start = (bf16[3,5,5,1,5,1,5,128]{7,0,6,5,4,3,2,1:T(4,128)(2,1)S(1)}, bf16[3,5,5,1,5,1,5,128]{7,0,6,5,4,3,2,1:T(4,128)(2,1)}, u32[]{:S(2)}) copy-start(bf16[3,5,5,1,5,1,5,128]{7,0,6,5,4,3,2,1:T(4,128)(2,1)} %param.15) | copy-start | bytes 1440004
  2.5 7.6 %collective-permute-start.1 = (f32[24,512]{1,0:T(8,128)S(1)}, f32[24,512]{1,0:T(8,128)S(1)}, u32[]{:S(2)}, u32[]{:S(2)}) collective-permute-start(f32[24,512]{1,0:T(8,128)S(1)} %get-tuple-element.47), channel_id=1, source_target_pairs={{1,2},{2,1},{3,4},{4,3},{5,6},{6,5},{7,8},{8,7},{9,10},{10,9},{11,... | collective-permute-start | bytes 147464 | tf_op jit(solution)/shard_map/ppermute | solution.py:765
  5.3 4.8 %collective-permute-start = (f32[16,512]{1,0:T(8,128)S(1)}, f32[16,512]{1,0:T(8,128)S(1)}, u32[]{:S(2)}, u32[]{:S(2)}) collective-permute-start(f32[16,512]{1,0:T(8,128)S(1)} %get-tuple-element.46), channel_id=1, source_target_pairs={{0,1},{1,0},{2,3},{3,2},{4,5},{5,4},{6,7},{7,6},{8,9},{9,8},{10,11... | collective-permute-start | bytes 98312 | tf_op jit(solution)/shard_map/ppermute | solution.py:765
  10.1 6.4 %collective-permute-start.2 = (f32[24,512]{1,0:T(8,128)S(1)}, f32[24,512]{1,0:T(8,128)S(1)}, u32[]{:S(2)}, u32[]{:S(2)}) collective-permute-start(f32[24,512]{1,0:T(8,128)S(1)} %get-tuple-element.49), channel_id=1, source_target_pairs={{0,32},{32,0},{64,96},{96,64},{128,160},{160,128},{192,224},{224,1... | collective-permute-start | bytes 147464 | tf_op jit(solution)/shard_map/ppermute | solution.py:765
  11.9 6.1 %collective-permute-start.3 = (f32[24,512]{1,0:T(8,128)S(1)}, f32[24,512]{1,0:T(8,128)S(1)}, u32[]{:S(2)}, u32[]{:S(2)}) collective-permute-start(f32[24,512]{1,0:T(8,128)S(1)} %get-tuple-element.50), channel_id=1, source_target_pairs={{32,64},{64,32},{96,128},{128,96},{160,192},{192,160},{224,0},{0,2... | collective-permute-start | bytes 147464 | tf_op jit(solution)/shard_map/ppermute | solution.py:765
  18.6 11.9 %collective-permute-start.7 = (f32[16,512]{1,0:T(8,128)S(1)}, f32[16,512]{1,0:T(8,128)S(1)}, u32[]{:S(2)}, u32[]{:S(2)}) collective-permute-start(f32[16,512]{1,0:T(8,128)S(1)} %get-tuple-element.57), channel_id=1, source_target_pairs={{1,2},{2,1},{3,4},{4,3},{5,6},{6,5},{7,8},{8,7},{9,10},{10,9},{11,... | collective-permute-start | bytes 98312 | tf_op jit(solution)/shard_map/ppermute | solution.py:765
  18.7 11.7 %collective-permute-start.4 = (f32[8,512]{1,0:T(8,128)S(1)}, f32[8,512]{1,0:T(8,128)S(1)}, u32[]{:S(2)}, u32[]{:S(2)}) collective-permute-start(f32[8,512]{1,0:T(8,128)S(1)} %get-tuple-element.54), channel_id=1, source_target_pairs={{0,32},{32,0},{64,96},{96,64},{128,160},{160,128},{192,224},{224,1... | collective-permute-start | bytes 49160 | tf_op jit(solution)/shard_map/ppermute | solution.py:765
  18.8 11.6 %collective-permute-start.5 = (f32[8,512]{1,0:T(8,128)S(1)}, f32[8,512]{1,0:T(8,128)S(1)}, u32[]{:S(2)}, u32[]{:S(2)}) collective-permute-start(f32[8,512]{1,0:T(8,128)S(1)} %get-tuple-element.55), channel_id=1, source_target_pairs={{32,64},{64,32},{96,128},{128,96},{160,192},{192,160},{224,0},{0,2... | collective-permute-start | bytes 49160 | tf_op jit(solution)/shard_map/ppermute | solution.py:765
  21.6 8.9 %collective-permute-start.6 = (f32[8,512]{1,0:T(8,128)S(1)}, f32[8,512]{1,0:T(8,128)S(1)}, u32[]{:S(2)}, u32[]{:S(2)}) collective-permute-start(f32[8,512]{1,0:T(8,128)S(1)} %get-tuple-element.56), channel_id=1, source_target_pairs={{0,1},{1,0},{2,3},{3,2},{4,5},{5,4},{6,7},{7,6},{8,9},{9,8},{10,11... | collective-permute-start | bytes 49160 | tf_op jit(solution)/shard_map/ppermute | solution.py:765
  30.8 5.8 %collective-permute-start.11 = (f32[32,512]{1,0:T(8,128)S(1)}, f32[32,512]{1,0:T(8,128)S(1)}, u32[]{:S(2)}, u32[]{:S(2)}) collective-permute-start(f32[32,512]{1,0:T(8,128)S(1)} %get-tuple-element.66), channel_id=1, source_target_pairs={{1,2},{2,1},{3,4},{4,3},{5,6},{6,5},{7,8},{8,7},{9,10},{10,9},{11,... | collective-permute-start | bytes 196616 | tf_op jit(solution)/shard_map/ppermute | solution.py:765
  30.9 5.7 %collective-permute-start.10 = (f32[24,512]{1,0:T(8,128)S(1)}, f32[24,512]{1,0:T(8,128)S(1)}, u32[]{:S(2)}, u32[]{:S(2)}) collective-permute-start(f32[24,512]{1,0:T(8,128)S(1)} %get-tuple-element.65), channel_id=1, source_target_pairs={{0,1},{1,0},{2,3},{3,2},{4,5},{5,4},{6,7},{7,6},{8,9},{9,8},{10,11... | collective-permute-start | bytes 147464 | tf_op jit(solution)/shard_map/ppermute | solution.py:765
  32.4 2.6 %collective-permute-start.8 = (f32[8,512]{1,0:T(8,128)S(1)}, f32[8,512]{1,0:T(8,128)S(1)}, u32[]{:S(2)}, u32[]{:S(2)}) collective-permute-start(f32[8,512]{1,0:T(8,128)S(1)} %get-tuple-element.63), channel_id=1, source_target_pairs={{0,32},{32,0},{64,96},{96,64},{128,160},{160,128},{192,224},{224,1... | collective-permute-start | bytes 49160 | tf_op jit(solution)/shard_map/ppermute | solution.py:765
  32.4 4.1 %collective-permute-start.9 = (f32[8,512]{1,0:T(8,128)S(1)}, f32[8,512]{1,0:T(8,128)S(1)}, u32[]{:S(2)}, u32[]{:S(2)}) collective-permute-start(f32[8,512]{1,0:T(8,128)S(1)} %get-tuple-element.64), channel_id=1, source_target_pairs={{32,64},{64,32},{96,128},{128,96},{160,192},{192,160},{224,0},{0,2... | collective-permute-start | bytes 49160 | tf_op jit(solution)/shard_map/ppermute | solution.py:765
  36.8 6.9 %collective-permute-start.15 = (f32[32,512]{1,0:T(8,128)S(1)}, f32[32,512]{1,0:T(8,128)S(1)}, u32[]{:S(2)}, u32[]{:S(2)}) collective-permute-start(f32[32,512]{1,0:T(8,128)S(1)} %get-tuple-element.72), channel_id=1, source_target_pairs={{1,2},{2,1},{3,4},{4,3},{5,6},{6,5},{7,8},{8,7},{9,10},{10,9},{11,... | collective-permute-start | bytes 196616 | tf_op jit(solution)/shard_map/ppermute | solution.py:765
  38.0 5.7 %collective-permute-start.12 = (f32[24,512]{1,0:T(8,128)S(1)}, f32[24,512]{1,0:T(8,128)S(1)}, u32[]{:S(2)}, u32[]{:S(2)}) collective-permute-start(f32[24,512]{1,0:T(8,128)S(1)} %get-tuple-element.69), channel_id=1, source_target_pairs={{0,32},{32,0},{64,96},{96,64},{128,160},{160,128},{192,224},{224,1... | collective-permute-start | bytes 147464 | tf_op jit(solution)/shard_map/ppermute | solution.py:765
  38.5 5.2 %collective-permute-start.13 = (f32[24,512]{1,0:T(8,128)S(1)}, f32[24,512]{1,0:T(8,128)S(1)}, u32[]{:S(2)}, u32[]{:S(2)}) collective-permute-start(f32[24,512]{1,0:T(8,128)S(1)} %get-tuple-element.70), channel_id=1, source_target_pairs={{32,64},{64,32},{96,128},{128,96},{160,192},{192,160},{224,0},{0,2... | collective-permute-start | bytes 147464 | tf_op jit(solution)/shard_map/ppermute | solution.py:765
  40.7 3.0 %collective-permute-start.14 = (f32[8,512]{1,0:T(8,128)S(1)}, f32[8,512]{1,0:T(8,128)S(1)}, u32[]{:S(2)}, u32[]{:S(2)}) collective-permute-start(f32[8,512]{1,0:T(8,128)S(1)} %get-tuple-element.71), channel_id=1, source_target_pairs={{0,1},{1,0},{2,3},{3,2},{4,5},{5,4},{6,7},{7,6},{8,9},{9,8},{10,11... | collective-permute-start | bytes 49160 | tf_op jit(solution)/shard_map/ppermute | solution.py:765
  44.1 22.3 %copy-start.1 = (f32[3,4,4,512]{3,2,1,0:T(4,128)S(1)}, f32[3,4,4,512]{3,2,1,0:T(4,128)}, u32[]{:S(2)}) copy-start(f32[3,4,4,512]{3,2,1,0:T(4,128)} %vel.1) | copy-start | bytes 294916
  44.1 22.3 %copy-start.2 = (f32[3,4,4,512]{3,2,1,0:T(4,128)S(1)}, f32[3,4,4,512]{3,2,1,0:T(4,128)}, u32[]{:S(2)}) copy-start(f32[3,4,4,512]{3,2,1,0:T(4,128)} %acc.1) | copy-start | bytes 294916

commit v3 on v2

--- a/solution.py
+++ b/solution.py
@@ -251,7 +251,7 @@
 
 
 def residual_kernel(
-    disp_new, phi, own_info, lat_first, lat_second, lon_first, lon_second,
+    disp_new, phi, own_info, lat_first, lat_second, lon_first, lon_second, _,
     coef, rho_coef, precond_out, w0_out, lat0, lat1, lon0, lon1,
 ):
     following, before = has_next(), has_before()
@@ -412,7 +412,7 @@
 
 
 def third_kernel(
-    field, coef, precond, lat_first, lat_second, lon_first, lon_second, lat_force,
+    field, coef, precond, lat_first, lat_second, lon_first, lon_second, lat_force, _,
     out, lat0, lat1, lon0, lon1,
 ):
     result = step(field, coef, precond, (lat_first, lat_second, lon_first, lon_second), out)
@@ -599,6 +599,33 @@
         rates[3 + l : 4 + l, :] = jnp.full((1, 128), (1.0 - decay[l]) * strength[l], F32)
 
 
+def unpack_kernel(memory, rates, _, decayed, flag, old):
+    for d in range(5):
+        for a in range(5):
+            for b in range(5):
+                for c in range(5):
+                    row = (b * 5 + c) * 4
+                    old[row : row + 3, :] = memory[d, a, b, c].astype(F32)
+            for c in range(5):
+                for l in range(3):
+                    was = old[pl.ds(4 * c + l, 8, stride=20), :]
+                    decayed[((d * 5 + a) * 5 + c) * 3 + l] = rates[l : l + 1, :] * was
+    flag[...] = jnp.zeros((8, 128), F32)
+
+
+def repack_kernel(dense, memory_new, flag, new):
+    for d in range(5):
+        for a in range(5):
+            for c in range(5):
+                for l in range(3):
+                    new[pl.ds(4 * c + l, 8, stride=20), :] = dense[((d * 5 + a) * 5 + c) * 3 + l]
+            for b in range(5):
+                for c in range(5):
+                    row = (b * 5 + c) * 4
+                    memory_new[d, a, b, c] = new[row : row + 3, :].astype(BF16)
+    flag[...] = jnp.zeros((8, 128), F32)
+
+
 def to_nodes(points, perm, elems):
     rows = points.shape[0]
     parts = jnp.concatenate(split3(points), 0)
@@ -613,9 +640,9 @@
 
 
 def elastic_kernel(
-    lat_first, lat_second, lon_first, lon_second, stiff, rates, perm, own, memory,
-    memory_new, force, lat_force, lon_force,
-    points, edge, elems, devs, old, new, flux,
+    lat_first, lat_second, lon_first, lon_second, stiff, rates, perm, own, decayed,
+    dense, force, lat_force, lon_force,
+    points, edge, elems, devs, flux,
 ):
     following = has_next()
     _, lat_above = arrived("lat", lat_first, lat_second)
@@ -683,25 +710,17 @@
             elastic_of.append(elastic)
         relaxed = []
         for d in range(5):
-            for b in range(5):
-                for c in range(5):
-                    row = (b * 5 + c) * 4
-                    old[row : row + 3, :] = memory[d, a, b, c].astype(F32)
             sums = []
             for c in range(5):
                 dev = devs[d * 5 + c]
                 total = None
                 for l in range(3):
-                    was = old[pl.ds(4 * c + l, 8, stride=20), :]
-                    now = rates[l : l + 1, :] * was + rates[3 + l : 4 + l, :] * dev
+                    pos = ((d * 5 + a) * 5 + c) * 3 + l
+                    now = decayed[pos] + rates[3 + l : 4 + l, :] * dev
                     now = now.astype(BF16).astype(F32)
-                    new[pl.ds(4 * c + l, 8, stride=20), :] = now
+                    dense[pos] = now
                     total = now if total is None else total + now
                 sums.append(total)
-            for b in range(5):
-                for c in range(5):
-                    row = (b * 5 + c) * 4
-                    memory_new[d, a, b, c] = new[row : row + 3, :].astype(BF16)
             relaxed.append(sums)
         for c in range(5):
             e = elastic_of[c]
@@ -825,25 +844,26 @@
         (disp, phi, own_info, *lon_a, tables[1]),
     )
     halo_a = (*swap_lat(*lat_a), *lon_a)
+    memory = memory_vars.reshape(3, 5, 5, 5, 5, 128).transpose(1, 2, 3, 4, 0, 5)
+    every = ((375, 8, 128), F32)
+    decayed, unpacked = call(
+        unpack_kernel, "unpack", [every, info], [VMEM] * 3, (memory, tables[1], lat_a[0]),
+        [pltpu.VMEM((160, 128), F32)],
+    )
     coef, rho_coef, precond, w0, *sent = call(
-        residual_kernel, "residual", [r32, r32, field, field, r8, r8, r8, r16], [VMEM] * 7,
-        (disp, phi, own_info, *halo_a),
+        residual_kernel, "residual", [r32, r32, field, field, r8, r8, r8, r16], [VMEM] * 8,
+        (disp, phi, own_info, *halo_a, unpacked),
     )
     lon_b = swap_lon(*sent[2:])
     halo_b = (*swap_lat(*sent[:2]), *lon_b)
-    memory = memory_vars.reshape(3, 5, 5, 5, 5, 128).transpose(1, 2, 3, 4, 0, 5)
-    memory_new, force, lat_force, lon_force = call(
-        elastic_kernel, "elastic",
-        [((5, 5, 5, 5, 3, 128), BF16), vector, r16, r16],
-        [VMEM] * 9,
-        (*halo_a, *tables, memory),
+    dense, force, lat_force, lon_force = call(
+        elastic_kernel, "elastic", [every, vector, r16, r16], [VMEM] * 9,
+        (*halo_a, *tables, decayed),
         [
             pltpu.VMEM((48, 512), F32),
             pltpu.VMEM((5, 48, 128), F32),
             pltpu.VMEM((5, 128, 128), F32),
             pltpu.VMEM((25, 8, 128), F32),
-            pltpu.VMEM((160, 128), F32),
-            pltpu.VMEM((160, 128), F32),
             pltpu.VMEM((6, 25, 8, 128), F32),
         ],
         flops=20000000, moved=2000000,
@@ -854,9 +874,13 @@
     )
     lon_c = swap_lon(*sent[2:])
     halo_c = (*swap_lat(*sent[:2]), *lon_c)
+    memory_new, packed = call(
+        repack_kernel, "repack", [((5, 5, 5, 5, 3, 128), BF16), info], [VMEM], (dense,),
+        [pltpu.VMEM((160, 128), F32)],
+    )
     w2, *sent = call(
-        third_kernel, "third", [field, r24, r24, r8, r32], [VMEM] * 8,
-        (w1, coef, precond, *halo_c, lat_force),
+        third_kernel, "third", [field, r24, r24, r8, r32], [VMEM] * 9,
+        (w1, coef, precond, *halo_c, lat_force, packed),
     )
     lon_d = swap_lon(*sent[2:])
     halo_d = (*swap_lat(*sent[:2]), *lon_d)

time: 67.8 us -> 67.1 us (0.990)
  waiting for transfers between devices: 4.25 us -> 1.09 us
  starting transfers between devices: 31 us -> 32.6 us
  local copies, waits for them, and re-layouts: 0.02 us -> 1.09 us
    ppermute x16, waiting for transfers between devices: 4.25 us -> 1.09 us  [swap(): return lax.ppermute(array, axis, pairs)]
    ppermute x16, starting transfers between devices: 31 us -> 32.6 us  [swap(): return lax.ppermute(array, axis, pairs)]
    unnamed x6, local copies, waits for them, and re-layouts: 0.02 us -> 1.09 us
    pallas_call x9 -> x11, Pallas kernels: 9.18 us -> 9.2 us  [call(): pl.pallas_call(kernel, name=name, out_shape=[jax.ShapeDtypeStruct(s, d) f...]
  transfers between devices with their start and end apart: 16 -> 16, of which waited for: 4 -> 3; matrix products, arithmetic and copies ran while one was open for 0% -> 0% of each run, Pallas kernels for 7% -> 7%
where the time goes in v3:
time: 67.1 us; the launch traced here: 66.8 us
  starting transfers between devices  32.6 us (49%)
  blocking collectives  22 us (33%)
  Pallas kernels  9.2 us (14%)
  waiting for transfers between devices  1.09 us (2%)
  local copies, waits for them, and re-layouts  1.09 us (2%)
  between operations  0.81 us (1%)
    ppermute x16, starting transfers between devices, swap(): return lax.ppermute(array, axis, pairs)  32.6 us
    all_to_all x1, blocking collectives, per_device(): moments = lax.all_to_all(line, AXES, 0, 0, tiled=True)  22 us
    pallas_call x11, Pallas kernels, call(): pl.pallas_call(kernel, name=name, out_shape=[jax.ShapeDtypeStruct(s, d) f...  9.2 us
  transfers between devices with their start and end apart: 16, of which 3 were waited for; matrix products, arithmetic and copies ran while one was open for 0% of the time, Pallas kernels for 7%

profile of v3, /device:TPU:1, one launch (start us, length us, event | category | flops | bytes accessed | tf_op | source)
XLA Modules:
  0.0 66.8 jit_solution(9878620027012912548)
XLA Ops:
  0.6 1.8 %start.1 = (f32[3,4,4,512]{3,2,1,0:T(4,128)}, f32[3,4,4,512]{3,2,1,0:T(4,128)S(1)}, f32[4,4,512]{2,1,0:T(4,128)S(1)}, f32[8,128]{1,0:T(8,128)S(1)}, f32[16,512]{1,0:T(8,128)S(1)}, /*index=5*/f32[24,512]{1,0:T(8,128)S(1)}) custom-call(f32[3,4,4,512]{3,2,1,0:T(4,128)} %disp_h.1, f32[3,4,4,512]{3,2,1,0:T(4,128)} %vel.1, f32[3,4,4,512]{3,2,1,0:T(4,128)} %acc.1, ...), custom_call_target="tpu_custom_call" | custom-call | flops 1000000 | bytes 500000 | tf_op jit(solution)/shard_map/start/pallas_call | solution.py:767
  2.4 2.8 %collective-permute-start.1 = (f32[24,512]{1,0:T(8,128)S(1)}, f32[24,512]{1,0:T(8,128)S(1)}, u32[]{:S(2)}, u32[]{:S(2)}) collective-permute-start(f32[24,512]{1,0:T(8,128)S(1)} %get-tuple-element.51), channel_id=1, source_target_pairs={{1,2},{2,1},{3,4},{4,3},{5,6},{6,5},{7,8},{8,7},{9,10},{10,9},{11,... | collective-permute-start | bytes 147464 | tf_op jit(solution)/shard_map/ppermute | solution.py:784
  5.2 3.5 %collective-permute-start = (f32[16,512]{1,0:T(8,128)S(1)}, f32[16,512]{1,0:T(8,128)S(1)}, u32[]{:S(2)}, u32[]{:S(2)}) collective-permute-start(f32[16,512]{1,0:T(8,128)S(1)} %get-tuple-element.50), channel_id=1, source_target_pairs={{0,1},{1,0},{2,3},{3,2},{4,5},{5,4},{6,7},{7,6},{8,9},{9,8},{10,11... | collective-permute-start | bytes 98312 | tf_op jit(solution)/shard_map/ppermute | solution.py:784
  8.7 1.3 %prepare.1 = (f32[40,128]{1,0:T(8,128)S(1)}, f32[8,128]{1,0:T(8,128)S(1)}, bf16[512,512]{1,0:T(8,128)(2,1)S(1)}, f32[5,96,128]{2,1,0:T(8,128)S(1)}) custom-call(f32[3,4,4,512]{3,2,1,0:T(4,128)S(1)} %get-tuple-element.47.disp.disp_new, s32[1,1,128]{2,1,0:T(1,128)} %mat_h.3, f32[6,8,6]{2,1,0:T(8,128)} %bitcast.16, f32[3]{0:T(128)} %decay_h.1, f32[3]{0:T(128)} %strength_h.1), custom_call_target="tpu_custom_call" | custom-call | flops 1000000 | bytes 500000 | tf_op jit(solution)/shard_map/prepare/pallas_call | solution.py:767
  10.1 1.7 %collective-permute-start.2 = (f32[24,512]{1,0:T(8,128)S(1)}, f32[24,512]{1,0:T(8,128)S(1)}, u32[]{:S(2)}, u32[]{:S(2)}) collective-permute-start(f32[24,512]{1,0:T(8,128)S(1)} %get-tuple-element.53._), channel_id=1, source_target_pairs={{0,32},{32,0},{64,96},{96,64},{128,160},{160,128},{192,224},{224,1... | collective-permute-start | bytes 147464 | tf_op jit(solution)/shard_map/ppermute | solution.py:784
  11.8 4.7 %collective-permute-start.3 = (f32[24,512]{1,0:T(8,128)S(1)}, f32[24,512]{1,0:T(8,128)S(1)}, u32[]{:S(2)}, u32[]{:S(2)}) collective-permute-start(f32[24,512]{1,0:T(8,128)S(1)} %get-tuple-element.54), channel_id=1, source_target_pairs={{32,64},{64,32},{96,128},{128,96},{160,192},{192,160},{224,0},{0,2... | collective-permute-start | bytes 147464 | tf_op jit(solution)/shard_map/ppermute | solution.py:784
  16.5 1.1 %copy-done = bf16[3,5,5,1,5,1,5,128]{7,0,6,5,4,3,2,1:T(4,128)(2,1)S(1)} copy-done((bf16[3,5,5,1,5,1,5,128]{7,0,6,5,4,3,2,1:T(4,128)(2,1)S(1)}, bf16[3,5,5,1,5,1,5,128]{7,0,6,5,4,3,2,1:T(4,128)(2,1)}, u32[]{:S(2)}) %copy-start) | copy-done | bytes 480024
  17.9 0.6 residual.1
  18.8 2.8 %collective-permute-start.5 = (f32[8,512]{1,0:T(8,128)S(1)}, f32[8,512]{1,0:T(8,128)S(1)}, u32[]{:S(2)}, u32[]{:S(2)}) collective-permute-start(f32[8,512]{1,0:T(8,128)S(1)} %get-tuple-element.60), channel_id=1, source_target_pairs={{32,64},{64,32},{96,128},{128,96},{160,192},{192,160},{224,0},{0,2... | collective-permute-start | bytes 49160 | tf_op jit(solution)/shard_map/ppermute | solution.py:784
  21.5 5.5 %collective-permute-start.6 = (f32[8,512]{1,0:T(8,128)S(1)}, f32[8,512]{1,0:T(8,128)S(1)}, u32[]{:S(2)}, u32[]{:S(2)}) collective-permute-start(f32[8,512]{1,0:T(8,128)S(1)} %get-tuple-element.61), channel_id=1, source_target_pairs={{0,1},{1,0},{2,3},{3,2},{4,5},{5,4},{6,7},{7,6},{8,9},{9,8},{10,11... | collective-permute-start | bytes 49160 | tf_op jit(solution)/shard_map/ppermute | solution.py:784
  27.1 1.8 %elastic.1 = (f32[375,8,128]{2,1,0:T(8,128)S(1)}, f32[3,4,4,512]{3,2,1,0:T(4,128)S(1)}, f32[16,512]{1,0:T(8,128)S(1)}, f32[16,512]{1,0:T(8,128)S(1)}) custom-call(f32[24,512]{1,0:T(8,128)S(1)} %collective-permute-done.2.lat_first.a0, f32[24,512]{1,0:T(8,128)S(1)} %collective-permute-done.3.lat_second.a1, f32[16,512]{1,0:T(8,128)S(1)} %collective-permute-done.lon_first.a2, ...), custom_call_target="tpu_custom_call" | custom-call | flops 20000000 | bytes 2000000 | tf_op jit(solution)/shard_map/elastic/pallas_call | solution.py:767
  29.0 0.3 second.1
  29.3 1.8 %collective-permute-start.10 = (f32[24,512]{1,0:T(8,128)S(1)}, f32[24,512]{1,0:T(8,128)S(1)}, u32[]{:S(2)}, u32[]{:S(2)}) collective-permute-start(f32[24,512]{1,0:T(8,128)S(1)} %get-tuple-element.71), channel_id=1, source_target_pairs={{0,1},{1,0},{2,3},{3,2},{4,5},{5,4},{6,7},{7,6},{8,9},{9,8},{10,11... | collective-permute-start | bytes 147464 | tf_op jit(solution)/shard_map/ppermute | solution.py:784
  31.1 2.7 %collective-permute-start.9 = (f32[8,512]{1,0:T(8,128)S(1)}, f32[8,512]{1,0:T(8,128)S(1)}, u32[]{:S(2)}, u32[]{:S(2)}) collective-permute-start(f32[8,512]{1,0:T(8,128)S(1)} %get-tuple-element.70), channel_id=1, source_target_pairs={{32,64},{64,32},{96,128},{128,96},{160,192},{192,160},{224,0},{0,2... | collective-permute-start | bytes 49160 | tf_op jit(solution)/shard_map/ppermute | solution.py:784
  33.8 1.3 %repack.1 = (bf16[5,5,5,5,3,128]{5,4,3,2,1,0:T(4,128)(2,1)}, f32[8,128]{1,0:T(8,128)S(1)}) custom-call(f32[375,8,128]{2,1,0:T(8,128)S(1)} %get-tuple-element.74.dense), custom_call_target="tpu_custom_call" | custom-call | flops 1000000 | bytes 500000 | tf_op jit(solution)/shard_map/repack/pallas_call | solution.py:767
  35.2 0.3 third.1
  35.5 1.0 %collective-permute-start.15 = (f32[32,512]{1,0:T(8,128)S(1)}, f32[32,512]{1,0:T(8,128)S(1)}, u32[]{:S(2)}, u32[]{:S(2)}) collective-permute-start(f32[32,512]{1,0:T(8,128)S(1)} %get-tuple-element.80), channel_id=1, source_target_pairs={{1,2},{2,1},{3,4},{4,3},{5,6},{6,5},{7,8},{8,7},{9,10},{10,9},{11,... | collective-permute-start | bytes 196616 | tf_op jit(solution)/shard_map/ppermute | solution.py:784
  36.5 0.5 collective-permute-start.12
  36.9 2.2 %collective-permute-start.13 = (f32[24,512]{1,0:T(8,128)S(1)}, f32[24,512]{1,0:T(8,128)S(1)}, u32[]{:S(2)}, u32[]{:S(2)}) collective-permute-start(f32[24,512]{1,0:T(8,128)S(1)} %get-tuple-element.78), channel_id=1, source_target_pairs={{32,64},{64,32},{96,128},{128,96},{160,192},{192,160},{224,0},{0,2... | collective-permute-start | bytes 147464 | tf_op jit(solution)/shard_map/ppermute | solution.py:784
  39.1 3.3 %collective-permute-start.14 = (f32[8,512]{1,0:T(8,128)S(1)}, f32[8,512]{1,0:T(8,128)S(1)}, u32[]{:S(2)}, u32[]{:S(2)}) collective-permute-start(f32[8,512]{1,0:T(8,128)S(1)} %get-tuple-element.79), channel_id=1, source_target_pairs={{0,1},{1,0},{2,3},{3,2},{4,5},{5,4},{6,7},{7,6},{8,9},{9,8},{10,11... | collective-permute-start | bytes 49160 | tf_op jit(solution)/shard_map/ppermute | solution.py:784
  42.5 0.8 %collective-permute-done.14.lon_first.d2 = f32[8,512]{1,0:T(8,128)S(1)} collective-permute-done((f32[8,512]{1,0:T(8,128)S(1)}, f32[8,512]{1,0:T(8,128)S(1)}, u32[]{:S(2)}, u32[]{:S(2)}) %collective-permute-start.14) | collective-permute-done | bytes 16416 | tf_op jit(solution)/shard_map/ppermute | solution.py:784
  43.3 0.3 moments.1
  43.7 22.0 %all_to_all.11 = f32[256,1,128]{2,1,0:T(1,128)S(1)} all-to-all(f32[256,1,128]{2,1,0:T(1,128)S(1)} %bitcast.15), channel_id=1, replica_groups=mesh['lat'=8,'lon'=32] {'lat','lon'}, dimensions={0} | all-to-all | bytes 262144 | tf_op jit(solution)/shard_map/all_to_all | solution.py:891
  65.7 1.1 %final.1 = (f32[4,4,512]{2,1,0:T(4,128)}, f32[3,4,4,512]{3,2,1,0:T(4,128)}, f32[3,4,4,512]{3,2,1,0:T(4,128)}) custom-call(f32[256,128]{1,0:T(8,128)S(1)} %bitcast.14, f32[4,4,512]{2,1,0:T(4,128)S(1)} %get-tuple-element.48.phi, f32[4,4,512]{2,1,0:T(4,128)S(1)} %get-tuple-element.56.field.w0, f32[4,4,512]{2,1,0:T(4,128)S(1)} %get-tuple-element.68.field.w1, ...), custom_call_target="tpu_custom_call" | custom-call | flops 1000000 | bytes 500000 | tf_op jit(solution)/shard_map/final/pallas_call | solution.py:767
  (26 shorter events, 0.8 us)
Async XLA Ops:
  2.4 7.6 %collective-permute-start.1 = (f32[24,512]{1,0:T(8,128)S(1)}, f32[24,512]{1,0:T(8,128)S(1)}, u32[]{:S(2)}, u32[]{:S(2)}) collective-permute-start(f32[24,512]{1,0:T(8,128)S(1)} %get-tuple-element.51), channel_id=1, source_target_pairs={{1,2},{2,1},{3,4},{4,3},{5,6},{6,5},{7,8},{8,7},{9,10},{10,9},{11,... | collective-permute-start | bytes 147464 | tf_op jit(solution)/shard_map/ppermute | solution.py:784
  5.2 4.8 %collective-permute-start = (f32[16,512]{1,0:T(8,128)S(1)}, f32[16,512]{1,0:T(8,128)S(1)}, u32[]{:S(2)}, u32[]{:S(2)}) collective-permute-start(f32[16,512]{1,0:T(8,128)S(1)} %get-tuple-element.50), channel_id=1, source_target_pairs={{0,1},{1,0},{2,3},{3,2},{4,5},{5,4},{6,7},{7,6},{8,9},{9,8},{10,11... | collective-permute-start | bytes 98312 | tf_op jit(solution)/shard_map/ppermute | solution.py:784
  10.1 7.7 %collective-permute-start.2 = (f32[24,512]{1,0:T(8,128)S(1)}, f32[24,512]{1,0:T(8,128)S(1)}, u32[]{:S(2)}, u32[]{:S(2)}) collective-permute-start(f32[24,512]{1,0:T(8,128)S(1)} %get-tuple-element.53._), channel_id=1, source_target_pairs={{0,32},{32,0},{64,96},{96,64},{128,160},{160,128},{192,224},{224,1... | collective-permute-start | bytes 147464 | tf_op jit(solution)/shard_map/ppermute | solution.py:784
  11.8 6.1 %collective-permute-start.3 = (f32[24,512]{1,0:T(8,128)S(1)}, f32[24,512]{1,0:T(8,128)S(1)}, u32[]{:S(2)}, u32[]{:S(2)}) collective-permute-start(f32[24,512]{1,0:T(8,128)S(1)} %get-tuple-element.54), channel_id=1, source_target_pairs={{32,64},{64,32},{96,128},{128,96},{160,192},{192,160},{224,0},{0,2... | collective-permute-start | bytes 147464 | tf_op jit(solution)/shard_map/ppermute | solution.py:784
  16.5 1.1 %copy-start = (bf16[3,5,5,1,5,1,5,128]{7,0,6,5,4,3,2,1:T(4,128)(2,1)S(1)}, bf16[3,5,5,1,5,1,5,128]{7,0,6,5,4,3,2,1:T(4,128)(2,1)}, u32[]{:S(2)}) copy-start(bf16[3,5,5,1,5,1,5,128]{7,0,6,5,4,3,2,1:T(4,128)(2,1)} %param.15) | copy-start | bytes 1440004
  18.6 10.4 %collective-permute-start.7 = (f32[16,512]{1,0:T(8,128)S(1)}, f32[16,512]{1,0:T(8,128)S(1)}, u32[]{:S(2)}, u32[]{:S(2)}) collective-permute-start(f32[16,512]{1,0:T(8,128)S(1)} %get-tuple-element.62), channel_id=1, source_target_pairs={{1,2},{2,1},{3,4},{4,3},{5,6},{6,5},{7,8},{8,7},{9,10},{10,9},{11,... | collective-permute-start | bytes 98312 | tf_op jit(solution)/shard_map/ppermute | solution.py:784
  18.7 10.3 %collective-permute-start.4 = (f32[8,512]{1,0:T(8,128)S(1)}, f32[8,512]{1,0:T(8,128)S(1)}, u32[]{:S(2)}, u32[]{:S(2)}) collective-permute-start(f32[8,512]{1,0:T(8,128)S(1)} %get-tuple-element.59), channel_id=1, source_target_pairs={{0,32},{32,0},{64,96},{96,64},{128,160},{160,128},{192,224},{224,1... | collective-permute-start | bytes 49160 | tf_op jit(solution)/shard_map/ppermute | solution.py:784
  18.8 10.2 %collective-permute-start.5 = (f32[8,512]{1,0:T(8,128)S(1)}, f32[8,512]{1,0:T(8,128)S(1)}, u32[]{:S(2)}, u32[]{:S(2)}) collective-permute-start(f32[8,512]{1,0:T(8,128)S(1)} %get-tuple-element.60), channel_id=1, source_target_pairs={{32,64},{64,32},{96,128},{128,96},{160,192},{192,160},{224,0},{0,2... | collective-permute-start | bytes 49160 | tf_op jit(solution)/shard_map/ppermute | solution.py:784
  21.5 7.4 %collective-permute-start.6 = (f32[8,512]{1,0:T(8,128)S(1)}, f32[8,512]{1,0:T(8,128)S(1)}, u32[]{:S(2)}, u32[]{:S(2)}) collective-permute-start(f32[8,512]{1,0:T(8,128)S(1)} %get-tuple-element.61), channel_id=1, source_target_pairs={{0,1},{1,0},{2,3},{3,2},{4,5},{5,4},{6,7},{7,6},{8,9},{9,8},{10,11... | collective-permute-start | bytes 49160 | tf_op jit(solution)/shard_map/ppermute | solution.py:784
  28.9 36.8 %copy-start.1 = (f32[3,4,4,512]{3,2,1,0:T(4,128)S(1)}, f32[3,4,4,512]{3,2,1,0:T(4,128)}, u32[]{:S(2)}) copy-start(f32[3,4,4,512]{3,2,1,0:T(4,128)} %vel.1) | copy-start | bytes 294916
  28.9 36.8 %copy-start.2 = (f32[3,4,4,512]{3,2,1,0:T(4,128)S(1)}, f32[3,4,4,512]{3,2,1,0:T(4,128)}, u32[]{:S(2)}) copy-start(f32[3,4,4,512]{3,2,1,0:T(4,128)} %acc.1) | copy-start | bytes 294916
  29.2 6.0 %collective-permute-start.11 = (f32[32,512]{1,0:T(8,128)S(1)}, f32[32,512]{1,0:T(8,128)S(1)}, u32[]{:S(2)}, u32[]{:S(2)}) collective-permute-start(f32[32,512]{1,0:T(8,128)S(1)} %get-tuple-element.72), channel_id=1, source_target_pairs={{1,2},{2,1},{3,4},{4,3},{5,6},{6,5},{7,8},{8,7},{9,10},{10,9},{11,... | collective-permute-start | bytes 196616 | tf_op jit(solution)/shard_map/ppermute | solution.py:784
  29.3 5.9 %collective-permute-start.10 = (f32[24,512]{1,0:T(8,128)S(1)}, f32[24,512]{1,0:T(8,128)S(1)}, u32[]{:S(2)}, u32[]{:S(2)}) collective-permute-start(f32[24,512]{1,0:T(8,128)S(1)} %get-tuple-element.71), channel_id=1, source_target_pairs={{0,1},{1,0},{2,3},{3,2},{4,5},{5,4},{6,7},{7,6},{8,9},{9,8},{10,11... | collective-permute-start | bytes 147464 | tf_op jit(solution)/shard_map/ppermute | solution.py:784
  31.1 4.0 %collective-permute-start.8 = (f32[8,512]{1,0:T(8,128)S(1)}, f32[8,512]{1,0:T(8,128)S(1)}, u32[]{:S(2)}, u32[]{:S(2)}) collective-permute-start(f32[8,512]{1,0:T(8,128)S(1)} %get-tuple-element.69), channel_id=1, source_target_pairs={{0,32},{32,0},{64,96},{96,64},{128,160},{160,128},{192,224},{224,1... | collective-permute-start | bytes 49160 | tf_op jit(solution)/shard_map/ppermute | solution.py:784
  31.1 4.1 %collective-permute-start.9 = (f32[8,512]{1,0:T(8,128)S(1)}, f32[8,512]{1,0:T(8,128)S(1)}, u32[]{:S(2)}, u32[]{:S(2)}) collective-permute-start(f32[8,512]{1,0:T(8,128)S(1)} %get-tuple-element.70), channel_id=1, source_target_pairs={{32,64},{64,32},{96,128},{128,96},{160,192},{192,160},{224,0},{0,2... | collective-permute-start | bytes 49160 | tf_op jit(solution)/shard_map/ppermute | solution.py:784
  35.5 7.8 %collective-permute-start.15 = (f32[32,512]{1,0:T(8,128)S(1)}, f32[32,512]{1,0:T(8,128)S(1)}, u32[]{:S(2)}, u32[]{:S(2)}) collective-permute-start(f32[32,512]{1,0:T(8,128)S(1)} %get-tuple-element.80), channel_id=1, source_target_pairs={{1,2},{2,1},{3,4},{4,3},{5,6},{6,5},{7,8},{8,7},{9,10},{10,9},{11,... | collective-permute-start | bytes 196616 | tf_op jit(solution)/shard_map/ppermute | solution.py:784
  36.5 6.8 %collective-permute-start.12 = (f32[24,512]{1,0:T(8,128)S(1)}, f32[24,512]{1,0:T(8,128)S(1)}, u32[]{:S(2)}, u32[]{:S(2)}) collective-permute-start(f32[24,512]{1,0:T(8,128)S(1)} %get-tuple-element.77), channel_id=1, source_target_pairs={{0,32},{32,0},{64,96},{96,64},{128,160},{160,128},{192,224},{224,1... | collective-permute-start | bytes 147464 | tf_op jit(solution)/shard_map/ppermute | solution.py:784
  36.9 6.4 %collective-permute-start.13 = (f32[24,512]{1,0:T(8,128)S(1)}, f32[24,512]{1,0:T(8,128)S(1)}, u32[]{:S(2)}, u32[]{:S(2)}) collective-permute-start(f32[24,512]{1,0:T(8,128)S(1)} %get-tuple-element.78), channel_id=1, source_target_pairs={{32,64},{64,32},{96,128},{128,96},{160,192},{192,160},{224,0},{0,2... | collective-permute-start | bytes 147464 | tf_op jit(solution)/shard_map/ppermute | solution.py:784
  39.1 4.2 %collective-permute-start.14 = (f32[8,512]{1,0:T(8,128)S(1)}, f32[8,512]{1,0:T(8,128)S(1)}, u32[]{:S(2)}, u32[]{:S(2)}) collective-permute-start(f32[8,512]{1,0:T(8,128)S(1)} %get-tuple-element.79), channel_id=1, source_target_pairs={{0,1},{1,0},{2,3},{3,2},{4,5},{5,4},{6,7},{7,6},{8,9},{9,8},{10,11... | collective-permute-start | bytes 49160 | tf_op jit(solution)/shard_map/ppermute | solution.py:784

commit v4 on v3

--- a/solution.py
+++ b/solution.py
@@ -173,7 +173,7 @@
 
 def start_kernel(
     disp_h, vel_h, acc_h, phi_h, mat_h, flag_h, dens_h,
-    disp_new, disp_out, phi_out, info_out, lon0, lon1,
+    disp_out, phi_out, info_out, lon0, lon1,
     disp, vel, acc, mat, flag, dens, sems,
 ):
     moves = [
@@ -208,7 +208,6 @@
                 + TIME_STEP * vel[comp, i]
                 + 0.5 * TIME_STEP * TIME_STEP * acc[comp, i]
             )
-            disp_new[comp, i] = value
             disp_out[comp, i] = value
             planes.append(value)
         u.append(planes)
@@ -250,9 +249,47 @@
     return own, back
 
 
+def radial_tools():
+    lane = lanes((4, 512))
+    node = lane & 3
+    joint = jnp.logical_and(node == 0, lane >= 4)
+    weight = by_index(node, W[:4])
+
+    def earlier(factor):
+        return jnp.where(joint, pltpu.roll(factor, 4, 1), 0.0)
+
+    def weighted(factor):
+        return weight * factor + W[4] * earlier(factor)
+
+    return node, weight, earlier, weighted
+
+
+def density_kernel(coef, disp, _, rho_coef, disp_new, flag):
+    _, _, earlier, weighted = radial_tools()
+    rho, inverse = coef[28:32, :], coef[32:36, :]
+    r_points = 0.25 * weighted(rho)
+    r_own, r_back = lat_rows(r_points)
+    r_col, r_col_back = lon_cols(r_points)
+    scaled = 0.25 * rho * inverse
+    g_own, g_back = lat_rows(scaled)
+    h_own, h_back = lat_rows(earlier(scaled))
+    rho_coef[0:4, :] = r_own
+    rho_coef[4:8, :] = r_back
+    rho_coef[8:12, :] = g_own + g_back
+    rho_coef[12:16, :] = g_own
+    rho_coef[16:20, :] = h_own + h_back
+    rho_coef[20:24, :] = h_own
+    rho_coef[24:25, :] = r_col[0]
+    rho_coef[25:26, :] = r_col[1]
+    rho_coef[26:27, :] = r_col_back[0]
+    rho_coef[27:28, :] = r_col_back[1]
+    flag[...] = jnp.zeros((8, 128), F32)
+    disp_new[...] = disp[...]
+
+
 def residual_kernel(
     disp_new, phi, own_info, lat_first, lat_second, lon_first, lon_second, _,
-    coef, rho_coef, precond_out, w0_out, lat0, lat1, lon0, lon1,
+    coef, precond_out, w0_out, lat0, lat1, lon0, lon1,
 ):
     following, before = has_next(), has_before()
     lat_below, lat_above = arrived("lat", lat_first, lat_second)
@@ -286,17 +323,7 @@
     stretch = jnp.where(valid, jnp.where(flagged, 3.0, 1.0), 0.0)
     inverse = jnp.where(valid, jnp.where(flagged, 1.0 / 3.0, 1.0), 0.0)
     rho_in = jnp.where(flagged, 0.0, rho)
-    lane = lanes((4, 512))
-    node = lane & 3
-    joint = jnp.logical_and(node == 0, lane >= 4)
-    weight = by_index(node, W[:4])
-
-    def earlier(factor):
-        return jnp.where(joint, pltpu.roll(factor, 4, 1), 0.0)
-
-    def weighted(factor):
-        return weight * factor + W[4] * earlier(factor)
-
+    node, weight, earlier, weighted = radial_tools()
     s_points = 0.5 * weighted(stretch)
     s_own, s_back = lat_rows(s_points)
     s_col, s_col_back = lon_cols(s_points)
@@ -313,22 +340,8 @@
     coef[25:26, :] = s_col[1]
     coef[26:27, :] = s_col_back[0]
     coef[27:28, :] = s_col_back[1]
-    r_points = 0.25 * weighted(rho)
-    r_own, r_back = lat_rows(r_points)
-    r_col, r_col_back = lon_cols(r_points)
-    scaled = 0.25 * rho * inverse
-    g_own, g_back = lat_rows(scaled)
-    h_own, h_back = lat_rows(earlier(scaled))
-    rho_coef[0:4, :] = r_own
-    rho_coef[4:8, :] = r_back
-    rho_coef[8:12, :] = g_own + g_back
-    rho_coef[12:16, :] = g_own
-    rho_coef[16:20, :] = h_own + h_back
-    rho_coef[20:24, :] = h_own
-    rho_coef[24:25, :] = r_col[0]
-    rho_coef[25:26, :] = r_col[1]
-    rho_coef[26:27, :] = r_col_back[0]
-    rho_coef[27:28, :] = r_col_back[1]
+    coef[28:32, :] = rho
+    coef[32:36, :] = inverse
     q_points = 0.25 * weighted(rho_in)
     q_own, q_back = lat_rows(q_points)
     q_col, q_col_back = lon_cols(q_points)
@@ -427,7 +440,9 @@
     messages(result, (lat0, lat1), (lon0, lon1), edges)
 
 
-def moment_kernel(w0, w1, w2, coef, precond, lat_first, lat_second, lon_first, lon_second, out):
+def moment_kernel(
+    w0, w1, w2, coef, precond, lat_first, lat_second, lon_first, lon_second, _, out
+):
     fields = [w2[i] for i in range(4)]
     image = poisson(fields, coef, lat_first, lat_second, lon_first, lon_second)
     sums = [None] * 6
@@ -799,11 +814,11 @@
 ):
     field = ((4, 4, 512), F32)
     vector = ((3, 4, 4, 512), F32)
-    r8, r16, r24, r32 = (((n, 512), F32) for n in (8, 16, 24, 32))
+    r8, r16, r24, r32, r40 = (((n, 512), F32) for n in (8, 16, 24, 32, 40))
     info = ((8, 128), F32)
     kept = pltpu.with_memory_space_constraint
-    disp_new, disp, phi, own_info, *sent = call(
-        start_kernel, "start", [vector, vector, field, info, r16, r24], [HBM] * 7,
+    disp, phi, own_info, *sent = call(
+        start_kernel, "start", [vector, field, info, r16, r24], [HBM] * 7,
         [
             kept(array, pltpu.HBM)
             for array in (
@@ -850,8 +865,8 @@
         unpack_kernel, "unpack", [every, info], [VMEM] * 3, (memory, tables[1], lat_a[0]),
         [pltpu.VMEM((160, 128), F32)],
     )
-    coef, rho_coef, precond, w0, *sent = call(
-        residual_kernel, "residual", [r32, r32, field, field, r8, r8, r8, r16], [VMEM] * 8,
+    coef, precond, w0, *sent = call(
+        residual_kernel, "residual", [r40, field, field, r8, r8, r8, r16], [VMEM] * 8,
         (disp, phi, own_info, *halo_a, unpacked),
     )
     lon_b = swap_lon(*sent[2:])
@@ -884,9 +899,12 @@
     )
     lon_d = swap_lon(*sent[2:])
     halo_d = (*swap_lat(*sent[:2]), *lon_d)
+    rho_coef, disp_new, dense_done = call(
+        density_kernel, "density", [r32, vector, info], [VMEM] * 3, (coef, disp, sent[0])
+    )
     (line,) = call(
-        moment_kernel, "moments", [((LAT * LON, 128), F32)], [VMEM] * 9,
-        (w0, w1, w2, coef, precond, *halo_d),
+        moment_kernel, "moments", [((LAT * LON, 128), F32)], [VMEM] * 10,
+        (w0, w1, w2, coef, precond, *halo_d, dense_done),
     )
     moments = lax.all_to_all(line, AXES, 0, 0, tiled=True)
     phi_new, acc_new, vel_new = call(

time: 67.1 us -> 66.5 us (level)
    pallas_call x11 -> x12, Pallas kernels: 9.2 us -> 9.26 us  [call(): pl.pallas_call(kernel, name=name, out_shape=[jax.ShapeDtypeStruct(s, d) f...]
  transfers between devices with their start and end apart: 16 -> 16, of which waited for: 3 -> 3; matrix products, arithmetic and copies ran while one was open for 0% -> 0% of each run, Pallas kernels for 7% -> 8%
where the time goes in v4:
time: 66.5 us; the launch traced here: 66.2 us
  starting transfers between devices  32.6 us (49%)
  blocking collectives  22 us (33%)
  Pallas kernels  9.26 us (14%)
  local copies, waits for them, and re-layouts  1.09 us (2%)
  between operations  0.81 us (1%)
    ppermute x16, starting transfers between devices, swap(): return lax.ppermute(array, axis, pairs)  32.6 us
    all_to_all x1, blocking collectives, per_device(): moments = lax.all_to_all(line, AXES, 0, 0, tiled=True)  22 us
    pallas_call x12, Pallas kernels, call(): pl.pallas_call(kernel, name=name, out_shape=[jax.ShapeDtypeStruct(s, d) f...  9.26 us
  transfers between devices with their start and end apart: 16, of which 3 were waited for; matrix products, arithmetic and copies ran while one was open for 0% of the time, Pallas kernels for 8%

profile of v4, /device:TPU:1, one launch (start us, length us, event | category | flops | bytes accessed | tf_op | source)
XLA Modules:
  0.0 66.2 jit_solution(4947713204843775439)
XLA Ops:
  0.6 1.2 %start.1 = (f32[3,4,4,512]{3,2,1,0:T(4,128)S(1)}, f32[4,4,512]{2,1,0:T(4,128)S(1)}, f32[8,128]{1,0:T(8,128)S(1)}, f32[16,512]{1,0:T(8,128)S(1)}, f32[24,512]{1,0:T(8,128)S(1)}) custom-call(f32[3,4,4,512]{3,2,1,0:T(4,128)} %disp_h.1, f32[3,4,4,512]{3,2,1,0:T(4,128)} %vel.1, f32[3,4,4,512]{3,2,1,0:T(4,128)} %acc.1, f32[4,4,512]{2,1,0:T(4,128)} %phi_h.1, ...), custom_call_target="tpu_custom_call" | custom-call | flops 1000000 | bytes 500000 | tf_op jit(solution)/shard_map/start/pallas_call | solution.py:782
  1.8 2.8 %collective-permute-start.1 = (f32[24,512]{1,0:T(8,128)S(1)}, f32[24,512]{1,0:T(8,128)S(1)}, u32[]{:S(2)}, u32[]{:S(2)}) collective-permute-start(f32[24,512]{1,0:T(8,128)S(1)} %get-tuple-element.51), channel_id=1, source_target_pairs={{1,2},{2,1},{3,4},{4,3},{5,6},{6,5},{7,8},{8,7},{9,10},{10,9},{11,... | collective-permute-start | bytes 147464 | tf_op jit(solution)/shard_map/ppermute | solution.py:799
  4.6 3.5 %collective-permute-start = (f32[16,512]{1,0:T(8,128)S(1)}, f32[16,512]{1,0:T(8,128)S(1)}, u32[]{:S(2)}, u32[]{:S(2)}) collective-permute-start(f32[16,512]{1,0:T(8,128)S(1)} %get-tuple-element.50), channel_id=1, source_target_pairs={{0,1},{1,0},{2,3},{3,2},{4,5},{5,4},{6,7},{7,6},{8,9},{9,8},{10,11... | collective-permute-start | bytes 98312 | tf_op jit(solution)/shard_map/ppermute | solution.py:799
  8.1 1.3 %prepare.1 = (f32[40,128]{1,0:T(8,128)S(1)}, f32[8,128]{1,0:T(8,128)S(1)}, bf16[512,512]{1,0:T(8,128)(2,1)S(1)}, f32[5,96,128]{2,1,0:T(8,128)S(1)}) custom-call(f32[3,4,4,512]{3,2,1,0:T(4,128)S(1)} %get-tuple-element.47.disp.disp_new, s32[1,1,128]{2,1,0:T(1,128)} %mat_h.3, f32[6,8,6]{2,1,0:T(8,128)} %bitcast.16, f32[3]{0:T(128)} %decay_h.1, f32[3]{0:T(128)} %strength_h.1), custom_call_target="tpu_custom_call" | custom-call | flops 1000000 | bytes 500000 | tf_op jit(solution)/shard_map/prepare/pallas_call | solution.py:782
  9.5 1.7 %collective-permute-start.2 = (f32[24,512]{1,0:T(8,128)S(1)}, f32[24,512]{1,0:T(8,128)S(1)}, u32[]{:S(2)}, u32[]{:S(2)}) collective-permute-start(f32[24,512]{1,0:T(8,128)S(1)} %get-tuple-element.53._), channel_id=1, source_target_pairs={{0,32},{32,0},{64,96},{96,64},{128,160},{160,128},{192,224},{224,1... | collective-permute-start | bytes 147464 | tf_op jit(solution)/shard_map/ppermute | solution.py:799
  11.2 4.7 %collective-permute-start.3 = (f32[24,512]{1,0:T(8,128)S(1)}, f32[24,512]{1,0:T(8,128)S(1)}, u32[]{:S(2)}, u32[]{:S(2)}) collective-permute-start(f32[24,512]{1,0:T(8,128)S(1)} %get-tuple-element.54), channel_id=1, source_target_pairs={{32,64},{64,32},{96,128},{128,96},{160,192},{192,160},{224,0},{0,2... | collective-permute-start | bytes 147464 | tf_op jit(solution)/shard_map/ppermute | solution.py:799
  15.9 1.1 %copy-done = bf16[3,5,5,1,5,1,5,128]{7,0,6,5,4,3,2,1:T(4,128)(2,1)S(1)} copy-done((bf16[3,5,5,1,5,1,5,128]{7,0,6,5,4,3,2,1:T(4,128)(2,1)S(1)}, bf16[3,5,5,1,5,1,5,128]{7,0,6,5,4,3,2,1:T(4,128)(2,1)}, u32[]{:S(2)}) %copy-start) | copy-done | bytes 480024
  17.4 0.6 residual.1
  18.2 2.8 %collective-permute-start.5 = (f32[8,512]{1,0:T(8,128)S(1)}, f32[8,512]{1,0:T(8,128)S(1)}, u32[]{:S(2)}, u32[]{:S(2)}) collective-permute-start(f32[8,512]{1,0:T(8,128)S(1)} %get-tuple-element.60), channel_id=1, source_target_pairs={{32,64},{64,32},{96,128},{128,96},{160,192},{192,160},{224,0},{0,2... | collective-permute-start | bytes 49160 | tf_op jit(solution)/shard_map/ppermute | solution.py:799
  20.9 5.5 %collective-permute-start.6 = (f32[8,512]{1,0:T(8,128)S(1)}, f32[8,512]{1,0:T(8,128)S(1)}, u32[]{:S(2)}, u32[]{:S(2)}) collective-permute-start(f32[8,512]{1,0:T(8,128)S(1)} %get-tuple-element.61), channel_id=1, source_target_pairs={{0,1},{1,0},{2,3},{3,2},{4,5},{5,4},{6,7},{7,6},{8,9},{9,8},{10,11... | collective-permute-start | bytes 49160 | tf_op jit(solution)/shard_map/ppermute | solution.py:799
  26.5 1.8 %elastic.1 = (f32[375,8,128]{2,1,0:T(8,128)S(1)}, f32[3,4,4,512]{3,2,1,0:T(4,128)S(1)}, f32[16,512]{1,0:T(8,128)S(1)}, f32[16,512]{1,0:T(8,128)S(1)}) custom-call(f32[24,512]{1,0:T(8,128)S(1)} %collective-permute-done.2.lat_first.a0, f32[24,512]{1,0:T(8,128)S(1)} %collective-permute-done.3.lat_second.a1, f32[16,512]{1,0:T(8,128)S(1)} %collective-permute-done.lon_first.a2, ...), custom_call_target="tpu_custom_call" | custom-call | flops 20000000 | bytes 2000000 | tf_op jit(solution)/shard_map/elastic/pallas_call | solution.py:782
  28.3 0.3 second.1
  28.7 1.8 %collective-permute-start.10 = (f32[24,512]{1,0:T(8,128)S(1)}, f32[24,512]{1,0:T(8,128)S(1)}, u32[]{:S(2)}, u32[]{:S(2)}) collective-permute-start(f32[24,512]{1,0:T(8,128)S(1)} %get-tuple-element.71), channel_id=1, source_target_pairs={{0,1},{1,0},{2,3},{3,2},{4,5},{5,4},{6,7},{7,6},{8,9},{9,8},{10,11... | collective-permute-start | bytes 147464 | tf_op jit(solution)/shard_map/ppermute | solution.py:799
  30.5 2.7 %collective-permute-start.9 = (f32[8,512]{1,0:T(8,128)S(1)}, f32[8,512]{1,0:T(8,128)S(1)}, u32[]{:S(2)}, u32[]{:S(2)}) collective-permute-start(f32[8,512]{1,0:T(8,128)S(1)} %get-tuple-element.70), channel_id=1, source_target_pairs={{32,64},{64,32},{96,128},{128,96},{160,192},{192,160},{224,0},{0,2... | collective-permute-start | bytes 49160 | tf_op jit(solution)/shard_map/ppermute | solution.py:799
  33.2 1.3 %repack.1 = (bf16[5,5,5,5,3,128]{5,4,3,2,1,0:T(4,128)(2,1)}, f32[8,128]{1,0:T(8,128)S(1)}) custom-call(f32[375,8,128]{2,1,0:T(8,128)S(1)} %get-tuple-element.74.dense), custom_call_target="tpu_custom_call" | custom-call | flops 1000000 | bytes 500000 | tf_op jit(solution)/shard_map/repack/pallas_call | solution.py:782
  34.6 0.3 third.1
  34.9 1.0 %collective-permute-start.15 = (f32[32,512]{1,0:T(8,128)S(1)}, f32[32,512]{1,0:T(8,128)S(1)}, u32[]{:S(2)}, u32[]{:S(2)}) collective-permute-start(f32[32,512]{1,0:T(8,128)S(1)} %get-tuple-element.81), channel_id=1, source_target_pairs={{1,2},{2,1},{3,4},{4,3},{5,6},{6,5},{7,8},{8,7},{9,10},{10,9},{11,... | collective-permute-start | bytes 196616 | tf_op jit(solution)/shard_map/ppermute | solution.py:799
  35.9 0.5 collective-permute-start.12
  36.3 2.2 %collective-permute-start.13 = (f32[24,512]{1,0:T(8,128)S(1)}, f32[24,512]{1,0:T(8,128)S(1)}, u32[]{:S(2)}, u32[]{:S(2)}) collective-permute-start(f32[24,512]{1,0:T(8,128)S(1)} %get-tuple-element.79), channel_id=1, source_target_pairs={{32,64},{64,32},{96,128},{128,96},{160,192},{192,160},{224,0},{0,2... | collective-permute-start | bytes 147464 | tf_op jit(solution)/shard_map/ppermute | solution.py:799
  38.5 3.3 %collective-permute-start.14 = (f32[8,512]{1,0:T(8,128)S(1)}, f32[8,512]{1,0:T(8,128)S(1)}, u32[]{:S(2)}, u32[]{:S(2)}) collective-permute-start(f32[8,512]{1,0:T(8,128)S(1)} %get-tuple-element.80), channel_id=1, source_target_pairs={{0,1},{1,0},{2,3},{3,2},{4,5},{5,4},{6,7},{7,6},{8,9},{9,8},{10,11... | collective-permute-start | bytes 49160 | tf_op jit(solution)/shard_map/ppermute | solution.py:799
  41.9 0.7 density.1
  42.7 0.4 moments.1
  43.1 22.0 %all_to_all.11 = f32[256,1,128]{2,1,0:T(1,128)S(1)} all-to-all(f32[256,1,128]{2,1,0:T(1,128)S(1)} %bitcast.15), channel_id=1, replica_groups=mesh['lat'=8,'lon'=32] {'lat','lon'}, dimensions={0} | all-to-all | bytes 262144 | tf_op jit(solution)/shard_map/all_to_all | solution.py:909
  65.1 1.1 %final.1 = (f32[4,4,512]{2,1,0:T(4,128)}, f32[3,4,4,512]{3,2,1,0:T(4,128)}, f32[3,4,4,512]{3,2,1,0:T(4,128)}) custom-call(f32[256,128]{1,0:T(8,128)S(1)} %bitcast.14, f32[4,4,512]{2,1,0:T(4,128)S(1)} %get-tuple-element.48.phi, f32[4,4,512]{2,1,0:T(4,128)S(1)} %get-tuple-element.57.field.w0, f32[4,4,512]{2,1,0:T(4,128)S(1)} %get-tuple-element.68.field.w1, ...), custom_call_target="tpu_custom_call" | custom-call | flops 1000000 | bytes 500000 | tf_op jit(solution)/shard_map/final/pallas_call | solution.py:782
  (27 shorter events, 1.0 us)
Async XLA Ops:
  1.8 7.6 %collective-permute-start.1 = (f32[24,512]{1,0:T(8,128)S(1)}, f32[24,512]{1,0:T(8,128)S(1)}, u32[]{:S(2)}, u32[]{:S(2)}) collective-permute-start(f32[24,512]{1,0:T(8,128)S(1)} %get-tuple-element.51), channel_id=1, source_target_pairs={{1,2},{2,1},{3,4},{4,3},{5,6},{6,5},{7,8},{8,7},{9,10},{10,9},{11,... | collective-permute-start | bytes 147464 | tf_op jit(solution)/shard_map/ppermute | solution.py:799
  4.6 4.8 %collective-permute-start = (f32[16,512]{1,0:T(8,128)S(1)}, f32[16,512]{1,0:T(8,128)S(1)}, u32[]{:S(2)}, u32[]{:S(2)}) collective-permute-start(f32[16,512]{1,0:T(8,128)S(1)} %get-tuple-element.50), channel_id=1, source_target_pairs={{0,1},{1,0},{2,3},{3,2},{4,5},{5,4},{6,7},{7,6},{8,9},{9,8},{10,11... | collective-permute-start | bytes 98312 | tf_op jit(solution)/shard_map/ppermute | solution.py:799
  9.5 7.7 %collective-permute-start.2 = (f32[24,512]{1,0:T(8,128)S(1)}, f32[24,512]{1,0:T(8,128)S(1)}, u32[]{:S(2)}, u32[]{:S(2)}) collective-permute-start(f32[24,512]{1,0:T(8,128)S(1)} %get-tuple-element.53._), channel_id=1, source_target_pairs={{0,32},{32,0},{64,96},{96,64},{128,160},{160,128},{192,224},{224,1... | collective-permute-start | bytes 147464 | tf_op jit(solution)/shard_map/ppermute | solution.py:799
  11.2 6.1 %collective-permute-start.3 = (f32[24,512]{1,0:T(8,128)S(1)}, f32[24,512]{1,0:T(8,128)S(1)}, u32[]{:S(2)}, u32[]{:S(2)}) collective-permute-start(f32[24,512]{1,0:T(8,128)S(1)} %get-tuple-element.54), channel_id=1, source_target_pairs={{32,64},{64,32},{96,128},{128,96},{160,192},{192,160},{224,0},{0,2... | collective-permute-start | bytes 147464 | tf_op jit(solution)/shard_map/ppermute | solution.py:799
  15.9 1.1 %copy-start = (bf16[3,5,5,1,5,1,5,128]{7,0,6,5,4,3,2,1:T(4,128)(2,1)S(1)}, bf16[3,5,5,1,5,1,5,128]{7,0,6,5,4,3,2,1:T(4,128)(2,1)}, u32[]{:S(2)}) copy-start(bf16[3,5,5,1,5,1,5,128]{7,0,6,5,4,3,2,1:T(4,128)(2,1)} %param.15) | copy-start | bytes 1440004
  18.0 10.4 %collective-permute-start.7 = (f32[16,512]{1,0:T(8,128)S(1)}, f32[16,512]{1,0:T(8,128)S(1)}, u32[]{:S(2)}, u32[]{:S(2)}) collective-permute-start(f32[16,512]{1,0:T(8,128)S(1)} %get-tuple-element.62), channel_id=1, source_target_pairs={{1,2},{2,1},{3,4},{4,3},{5,6},{6,5},{7,8},{8,7},{9,10},{10,9},{11,... | collective-permute-start | bytes 98312 | tf_op jit(solution)/shard_map/ppermute | solution.py:799
  18.1 10.2 %collective-permute-start.4 = (f32[8,512]{1,0:T(8,128)S(1)}, f32[8,512]{1,0:T(8,128)S(1)}, u32[]{:S(2)}, u32[]{:S(2)}) collective-permute-start(f32[8,512]{1,0:T(8,128)S(1)} %get-tuple-element.59), channel_id=1, source_target_pairs={{0,32},{32,0},{64,96},{96,64},{128,160},{160,128},{192,224},{224,1... | collective-permute-start | bytes 49160 | tf_op jit(solution)/shard_map/ppermute | solution.py:799
  18.2 10.1 %collective-permute-start.5 = (f32[8,512]{1,0:T(8,128)S(1)}, f32[8,512]{1,0:T(8,128)S(1)}, u32[]{:S(2)}, u32[]{:S(2)}) collective-permute-start(f32[8,512]{1,0:T(8,128)S(1)} %get-tuple-element.60), channel_id=1, source_target_pairs={{32,64},{64,32},{96,128},{128,96},{160,192},{192,160},{224,0},{0,2... | collective-permute-start | bytes 49160 | tf_op jit(solution)/shard_map/ppermute | solution.py:799
  20.9 7.4 %collective-permute-start.6 = (f32[8,512]{1,0:T(8,128)S(1)}, f32[8,512]{1,0:T(8,128)S(1)}, u32[]{:S(2)}, u32[]{:S(2)}) collective-permute-start(f32[8,512]{1,0:T(8,128)S(1)} %get-tuple-element.61), channel_id=1, source_target_pairs={{0,1},{1,0},{2,3},{3,2},{4,5},{5,4},{6,7},{7,6},{8,9},{9,8},{10,11... | collective-permute-start | bytes 49160 | tf_op jit(solution)/shard_map/ppermute | solution.py:799
  28.3 36.8 %copy-start.1 = (f32[3,4,4,512]{3,2,1,0:T(4,128)S(1)}, f32[3,4,4,512]{3,2,1,0:T(4,128)}, u32[]{:S(2)}) copy-start(f32[3,4,4,512]{3,2,1,0:T(4,128)} %vel.1) | copy-start | bytes 294916
  28.3 36.7 %copy-start.2 = (f32[3,4,4,512]{3,2,1,0:T(4,128)S(1)}, f32[3,4,4,512]{3,2,1,0:T(4,128)}, u32[]{:S(2)}) copy-start(f32[3,4,4,512]{3,2,1,0:T(4,128)} %acc.1) | copy-start | bytes 294916
  28.6 6.0 %collective-permute-start.11 = (f32[32,512]{1,0:T(8,128)S(1)}, f32[32,512]{1,0:T(8,128)S(1)}, u32[]{:S(2)}, u32[]{:S(2)}) collective-permute-start(f32[32,512]{1,0:T(8,128)S(1)} %get-tuple-element.72), channel_id=1, source_target_pairs={{1,2},{2,1},{3,4},{4,3},{5,6},{6,5},{7,8},{8,7},{9,10},{10,9},{11,... | collective-permute-start | bytes 196616 | tf_op jit(solution)/shard_map/ppermute | solution.py:799
  28.7 5.9 %collective-permute-start.10 = (f32[24,512]{1,0:T(8,128)S(1)}, f32[24,512]{1,0:T(8,128)S(1)}, u32[]{:S(2)}, u32[]{:S(2)}) collective-permute-start(f32[24,512]{1,0:T(8,128)S(1)} %get-tuple-element.71), channel_id=1, source_target_pairs={{0,1},{1,0},{2,3},{3,2},{4,5},{5,4},{6,7},{7,6},{8,9},{9,8},{10,11... | collective-permute-start | bytes 147464 | tf_op jit(solution)/shard_map/ppermute | solution.py:799
  30.5 4.0 %collective-permute-start.8 = (f32[8,512]{1,0:T(8,128)S(1)}, f32[8,512]{1,0:T(8,128)S(1)}, u32[]{:S(2)}, u32[]{:S(2)}) collective-permute-start(f32[8,512]{1,0:T(8,128)S(1)} %get-tuple-element.69), channel_id=1, source_target_pairs={{0,32},{32,0},{64,96},{96,64},{128,160},{160,128},{192,224},{224,1... | collective-permute-start | bytes 49160 | tf_op jit(solution)/shard_map/ppermute | solution.py:799
  30.5 4.1 %collective-permute-start.9 = (f32[8,512]{1,0:T(8,128)S(1)}, f32[8,512]{1,0:T(8,128)S(1)}, u32[]{:S(2)}, u32[]{:S(2)}) collective-permute-start(f32[8,512]{1,0:T(8,128)S(1)} %get-tuple-element.70), channel_id=1, source_target_pairs={{32,64},{64,32},{96,128},{128,96},{160,192},{192,160},{224,0},{0,2... | collective-permute-start | bytes 49160 | tf_op jit(solution)/shard_map/ppermute | solution.py:799
  34.9 7.8 %collective-permute-start.15 = (f32[32,512]{1,0:T(8,128)S(1)}, f32[32,512]{1,0:T(8,128)S(1)}, u32[]{:S(2)}, u32[]{:S(2)}) collective-permute-start(f32[32,512]{1,0:T(8,128)S(1)} %get-tuple-element.81), channel_id=1, source_target_pairs={{1,2},{2,1},{3,4},{4,3},{5,6},{6,5},{7,8},{8,7},{9,10},{10,9},{11,... | collective-permute-start | bytes 196616 | tf_op jit(solution)/shard_map/ppermute | solution.py:799
  35.9 6.8 %collective-permute-start.12 = (f32[24,512]{1,0:T(8,128)S(1)}, f32[24,512]{1,0:T(8,128)S(1)}, u32[]{:S(2)}, u32[]{:S(2)}) collective-permute-start(f32[24,512]{1,0:T(8,128)S(1)} %get-tuple-element.76._), channel_id=1, source_target_pairs={{0,32},{32,0},{64,96},{96,64},{128,160},{160,128},{192,224},{224,1... | collective-permute-start | bytes 147464 | tf_op jit(solution)/shard_map/ppermute | solution.py:799
  36.3 6.4 %collective-permute-start.13 = (f32[24,512]{1,0:T(8,128)S(1)}, f32[24,512]{1,0:T(8,128)S(1)}, u32[]{:S(2)}, u32[]{:S(2)}) collective-permute-start(f32[24,512]{1,0:T(8,128)S(1)} %get-tuple-element.79), channel_id=1, source_target_pairs={{32,64},{64,32},{96,128},{128,96},{160,192},{192,160},{224,0},{0,2... | collective-permute-start | bytes 147464 | tf_op jit(solution)/shard_map/ppermute | solution.py:799
  38.5 4.2 %collective-permute-start.14 = (f32[8,512]{1,0:T(8,128)S(1)}, f32[8,512]{1,0:T(8,128)S(1)}, u32[]{:S(2)}, u32[]{:S(2)}) collective-permute-start(f32[8,512]{1,0:T(8,128)S(1)} %get-tuple-element.80), channel_id=1, source_target_pairs={{0,1},{1,0},{2,3},{3,2},{4,5},{5,4},{6,7},{7,6},{8,9},{9,8},{10,11... | collective-permute-start | bytes 49160 | tf_op jit(solution)/shard_map/ppermute | solution.py:799

commit v5 on v4

--- a/solution.py
+++ b/solution.py
@@ -216,9 +216,9 @@
     up += [partial_lon(potential[i], M_GRAVITY) for i in range(4)]
     down = [u[comp][i][0:1] for comp in range(3) for i in range(4)]
     down += [potential[i][0:1] for i in range(4)]
-    post("lon", (lon0, lon1), stack(up + [info], 24), stack(down, 24))
-
-def pack_kernel(disp, phi, own_info, lon_first, lon_second, _, lat0, lat1):
+    post("lon", (lon0, lon1), stack(up + [info], 16), stack(down, 16))
+
+def pack_kernel(lon_second, lon_first, disp, phi, own_info, _, lat0, lat1):
     below, above = arrived("lon", lon_first, lon_second)
     potential = [phi[i] for i in range(4)]
     info = jnp.concatenate(
@@ -288,7 +288,7 @@
 
 
 def residual_kernel(
-    disp_new, phi, own_info, lat_first, lat_second, lon_first, lon_second, _,
+    disp_new, phi, own_info, lon_second, lat_first, lat_second, lon_first, _,
     coef, precond_out, w0_out, lat0, lat1, lon0, lon1,
 ):
     following, before = has_next(), has_before()
@@ -389,7 +389,7 @@
     messages(w0, (lat0, lat1), (lon0, lon1))
 
 
-def poisson(fields, coef, lat_first, lat_second, lon_first, lon_second):
+def poisson(fields, coef, lon_second, lat_first, lat_second, lon_first):
     following = has_next()
     lat_below, lat_above = arrived("lat", lat_first, lat_second)
     lon_below, lon_above = arrived("lon", lon_first, lon_second)
@@ -417,18 +417,18 @@
 
 
 def second_kernel(
-    field, coef, precond, lat_first, lat_second, lon_first, lon_second, lon_force,
+    field, coef, precond, lon_second, lat_first, lat_second, lon_first, lon_force,
     out, lat0, lat1, lon0, lon1,
 ):
-    result = step(field, coef, precond, (lat_first, lat_second, lon_first, lon_second), out)
+    result = step(field, coef, precond, (lon_second, lat_first, lat_second, lon_first), out)
     messages(result, (lat0, lat1), (lon0, lon1), (), (lon_force[...],))
 
 
 def third_kernel(
-    field, coef, precond, lat_first, lat_second, lon_first, lon_second, lat_force, _,
+    field, coef, precond, lon_second, lat_first, lat_second, lon_first, lat_force, _,
     out, lat0, lat1, lon0, lon1,
 ):
-    result = step(field, coef, precond, (lat_first, lat_second, lon_first, lon_second), out)
+    result = step(field, coef, precond, (lon_second, lat_first, lat_second, lon_first), out)
     below, _ = arrived("lon", lon_first, lon_second)
     first = column([1.0, 0.0, 0.0, 0.0])
     edges = []
@@ -441,10 +441,10 @@
 
 
 def moment_kernel(
-    w0, w1, w2, coef, precond, lat_first, lat_second, lon_first, lon_second, _, out
+    w0, w1, w2, coef, precond, lon_second, lat_first, lat_second, lon_first, _, out
 ):
     fields = [w2[i] for i in range(4)]
-    image = poisson(fields, coef, lat_first, lat_second, lon_first, lon_second)
+    image = poisson(fields, coef, lon_second, lat_first, lat_second, lon_first)
     sums = [None] * 6
     for i in range(4):
         m = precond[i]
@@ -529,14 +529,14 @@
         phi_new[i] = value
         potential.append(value)
     following, before = has_next(), has_before()
-    ma, na = arrived("lat", a0, a1)
-    mb, nb = arrived("lat", b0, b1)
-    mc, nc = arrived("lat", c0, c1)
-    md, nd = arrived("lat", d0, d1)
-    fa, ga = arrived("lon", a2, a3)
-    fb, gb = arrived("lon", b2, b3)
-    fc, gc = arrived("lon", c2, c3)
-    fd, gd = arrived("lon", d2, d3)
+    ma, na = arrived("lat", a1, a2)
+    mb, nb = arrived("lat", b1, b2)
+    mc, nc = arrived("lat", c1, c2)
+    md, nd = arrived("lat", d1, d2)
+    fa, ga = arrived("lon", a3, a0)
+    fb, gb = arrived("lon", b3, b0)
+    fc, gc = arrived("lon", c3, c0)
+    fd, gd = arrived("lon", d3, d0)
     lat_below = combined(ma[8:12, :], mb[4:8, :], mc[4:8, :], md[4:8, :])
     lat_above = following * combined(na[12:16, :], nb[0:4, :], nc[0:4, :], nd[0:4, :])
     lon_below = combined(fa[8:12, :], fb[4:8, :], fc[4:8, :], fd[4:8, :])
@@ -655,7 +655,7 @@
 
 
 def elastic_kernel(
-    lat_first, lat_second, lon_first, lon_second, stiff, rates, perm, own, decayed,
+    lon_second, lat_first, lat_second, lon_first, stiff, rates, perm, own, decayed,
     dense, force, lat_force, lon_force,
     points, edge, elems, devs, flux,
 ):
@@ -818,7 +818,7 @@
     info = ((8, 128), F32)
     kept = pltpu.with_memory_space_constraint
     disp, phi, own_info, *sent = call(
-        start_kernel, "start", [vector, field, info, r16, r24], [HBM] * 7,
+        start_kernel, "start", [vector, field, info, r16, r16], [HBM] * 7,
         [
             kept(array, pltpu.HBM)
             for array in (
@@ -856,9 +856,9 @@
     )
     lat_a = call(
         pack_kernel, "pack", [r24, r24], [VMEM] * 6,
-        (disp, phi, own_info, *lon_a, tables[1]),
-    )
-    halo_a = (*swap_lat(*lat_a), *lon_a)
+        (lon_a[1], lon_a[0], disp, phi, own_info, tables[1]),
+    )
+    halo_a = (lon_a[1], *swap_lat(*lat_a), lon_a[0])
     memory = memory_vars.reshape(3, 5, 5, 5, 5, 128).transpose(1, 2, 3, 4, 0, 5)
     every = ((375, 8, 128), F32)
     decayed, unpacked = call(
@@ -866,11 +866,11 @@
         [pltpu.VMEM((160, 128), F32)],
     )
     coef, precond, w0, *sent = call(
-        residual_kernel, "residual", [r40, field, field, r8, r8, r8, r16], [VMEM] * 8,
+        residual_kernel, "residual", [r40, field, field, r8, r8, r8, r8], [VMEM] * 8,
         (disp, phi, own_info, *halo_a, unpacked),
     )
     lon_b = swap_lon(*sent[2:])
-    halo_b = (*swap_lat(*sent[:2]), *lon_b)
+    halo_b = (lon_b[1], *swap_lat(*sent[:2]), lon_b[0])
     dense, force, lat_force, lon_force = call(
         elastic_kernel, "elastic", [every, vector, r16, r16], [VMEM] * 9,
         (*halo_a, *tables, decayed),
@@ -884,11 +884,11 @@
         flops=20000000, moved=2000000,
     )
     w1, *sent = call(
-        second_kernel, "second", [field, r8, r8, r24, r32], [VMEM] * 8,
+        second_kernel, "second", [field, r8, r8, r24, r24], [VMEM] * 8,
         (w0, coef, precond, *halo_b, lon_force),
     )
     lon_c = swap_lon(*sent[2:])
-    halo_c = (*swap_lat(*sent[:2]), *lon_c)
+    halo_c = (lon_c[1], *swap_lat(*sent[:2]), lon_c[0])
     memory_new, packed = call(
         repack_kernel, "repack", [((5, 5, 5, 5, 3, 128), BF16), info], [VMEM], (dense,),
         [pltpu.VMEM((160, 128), F32)],
@@ -898,7 +898,7 @@
         (w1, coef, precond, *halo_c, lat_force, packed),
     )
     lon_d = swap_lon(*sent[2:])
-    halo_d = (*swap_lat(*sent[:2]), *lon_d)
+    halo_d = (lon_d[1], *swap_lat(*sent[:2]), lon_d[0])
     rho_coef, disp_new, dense_done = call(
         density_kernel, "density", [r32, vector, info], [VMEM] * 3, (coef, disp, sent[0])
     )

time: 66.5 us -> 65.9 us (level)
  starting transfers between devices: 32.6 us -> 30.6 us
  waiting for transfers between devices: 0.43 us -> 1.89 us
    ppermute x16, starting transfers between devices: 32.6 us -> 30.6 us  [swap(): return lax.ppermute(array, axis, pairs)]
    ppermute x16, waiting for transfers between devices: 0.43 us -> 1.89 us  [swap(): return lax.ppermute(array, axis, pairs)]
where the time goes in v5:
time: 65.9 us; the launch traced here: 65.6 us
  starting transfers between devices  30.6 us (46%)
  blocking collectives  22 us (33%)
  Pallas kernels  9.25 us (14%)
  waiting for transfers between devices  1.89 us (3%)
  local copies, waits for them, and re-layouts  1.09 us (2%)
  between operations  0.81 us (1%)
    ppermute x16, starting transfers between devices, swap(): return lax.ppermute(array, axis, pairs)  30.6 us
    all_to_all x1, blocking collectives, per_device(): moments = lax.all_to_all(line, AXES, 0, 0, tiled=True)  22 us
    pallas_call x12, Pallas kernels, call(): pl.pallas_call(kernel, name=name, out_shape=[jax.ShapeDtypeStruct(s, d) f...  9.25 us
    ppermute x16, waiting for transfers between devices, swap(): return lax.ppermute(array, axis, pairs)  1.89 us
  transfers between devices with their start and end apart: 16, of which 3 were waited for; matrix products, arithmetic and copies ran while one was open for 0% of the time, Pallas kernels for 8%

profile of v5, /device:TPU:1, one launch (start us, length us, event | category | flops | bytes accessed | tf_op | source)
XLA Modules:
  0.0 65.6 jit_solution(9664016845179960838)
XLA Ops:
  0.6 1.2 %start.1 = (f32[3,4,4,512]{3,2,1,0:T(4,128)S(1)}, f32[4,4,512]{2,1,0:T(4,128)S(1)}, f32[8,128]{1,0:T(8,128)S(1)}, f32[16,512]{1,0:T(8,128)S(1)}, f32[16,512]{1,0:T(8,128)S(1)}) custom-call(f32[3,4,4,512]{3,2,1,0:T(4,128)} %disp_h.1, f32[3,4,4,512]{3,2,1,0:T(4,128)} %vel.1, f32[3,4,4,512]{3,2,1,0:T(4,128)} %acc.1, f32[4,4,512]{2,1,0:T(4,128)} %phi_h.1, ...), custom_call_target="tpu_custom_call" | custom-call | flops 1000000 | bytes 500000 | tf_op jit(solution)/shard_map/start/pallas_call | solution.py:782
  1.8 2.8 %collective-permute-start = (f32[16,512]{1,0:T(8,128)S(1)}, f32[16,512]{1,0:T(8,128)S(1)}, u32[]{:S(2)}, u32[]{:S(2)}) collective-permute-start(f32[16,512]{1,0:T(8,128)S(1)} %get-tuple-element.50), channel_id=1, source_target_pairs={{1,2},{2,1},{3,4},{4,3},{5,6},{6,5},{7,8},{8,7},{9,10},{10,9},{11,... | collective-permute-start | bytes 98312 | tf_op jit(solution)/shard_map/ppermute | solution.py:799
  4.6 3.5 %collective-permute-start.1 = (f32[16,512]{1,0:T(8,128)S(1)}, f32[16,512]{1,0:T(8,128)S(1)}, u32[]{:S(2)}, u32[]{:S(2)}) collective-permute-start(f32[16,512]{1,0:T(8,128)S(1)} %get-tuple-element.51), channel_id=1, source_target_pairs={{0,1},{1,0},{2,3},{3,2},{4,5},{5,4},{6,7},{7,6},{8,9},{9,8},{10,11... | collective-permute-start | bytes 98312 | tf_op jit(solution)/shard_map/ppermute | solution.py:799
  8.1 1.3 %prepare.1 = (f32[40,128]{1,0:T(8,128)S(1)}, f32[8,128]{1,0:T(8,128)S(1)}, bf16[512,512]{1,0:T(8,128)(2,1)S(1)}, f32[5,96,128]{2,1,0:T(8,128)S(1)}) custom-call(f32[3,4,4,512]{3,2,1,0:T(4,128)S(1)} %get-tuple-element.47.disp.disp_new, s32[1,1,128]{2,1,0:T(1,128)} %mat_h.3, f32[6,8,6]{2,1,0:T(8,128)} %bitcast.16, f32[3]{0:T(128)} %decay_h.1, f32[3]{0:T(128)} %strength_h.1), custom_call_target="tpu_custom_call" | custom-call | flops 1000000 | bytes 500000 | tf_op jit(solution)/shard_map/prepare/pallas_call | solution.py:782
  9.5 1.7 %collective-permute-start.2 = (f32[24,512]{1,0:T(8,128)S(1)}, f32[24,512]{1,0:T(8,128)S(1)}, u32[]{:S(2)}, u32[]{:S(2)}) collective-permute-start(f32[24,512]{1,0:T(8,128)S(1)} %get-tuple-element.53._), channel_id=1, source_target_pairs={{0,32},{32,0},{64,96},{96,64},{128,160},{160,128},{192,224},{224,1... | collective-permute-start | bytes 147464 | tf_op jit(solution)/shard_map/ppermute | solution.py:799
  11.2 4.7 %collective-permute-start.3 = (f32[24,512]{1,0:T(8,128)S(1)}, f32[24,512]{1,0:T(8,128)S(1)}, u32[]{:S(2)}, u32[]{:S(2)}) collective-permute-start(f32[24,512]{1,0:T(8,128)S(1)} %get-tuple-element.54), channel_id=1, source_target_pairs={{32,64},{64,32},{96,128},{128,96},{160,192},{192,160},{224,0},{0,2... | collective-permute-start | bytes 147464 | tf_op jit(solution)/shard_map/ppermute | solution.py:799
  15.9 1.1 %copy-done = bf16[3,5,5,1,5,1,5,128]{7,0,6,5,4,3,2,1:T(4,128)(2,1)S(1)} copy-done((bf16[3,5,5,1,5,1,5,128]{7,0,6,5,4,3,2,1:T(4,128)(2,1)S(1)}, bf16[3,5,5,1,5,1,5,128]{7,0,6,5,4,3,2,1:T(4,128)(2,1)}, u32[]{:S(2)}) %copy-start) | copy-done | bytes 480024
  17.0 0.3 unpack.1
  17.4 0.6 residual.1
  18.2 2.8 %collective-permute-start.6 = (f32[8,512]{1,0:T(8,128)S(1)}, f32[8,512]{1,0:T(8,128)S(1)}, u32[]{:S(2)}, u32[]{:S(2)}) collective-permute-start(f32[8,512]{1,0:T(8,128)S(1)} %get-tuple-element.61), channel_id=1, source_target_pairs={{32,64},{64,32},{96,128},{128,96},{160,192},{192,160},{224,0},{0,2... | collective-permute-start | bytes 49160 | tf_op jit(solution)/shard_map/ppermute | solution.py:799
  20.9 5.4 %collective-permute-start.7 = (f32[8,512]{1,0:T(8,128)S(1)}, f32[8,512]{1,0:T(8,128)S(1)}, u32[]{:S(2)}, u32[]{:S(2)}) collective-permute-start(f32[8,512]{1,0:T(8,128)S(1)} %get-tuple-element.62), channel_id=1, source_target_pairs={{0,1},{1,0},{2,3},{3,2},{4,5},{5,4},{6,7},{7,6},{8,9},{9,8},{10,11... | collective-permute-start | bytes 49160 | tf_op jit(solution)/shard_map/ppermute | solution.py:799
  26.3 1.8 %elastic.1 = (f32[375,8,128]{2,1,0:T(8,128)S(1)}, f32[3,4,4,512]{3,2,1,0:T(4,128)S(1)}, f32[16,512]{1,0:T(8,128)S(1)}, f32[16,512]{1,0:T(8,128)S(1)}) custom-call(f32[16,512]{1,0:T(8,128)S(1)} %collective-permute-done.lon_second.a0, f32[24,512]{1,0:T(8,128)S(1)} %collective-permute-done.2.lat_first.a1, f32[24,512]{1,0:T(8,128)S(1)} %collective-permute-done.3.lat_second.a2, ...), custom_call_target="tpu_custom_call" | custom-call | flops 20000000 | bytes 2000000 | tf_op jit(solution)/shard_map/elastic/pallas_call | solution.py:782
  28.2 0.3 second.1
  28.7 2.7 %collective-permute-start.10 = (f32[8,512]{1,0:T(8,128)S(1)}, f32[8,512]{1,0:T(8,128)S(1)}, u32[]{:S(2)}, u32[]{:S(2)}) collective-permute-start(f32[8,512]{1,0:T(8,128)S(1)} %get-tuple-element.71), channel_id=1, source_target_pairs={{32,64},{64,32},{96,128},{128,96},{160,192},{192,160},{224,0},{0,2... | collective-permute-start | bytes 49160 | tf_op jit(solution)/shard_map/ppermute | solution.py:799
  31.3 1.3 %repack.1 = (bf16[5,5,5,5,3,128]{5,4,3,2,1,0:T(4,128)(2,1)}, f32[8,128]{1,0:T(8,128)S(1)}) custom-call(f32[375,8,128]{2,1,0:T(8,128)S(1)} %get-tuple-element.74.dense), custom_call_target="tpu_custom_call" | custom-call | flops 1000000 | bytes 500000 | tf_op jit(solution)/shard_map/repack/pallas_call | solution.py:782
  32.6 1.6 %collective-permute-done.9.lat_first.c1 = f32[8,512]{1,0:T(8,128)S(1)} collective-permute-done((f32[8,512]{1,0:T(8,128)S(1)}, f32[8,512]{1,0:T(8,128)S(1)}, u32[]{:S(2)}, u32[]{:S(2)}) %collective-permute-start.9) | collective-permute-done | bytes 16416 | tf_op jit(solution)/shard_map/ppermute | solution.py:799
  34.2 0.3 third.1
  34.5 3.0 %collective-permute-start.12 = (f32[32,512]{1,0:T(8,128)S(1)}, f32[32,512]{1,0:T(8,128)S(1)}, u32[]{:S(2)}, u32[]{:S(2)}) collective-permute-start(f32[32,512]{1,0:T(8,128)S(1)} %get-tuple-element.79), channel_id=1, source_target_pairs={{1,2},{2,1},{3,4},{4,3},{5,6},{6,5},{7,8},{8,7},{9,10},{10,9},{11,... | collective-permute-start | bytes 196616 | tf_op jit(solution)/shard_map/ppermute | solution.py:799
  37.5 1.3 %collective-permute-start.14 = (f32[24,512]{1,0:T(8,128)S(1)}, f32[24,512]{1,0:T(8,128)S(1)}, u32[]{:S(2)}, u32[]{:S(2)}) collective-permute-start(f32[24,512]{1,0:T(8,128)S(1)} %get-tuple-element.80), channel_id=1, source_target_pairs={{32,64},{64,32},{96,128},{128,96},{160,192},{192,160},{224,0},{0,2... | collective-permute-start | bytes 147464 | tf_op jit(solution)/shard_map/ppermute | solution.py:799
  38.8 2.5 %collective-permute-start.15 = (f32[8,512]{1,0:T(8,128)S(1)}, f32[8,512]{1,0:T(8,128)S(1)}, u32[]{:S(2)}, u32[]{:S(2)}) collective-permute-start(f32[8,512]{1,0:T(8,128)S(1)} %get-tuple-element.81), channel_id=1, source_target_pairs={{0,1},{1,0},{2,3},{3,2},{4,5},{5,4},{6,7},{7,6},{8,9},{9,8},{10,11... | collective-permute-start | bytes 49160 | tf_op jit(solution)/shard_map/ppermute | solution.py:799
  41.3 0.7 %density.1 = (f32[32,512]{1,0:T(8,128)S(1)}, f32[3,4,4,512]{3,2,1,0:T(4,128)}, f32[8,128]{1,0:T(8,128)S(1)}) custom-call(f32[40,512]{1,0:T(8,128)S(1)} %get-tuple-element.56.coef, f32[3,4,4,512]{3,2,1,0:T(4,128)S(1)} %get-tuple-element.47.disp.disp_new, f32[24,512]{1,0:T(8,128)S(1)} %get-tuple-element.76._), custom_call_target="tpu_custom_call" | custom-call | flops 1000000 | bytes 500000 | tf_op jit(solution)/shard_map/density/pallas_call | solution.py:782
  42.1 0.3 moments.1
  42.5 22.0 %all_to_all.11 = f32[256,1,128]{2,1,0:T(1,128)S(1)} all-to-all(f32[256,1,128]{2,1,0:T(1,128)S(1)} %bitcast.15), channel_id=1, replica_groups=mesh['lat'=8,'lon'=32] {'lat','lon'}, dimensions={0} | all-to-all | bytes 262144 | tf_op jit(solution)/shard_map/all_to_all | solution.py:909
  64.5 1.1 %final.1 = (f32[4,4,512]{2,1,0:T(4,128)}, f32[3,4,4,512]{3,2,1,0:T(4,128)}, f32[3,4,4,512]{3,2,1,0:T(4,128)}) custom-call(f32[256,128]{1,0:T(8,128)S(1)} %bitcast.14, f32[4,4,512]{2,1,0:T(4,128)S(1)} %get-tuple-element.48.phi, f32[4,4,512]{2,1,0:T(4,128)S(1)} %get-tuple-element.57.field.w0, f32[4,4,512]{2,1,0:T(4,128)S(1)} %get-tuple-element.68.field.w1, ...), custom_call_target="tpu_custom_call" | custom-call | flops 1000000 | bytes 500000 | tf_op jit(solution)/shard_map/final/pallas_call | solution.py:782
  (27 shorter events, 0.8 us)
Async XLA Ops:
  1.8 7.6 %collective-permute-start = (f32[16,512]{1,0:T(8,128)S(1)}, f32[16,512]{1,0:T(8,128)S(1)}, u32[]{:S(2)}, u32[]{:S(2)}) collective-permute-start(f32[16,512]{1,0:T(8,128)S(1)} %get-tuple-element.50), channel_id=1, source_target_pairs={{1,2},{2,1},{3,4},{4,3},{5,6},{6,5},{7,8},{8,7},{9,10},{10,9},{11,... | collective-permute-start | bytes 98312 | tf_op jit(solution)/shard_map/ppermute | solution.py:799
  4.6 4.8 %collective-permute-start.1 = (f32[16,512]{1,0:T(8,128)S(1)}, f32[16,512]{1,0:T(8,128)S(1)}, u32[]{:S(2)}, u32[]{:S(2)}) collective-permute-start(f32[16,512]{1,0:T(8,128)S(1)} %get-tuple-element.51), channel_id=1, source_target_pairs={{0,1},{1,0},{2,3},{3,2},{4,5},{5,4},{6,7},{7,6},{8,9},{9,8},{10,11... | collective-permute-start | bytes 98312 | tf_op jit(solution)/shard_map/ppermute | solution.py:799
  9.5 7.7 %collective-permute-start.2 = (f32[24,512]{1,0:T(8,128)S(1)}, f32[24,512]{1,0:T(8,128)S(1)}, u32[]{:S(2)}, u32[]{:S(2)}) collective-permute-start(f32[24,512]{1,0:T(8,128)S(1)} %get-tuple-element.53._), channel_id=1, source_target_pairs={{0,32},{32,0},{64,96},{96,64},{128,160},{160,128},{192,224},{224,1... | collective-permute-start | bytes 147464 | tf_op jit(solution)/shard_map/ppermute | solution.py:799
  11.2 6.1 %collective-permute-start.3 = (f32[24,512]{1,0:T(8,128)S(1)}, f32[24,512]{1,0:T(8,128)S(1)}, u32[]{:S(2)}, u32[]{:S(2)}) collective-permute-start(f32[24,512]{1,0:T(8,128)S(1)} %get-tuple-element.54), channel_id=1, source_target_pairs={{32,64},{64,32},{96,128},{128,96},{160,192},{192,160},{224,0},{0,2... | collective-permute-start | bytes 147464 | tf_op jit(solution)/shard_map/ppermute | solution.py:799
  15.9 1.1 %copy-start = (bf16[3,5,5,1,5,1,5,128]{7,0,6,5,4,3,2,1:T(4,128)(2,1)S(1)}, bf16[3,5,5,1,5,1,5,128]{7,0,6,5,4,3,2,1:T(4,128)(2,1)}, u32[]{:S(2)}) copy-start(bf16[3,5,5,1,5,1,5,128]{7,0,6,5,4,3,2,1:T(4,128)(2,1)} %param.15) | copy-start | bytes 1440004
  18.0 10.1 %collective-permute-start.4 = (f32[8,512]{1,0:T(8,128)S(1)}, f32[8,512]{1,0:T(8,128)S(1)}, u32[]{:S(2)}, u32[]{:S(2)}) collective-permute-start(f32[8,512]{1,0:T(8,128)S(1)} %get-tuple-element.59), channel_id=1, source_target_pairs={{1,2},{2,1},{3,4},{4,3},{5,6},{6,5},{7,8},{8,7},{9,10},{10,9},{11,... | collective-permute-start | bytes 49160 | tf_op jit(solution)/shard_map/ppermute | solution.py:799
  18.1 10.1 %collective-permute-start.5 = (f32[8,512]{1,0:T(8,128)S(1)}, f32[8,512]{1,0:T(8,128)S(1)}, u32[]{:S(2)}, u32[]{:S(2)}) collective-permute-start(f32[8,512]{1,0:T(8,128)S(1)} %get-tuple-element.60), channel_id=1, source_target_pairs={{0,32},{32,0},{64,96},{96,64},{128,160},{160,128},{192,224},{224,1... | collective-permute-start | bytes 49160 | tf_op jit(solution)/shard_map/ppermute | solution.py:799
  18.2 10.0 %collective-permute-start.6 = (f32[8,512]{1,0:T(8,128)S(1)}, f32[8,512]{1,0:T(8,128)S(1)}, u32[]{:S(2)}, u32[]{:S(2)}) collective-permute-start(f32[8,512]{1,0:T(8,128)S(1)} %get-tuple-element.61), channel_id=1, source_target_pairs={{32,64},{64,32},{96,128},{128,96},{160,192},{192,160},{224,0},{0,2... | collective-permute-start | bytes 49160 | tf_op jit(solution)/shard_map/ppermute | solution.py:799
  20.9 7.2 %collective-permute-start.7 = (f32[8,512]{1,0:T(8,128)S(1)}, f32[8,512]{1,0:T(8,128)S(1)}, u32[]{:S(2)}, u32[]{:S(2)}) collective-permute-start(f32[8,512]{1,0:T(8,128)S(1)} %get-tuple-element.62), channel_id=1, source_target_pairs={{0,1},{1,0},{2,3},{3,2},{4,5},{5,4},{6,7},{7,6},{8,9},{9,8},{10,11... | collective-permute-start | bytes 49160 | tf_op jit(solution)/shard_map/ppermute | solution.py:799
  28.1 36.3 %copy-start.1 = (f32[3,4,4,512]{3,2,1,0:T(4,128)S(1)}, f32[3,4,4,512]{3,2,1,0:T(4,128)}, u32[]{:S(2)}) copy-start(f32[3,4,4,512]{3,2,1,0:T(4,128)} %vel.1) | copy-start | bytes 294916
  28.2 36.3 %copy-start.2 = (f32[3,4,4,512]{3,2,1,0:T(4,128)S(1)}, f32[3,4,4,512]{3,2,1,0:T(4,128)}, u32[]{:S(2)}) copy-start(f32[3,4,4,512]{3,2,1,0:T(4,128)} %acc.1) | copy-start | bytes 294916
  28.4 5.8 %collective-permute-start.11 = (f32[24,512]{1,0:T(8,128)S(1)}, f32[24,512]{1,0:T(8,128)S(1)}, u32[]{:S(2)}, u32[]{:S(2)}) collective-permute-start(f32[24,512]{1,0:T(8,128)S(1)} %get-tuple-element.72), channel_id=1, source_target_pairs={{0,1},{1,0},{2,3},{3,2},{4,5},{5,4},{6,7},{7,6},{8,9},{9,8},{10,11... | collective-permute-start | bytes 147464 | tf_op jit(solution)/shard_map/ppermute | solution.py:799
  28.6 5.6 %collective-permute-start.8 = (f32[24,512]{1,0:T(8,128)S(1)}, f32[24,512]{1,0:T(8,128)S(1)}, u32[]{:S(2)}, u32[]{:S(2)}) collective-permute-start(f32[24,512]{1,0:T(8,128)S(1)} %get-tuple-element.69), channel_id=1, source_target_pairs={{1,2},{2,1},{3,4},{4,3},{5,6},{6,5},{7,8},{8,7},{9,10},{10,9},{11,... | collective-permute-start | bytes 147464 | tf_op jit(solution)/shard_map/ppermute | solution.py:799
  28.7 4.0 %collective-permute-start.10 = (f32[8,512]{1,0:T(8,128)S(1)}, f32[8,512]{1,0:T(8,128)S(1)}, u32[]{:S(2)}, u32[]{:S(2)}) collective-permute-start(f32[8,512]{1,0:T(8,128)S(1)} %get-tuple-element.71), channel_id=1, source_target_pairs={{32,64},{64,32},{96,128},{128,96},{160,192},{192,160},{224,0},{0,2... | collective-permute-start | bytes 49160 | tf_op jit(solution)/shard_map/ppermute | solution.py:799
  31.3 2.9 %collective-permute-start.9 = (f32[8,512]{1,0:T(8,128)S(1)}, f32[8,512]{1,0:T(8,128)S(1)}, u32[]{:S(2)}, u32[]{:S(2)}) collective-permute-start(f32[8,512]{1,0:T(8,128)S(1)} %get-tuple-element.70), channel_id=1, source_target_pairs={{0,32},{32,0},{64,96},{96,64},{128,160},{160,128},{192,224},{224,1... | collective-permute-start | bytes 49160 | tf_op jit(solution)/shard_map/ppermute | solution.py:799
  34.5 7.6 %collective-permute-start.12 = (f32[32,512]{1,0:T(8,128)S(1)}, f32[32,512]{1,0:T(8,128)S(1)}, u32[]{:S(2)}, u32[]{:S(2)}) collective-permute-start(f32[32,512]{1,0:T(8,128)S(1)} %get-tuple-element.79), channel_id=1, source_target_pairs={{1,2},{2,1},{3,4},{4,3},{5,6},{6,5},{7,8},{8,7},{9,10},{10,9},{11,... | collective-permute-start | bytes 196616 | tf_op jit(solution)/shard_map/ppermute | solution.py:799
  37.5 4.7 %collective-permute-start.13 = (f32[24,512]{1,0:T(8,128)S(1)}, f32[24,512]{1,0:T(8,128)S(1)}, u32[]{:S(2)}, u32[]{:S(2)}) collective-permute-start(f32[24,512]{1,0:T(8,128)S(1)} %get-tuple-element.76._), channel_id=1, source_target_pairs={{0,32},{32,0},{64,96},{96,64},{128,160},{160,128},{192,224},{224,1... | collective-permute-start | bytes 147464 | tf_op jit(solution)/shard_map/ppermute | solution.py:799
  37.5 4.7 %collective-permute-start.14 = (f32[24,512]{1,0:T(8,128)S(1)}, f32[24,512]{1,0:T(8,128)S(1)}, u32[]{:S(2)}, u32[]{:S(2)}) collective-permute-start(f32[24,512]{1,0:T(8,128)S(1)} %get-tuple-element.80), channel_id=1, source_target_pairs={{32,64},{64,32},{96,128},{128,96},{160,192},{192,160},{224,0},{0,2... | collective-permute-start | bytes 147464 | tf_op jit(solution)/shard_map/ppermute | solution.py:799
  38.8 3.4 %collective-permute-start.15 = (f32[8,512]{1,0:T(8,128)S(1)}, f32[8,512]{1,0:T(8,128)S(1)}, u32[]{:S(2)}, u32[]{:S(2)}) collective-permute-start(f32[8,512]{1,0:T(8,128)S(1)} %get-tuple-element.81), channel_id=1, source_target_pairs={{0,1},{1,0},{2,3},{3,2},{4,5},{5,4},{6,7},{7,6},{8,9},{9,8},{10,11... | collective-permute-start | bytes 49160 | tf_op jit(solution)/shard_map/ppermute | solution.py:799

commit v6 on v5

--- a/solution.py
+++ b/solution.py
@@ -173,7 +173,7 @@
 
 def start_kernel(
     disp_h, vel_h, acc_h, phi_h, mat_h, flag_h, dens_h,
-    disp_out, phi_out, info_out, lon0, lon1,
+    disp_out, phi_out, info_out, down_lat, lon0, lon1,
     disp, vel, acc, mat, flag, dens, sems,
 ):
     moves = [
@@ -217,8 +217,11 @@
     down = [u[comp][i][0:1] for comp in range(3) for i in range(4)]
     down += [potential[i][0:1] for i in range(4)]
     post("lon", (lon0, lon1), stack(up + [info], 16), stack(down, 16))
-
-def pack_kernel(lon_second, lon_first, disp, phi, own_info, _, lat0, lat1):
+    for comp in range(3):
+        down_lat[4 * comp : 4 * comp + 4, :] = u[comp][0]
+    down_lat[12:16, :] = potential[0]
+
+def pack_kernel(lon_second, lon_first, disp, phi, own_info, _, up_lat, corner):
     below, above = arrived("lon", lon_first, lon_second)
     potential = [phi[i] for i in range(4)]
     info = jnp.concatenate(
@@ -231,9 +234,8 @@
         info,
         below[12:13],
     ]
-    down = [disp[0, 0], disp[1, 0], disp[2, 0], potential[0]]
-    down += [above[4 * comp : 4 * comp + 1] for comp in range(3)]
-    post("lat", (lat0, lat1), stack(up, 24), stack(down, 24))
+    up_lat[...] = stack(up, 16)
+    corner[...] = stack([above[4 * comp : 4 * comp + 1] for comp in range(3)], 8)
 
 
 def lat_rows(factor):
@@ -288,11 +290,10 @@
 
 
 def residual_kernel(
-    disp_new, phi, own_info, lon_second, lat_first, lat_second, lon_first, _,
+    disp_new, phi, own_info, lon_second, lat_below, lat_above, lon_first, _,
     coef, precond_out, w0_out, lat0, lat1, lon0, lon1,
 ):
     following, before = has_next(), has_before()
-    lat_below, lat_above = arrived("lat", lat_first, lat_second)
     lon_below, lon_above = arrived("lon", lon_first, lon_second)
     rho, shell = (
         jnp.concatenate(
@@ -529,7 +530,7 @@
         phi_new[i] = value
         potential.append(value)
     following, before = has_next(), has_before()
-    ma, na = arrived("lat", a1, a2)
+    ma, na = a1[...], a2[...]
     mb, nb = arrived("lat", b1, b2)
     mc, nc = arrived("lat", c1, c2)
     md, nd = arrived("lat", d1, d2)
@@ -655,17 +656,16 @@
 
 
 def elastic_kernel(
-    lon_second, lat_first, lat_second, lon_first, stiff, rates, perm, own, decayed,
+    lon_second, corner, lat_above, lon_first, stiff, rates, perm, own, decayed,
     dense, force, lat_force, lon_force,
     points, edge, elems, devs, flux,
 ):
     following = has_next()
-    _, lat_above = arrived("lat", lat_first, lat_second)
     _, lon_above = arrived("lon", lon_first, lon_second)
     points[...] = jnp.zeros(points.shape, F32)
     for comp in range(3):
-        points[8 * comp : 8 * comp + 4, :] = following * lat_above[4 * comp : 4 * comp + 4]
-        points[8 * comp + 4 : 8 * comp + 5, :] = following * lat_above[16 + comp : 17 + comp]
+        points[8 * comp : 8 * comp + 4, :] = following * lat_above[4 * comp : 4 * comp + 4, :]
+        points[8 * comp + 4 : 8 * comp + 5, :] = following * corner[comp : comp + 1]
     points[24:36, :] = lon_above[0:12]
     to_nodes(points[...], perm, edge)
     fifth = sublanes((8, 128)) == 4
@@ -799,6 +799,10 @@
     return lax.ppermute(array, axis, pairs)
 
 
+def ring(array, axis, size, by):
+    return lax.ppermute(array, axis, [(i, (i + by) % size) for i in range(size)])
+
+
 def swap_lat(first, second):
     return swap(first, "lat", LAT, 0), swap(second, "lat", LAT, 1)
 
@@ -817,8 +821,8 @@
     r8, r16, r24, r32, r40 = (((n, 512), F32) for n in (8, 16, 24, 32, 40))
     info = ((8, 128), F32)
     kept = pltpu.with_memory_space_constraint
-    disp, phi, own_info, *sent = call(
-        start_kernel, "start", [vector, field, info, r16, r16], [HBM] * 7,
+    disp, phi, own_info, down_lat, *sent = call(
+        start_kernel, "start", [vector, field, info, r16, r16, r16], [HBM] * 7,
         [
             kept(array, pltpu.HBM)
             for array in (
@@ -836,6 +840,7 @@
         ],
     )
     lon_a = swap_lon(*sent)
+    above_a = ring(down_lat, "lat", LAT, -1)
     tables = call(
         prepare_kernel, "prepare",
         [((40, 128), F32), info, ((512, 512), BF16), ((5, 96, 128), F32)],
@@ -855,10 +860,11 @@
         ],
     )
     lat_a = call(
-        pack_kernel, "pack", [r24, r24], [VMEM] * 6,
+        pack_kernel, "pack", [r16, r8], [VMEM] * 6,
         (lon_a[1], lon_a[0], disp, phi, own_info, tables[1]),
     )
-    halo_a = (lon_a[1], *swap_lat(*lat_a), lon_a[0])
+    halo_a = (lon_a[1], ring(lat_a[0], "lat", LAT, 1), above_a, lon_a[0])
+    corner = ring(lat_a[1], "lat", LAT, -1)
     memory = memory_vars.reshape(3, 5, 5, 5, 5, 128).transpose(1, 2, 3, 4, 0, 5)
     every = ((375, 8, 128), F32)
     decayed, unpacked = call(
@@ -873,7 +879,7 @@
     halo_b = (lon_b[1], *swap_lat(*sent[:2]), lon_b[0])
     dense, force, lat_force, lon_force = call(
         elastic_kernel, "elastic", [every, vector, r16, r16], [VMEM] * 9,
-        (*halo_a, *tables, decayed),
+        (lon_a[1], corner, above_a, lon_a[0], *tables, decayed),
         [
             pltpu.VMEM((48, 512), F32),
             pltpu.VMEM((5, 48, 128), F32),

time: 65.9 us -> 65.2 us (0.989)
  waiting for transfers between devices: 1.89 us -> 0.72 us
    ppermute x0 -> x3, starting transfers between devices: none -> 8.32 us  [ring(): lax.ppermute(array, axis, [(i, (i + by) % size) for i in range(size)])]
    ppermute x16 -> x14, starting transfers between devices: 30.6 us -> 22.7 us  [swap(): return lax.ppermute(array, axis, pairs)]
    ppermute x16 -> x14, waiting for transfers between devices: 1.89 us -> 0.71 us  [swap(): return lax.ppermute(array, axis, pairs)]
  transfers between devices with their start and end apart: 16 -> 17, of which waited for: 3 -> 2; matrix products, arithmetic and copies ran while one was open for 0% -> 0% of each run, Pallas kernels for 8% -> 9%
where the time goes in v6:
time: 65.2 us; the launch traced here: 64.9 us
  starting transfers between devices  31.1 us (48%)
  blocking collectives  22 us (34%)
  Pallas kernels  9.25 us (14%)
  local copies, waits for them, and re-layouts  1.09 us (2%)
  between operations  0.82 us (1%)
  waiting for transfers between devices  0.72 us (1%)
    ppermute x14, starting transfers between devices, swap(): return lax.ppermute(array, axis, pairs)  22.7 us
    all_to_all x1, blocking collectives, per_device(): moments = lax.all_to_all(line, AXES, 0, 0, tiled=True)  22 us
    pallas_call x12, Pallas kernels, call(): pl.pallas_call(kernel, name=name, out_shape=[jax.ShapeDtypeStruct(s, d) f...  9.25 us
    ppermute x3, starting transfers between devices, ring(): lax.ppermute(array, axis, [(i, (i + by) % size) for i in range(size)])  8.32 us
  transfers between devices with their start and end apart: 17, of which 2 were waited for; matrix products, arithmetic and copies ran while one was open for 0% of the time, Pallas kernels for 9%

profile of v6, /device:TPU:1, one launch (start us, length us, event | category | flops | bytes accessed | tf_op | source)
XLA Modules:
  0.0 64.9 jit_solution(12801972413560694849)
XLA Ops:
  0.6 1.2 %start.1 = (f32[3,4,4,512]{3,2,1,0:T(4,128)S(1)}, f32[4,4,512]{2,1,0:T(4,128)S(1)}, f32[8,128]{1,0:T(8,128)S(1)}, f32[16,512]{1,0:T(8,128)S(1)}, f32[16,512]{1,0:T(8,128)S(1)}, /*index=5*/f32[16,512]{1,0:T(8,128)S(1)}) custom-call(f32[3,4,4,512]{3,2,1,0:T(4,128)} %disp_h.1, f32[3,4,4,512]{3,2,1,0:T(4,128)} %vel.1, f32[3,4,4,512]{3,2,1,0:T(4,128)} %acc.1, ...), custom_call_target="tpu_custom_call" | custom-call | flops 1000000 | bytes 500000 | tf_op jit(solution)/shard_map/start/pallas_call | solution.py:782
  1.8 2.8 %collective-permute-start = (f32[16,512]{1,0:T(8,128)S(1)}, f32[16,512]{1,0:T(8,128)S(1)}, u32[]{:S(2)}, u32[]{:S(2)}) collective-permute-start(f32[16,512]{1,0:T(8,128)S(1)} %get-tuple-element.51), channel_id=1, source_target_pairs={{1,2},{2,1},{3,4},{4,3},{5,6},{6,5},{7,8},{8,7},{9,10},{10,9},{11,... | collective-permute-start | bytes 98312 | tf_op jit(solution)/shard_map/ppermute | solution.py:799
  4.6 3.5 %collective-permute-start.1 = (f32[16,512]{1,0:T(8,128)S(1)}, f32[16,512]{1,0:T(8,128)S(1)}, u32[]{:S(2)}, u32[]{:S(2)}) collective-permute-start(f32[16,512]{1,0:T(8,128)S(1)} %get-tuple-element.52), channel_id=1, source_target_pairs={{0,1},{1,0},{2,3},{3,2},{4,5},{5,4},{6,7},{7,6},{8,9},{9,8},{10,11... | collective-permute-start | bytes 98312 | tf_op jit(solution)/shard_map/ppermute | solution.py:799
  8.1 5.6 %collective-permute-start.3 = (f32[16,512]{1,0:T(8,128)S(1)}, f32[16,512]{1,0:T(8,128)S(1)}, u32[]{:S(2)}, u32[]{:S(2)}) collective-permute-start(f32[16,512]{1,0:T(8,128)S(1)} %get-tuple-element.55), channel_id=1, source_target_pairs={{0,224},{32,0},{64,32},{96,64},{128,96},{160,128},{192,160},{224,1... | collective-permute-start | bytes 98312 | tf_op jit(solution)/shard_map/ppermute | solution.py:803
  13.7 1.3 %prepare.1 = (f32[40,128]{1,0:T(8,128)S(1)}, f32[8,128]{1,0:T(8,128)S(1)}, bf16[512,512]{1,0:T(8,128)(2,1)S(1)}, f32[5,96,128]{2,1,0:T(8,128)S(1)}) custom-call(f32[3,4,4,512]{3,2,1,0:T(4,128)S(1)} %get-tuple-element.48.disp.disp_new, s32[1,1,128]{2,1,0:T(1,128)} %mat_h.3, f32[6,8,6]{2,1,0:T(8,128)} %bitcast.16, f32[3]{0:T(128)} %decay_h.1, f32[3]{0:T(128)} %strength_h.1), custom_call_target="tpu_custom_call" | custom-call | flops 1000000 | bytes 500000 | tf_op jit(solution)/shard_map/prepare/pallas_call | solution.py:782
  15.2 2.7 %collective-permute-start.8 = (f32[8,512]{1,0:T(8,128)S(1)}, f32[8,512]{1,0:T(8,128)S(1)}, u32[]{:S(2)}, u32[]{:S(2)}) collective-permute-start(f32[8,512]{1,0:T(8,128)S(1)} %get-tuple-element.64), channel_id=1, source_target_pairs={{0,224},{32,0},{64,32},{96,64},{128,96},{160,128},{192,160},{224,1... | collective-permute-start | bytes 49160 | tf_op jit(solution)/shard_map/ppermute | solution.py:803
  17.8 1.1 %copy-done = bf16[3,5,5,1,5,1,5,128]{7,0,6,5,4,3,2,1:T(4,128)(2,1)S(1)} copy-done((bf16[3,5,5,1,5,1,5,128]{7,0,6,5,4,3,2,1:T(4,128)(2,1)S(1)}, bf16[3,5,5,1,5,1,5,128]{7,0,6,5,4,3,2,1:T(4,128)(2,1)}, u32[]{:S(2)}) %copy-start) | copy-done | bytes 480024
  19.2 0.6 residual.1
  20.2 5.0 %collective-permute-start.7 = (f32[8,512]{1,0:T(8,128)S(1)}, f32[8,512]{1,0:T(8,128)S(1)}, u32[]{:S(2)}, u32[]{:S(2)}) collective-permute-start(f32[8,512]{1,0:T(8,128)S(1)} %get-tuple-element.63), channel_id=1, source_target_pairs={{0,1},{1,0},{2,3},{3,2},{4,5},{5,4},{6,7},{7,6},{8,9},{9,8},{10,11... | collective-permute-start | bytes 49160 | tf_op jit(solution)/shard_map/ppermute | solution.py:799
  25.2 1.8 %elastic.1 = (f32[375,8,128]{2,1,0:T(8,128)S(1)}, f32[3,4,4,512]{3,2,1,0:T(4,128)S(1)}, f32[16,512]{1,0:T(8,128)S(1)}, f32[16,512]{1,0:T(8,128)S(1)}) custom-call(f32[16,512]{1,0:T(8,128)S(1)} %collective-permute-done.lon_second.a0, f32[8,512]{1,0:T(8,128)S(1)} %collective-permute-done.8.corner, f32[16,512]{1,0:T(8,128)S(1)} %collective-permute-done.3.lat_above.a2, ...), custom_call_target="tpu_custom_call" | custom-call | flops 20000000 | bytes 2000000 | tf_op jit(solution)/shard_map/elastic/pallas_call | solution.py:782
  27.1 0.3 second.1
  27.4 0.7 %collective-permute-start.12 = (f32[24,512]{1,0:T(8,128)S(1)}, f32[24,512]{1,0:T(8,128)S(1)}, u32[]{:S(2)}, u32[]{:S(2)}) collective-permute-start(f32[24,512]{1,0:T(8,128)S(1)} %get-tuple-element.74), channel_id=1, source_target_pairs={{0,1},{1,0},{2,3},{3,2},{4,5},{5,4},{6,7},{7,6},{8,9},{9,8},{10,11... | collective-permute-start | bytes 147464 | tf_op jit(solution)/shard_map/ppermute | solution.py:799
  28.1 0.3 collective-permute-start.10
  28.4 2.0 %collective-permute-start.11 = (f32[8,512]{1,0:T(8,128)S(1)}, f32[8,512]{1,0:T(8,128)S(1)}, u32[]{:S(2)}, u32[]{:S(2)}) collective-permute-start(f32[8,512]{1,0:T(8,128)S(1)} %get-tuple-element.73), channel_id=1, source_target_pairs={{32,64},{64,32},{96,128},{128,96},{160,192},{192,160},{224,0},{0,2... | collective-permute-start | bytes 49160 | tf_op jit(solution)/shard_map/ppermute | solution.py:799
  30.4 1.3 %repack.1 = (bf16[5,5,5,5,3,128]{5,4,3,2,1,0:T(4,128)(2,1)}, f32[8,128]{1,0:T(8,128)S(1)}) custom-call(f32[375,8,128]{2,1,0:T(8,128)S(1)} %get-tuple-element.76.dense), custom_call_target="tpu_custom_call" | custom-call | flops 1000000 | bytes 500000 | tf_op jit(solution)/shard_map/repack/pallas_call | solution.py:782
  31.7 0.5 collective-permute-done.11.lat_second.c2
  32.2 0.3 third.1
  32.5 3.4 %collective-permute-start.13 = (f32[32,512]{1,0:T(8,128)S(1)}, f32[32,512]{1,0:T(8,128)S(1)}, u32[]{:S(2)}, u32[]{:S(2)}) collective-permute-start(f32[32,512]{1,0:T(8,128)S(1)} %get-tuple-element.81), channel_id=1, source_target_pairs={{1,2},{2,1},{3,4},{4,3},{5,6},{6,5},{7,8},{8,7},{9,10},{10,9},{11,... | collective-permute-start | bytes 196616 | tf_op jit(solution)/shard_map/ppermute | solution.py:799
  35.9 2.1 %collective-permute-start.15 = (f32[24,512]{1,0:T(8,128)S(1)}, f32[24,512]{1,0:T(8,128)S(1)}, u32[]{:S(2)}, u32[]{:S(2)}) collective-permute-start(f32[24,512]{1,0:T(8,128)S(1)} %get-tuple-element.82), channel_id=1, source_target_pairs={{32,64},{64,32},{96,128},{128,96},{160,192},{192,160},{224,0},{0,2... | collective-permute-start | bytes 147464 | tf_op jit(solution)/shard_map/ppermute | solution.py:799
  38.0 2.5 %collective-permute-start.16 = (f32[8,512]{1,0:T(8,128)S(1)}, f32[8,512]{1,0:T(8,128)S(1)}, u32[]{:S(2)}, u32[]{:S(2)}) collective-permute-start(f32[8,512]{1,0:T(8,128)S(1)} %get-tuple-element.83), channel_id=1, source_target_pairs={{0,1},{1,0},{2,3},{3,2},{4,5},{5,4},{6,7},{7,6},{8,9},{9,8},{10,11... | collective-permute-start | bytes 49160 | tf_op jit(solution)/shard_map/ppermute | solution.py:799
  40.6 0.7 %density.1 = (f32[32,512]{1,0:T(8,128)S(1)}, f32[3,4,4,512]{3,2,1,0:T(4,128)}, f32[8,128]{1,0:T(8,128)S(1)}) custom-call(f32[40,512]{1,0:T(8,128)S(1)} %get-tuple-element.57.coef, f32[3,4,4,512]{3,2,1,0:T(4,128)S(1)} %get-tuple-element.48.disp.disp_new, f32[24,512]{1,0:T(8,128)S(1)} %get-tuple-element.78._), custom_call_target="tpu_custom_call" | custom-call | flops 1000000 | bytes 500000 | tf_op jit(solution)/shard_map/density/pallas_call | solution.py:782
  41.4 0.3 moments.1
  41.8 22.0 %all_to_all.11 = f32[256,1,128]{2,1,0:T(1,128)S(1)} all-to-all(f32[256,1,128]{2,1,0:T(1,128)S(1)} %bitcast.15), channel_id=1, replica_groups=mesh['lat'=8,'lon'=32] {'lat','lon'}, dimensions={0} | all-to-all | bytes 262144 | tf_op jit(solution)/shard_map/all_to_all | solution.py:915
  63.8 1.1 %final.1 = (f32[4,4,512]{2,1,0:T(4,128)}, f32[3,4,4,512]{3,2,1,0:T(4,128)}, f32[3,4,4,512]{3,2,1,0:T(4,128)}) custom-call(f32[256,128]{1,0:T(8,128)S(1)} %bitcast.14, f32[4,4,512]{2,1,0:T(4,128)S(1)} %get-tuple-element.49.phi, f32[4,4,512]{2,1,0:T(4,128)S(1)} %get-tuple-element.58.field.w0, f32[4,4,512]{2,1,0:T(4,128)S(1)} %get-tuple-element.70.field.w1, ...), custom_call_target="tpu_custom_call" | custom-call | flops 1000000 | bytes 500000 | tf_op jit(solution)/shard_map/final/pallas_call | solution.py:782
  (29 shorter events, 1.0 us)
Async XLA Ops:
  1.8 13.2 %collective-permute-start = (f32[16,512]{1,0:T(8,128)S(1)}, f32[16,512]{1,0:T(8,128)S(1)}, u32[]{:S(2)}, u32[]{:S(2)}) collective-permute-start(f32[16,512]{1,0:T(8,128)S(1)} %get-tuple-element.51), channel_id=1, source_target_pairs={{1,2},{2,1},{3,4},{4,3},{5,6},{6,5},{7,8},{8,7},{9,10},{10,9},{11,... | collective-permute-start | bytes 98312 | tf_op jit(solution)/shard_map/ppermute | solution.py:799
  4.6 10.4 %collective-permute-start.1 = (f32[16,512]{1,0:T(8,128)S(1)}, f32[16,512]{1,0:T(8,128)S(1)}, u32[]{:S(2)}, u32[]{:S(2)}) collective-permute-start(f32[16,512]{1,0:T(8,128)S(1)} %get-tuple-element.52), channel_id=1, source_target_pairs={{0,1},{1,0},{2,3},{3,2},{4,5},{5,4},{6,7},{7,6},{8,9},{9,8},{10,11... | collective-permute-start | bytes 98312 | tf_op jit(solution)/shard_map/ppermute | solution.py:799
  8.1 11.1 %collective-permute-start.3 = (f32[16,512]{1,0:T(8,128)S(1)}, f32[16,512]{1,0:T(8,128)S(1)}, u32[]{:S(2)}, u32[]{:S(2)}) collective-permute-start(f32[16,512]{1,0:T(8,128)S(1)} %get-tuple-element.55), channel_id=1, source_target_pairs={{0,224},{32,0},{64,32},{96,64},{128,96},{160,128},{192,160},{224,1... | collective-permute-start | bytes 98312 | tf_op jit(solution)/shard_map/ppermute | solution.py:803
  15.1 4.1 %collective-permute-start.2 = (f32[16,512]{1,0:T(8,128)S(1)}, f32[16,512]{1,0:T(8,128)S(1)}, u32[]{:S(2)}, u32[]{:S(2)}) collective-permute-start(f32[16,512]{1,0:T(8,128)S(1)} %get-tuple-element.54._), channel_id=1, source_target_pairs={{0,32},{32,64},{64,96},{96,128},{128,160},{160,192},{192,224},{224... | collective-permute-start | bytes 98312 | tf_op jit(solution)/shard_map/ppermute | solution.py:803
  15.2 10.1 %collective-permute-start.8 = (f32[8,512]{1,0:T(8,128)S(1)}, f32[8,512]{1,0:T(8,128)S(1)}, u32[]{:S(2)}, u32[]{:S(2)}) collective-permute-start(f32[8,512]{1,0:T(8,128)S(1)} %get-tuple-element.64), channel_id=1, source_target_pairs={{0,224},{32,0},{64,32},{96,64},{128,96},{160,128},{192,160},{224,1... | collective-permute-start | bytes 49160 | tf_op jit(solution)/shard_map/ppermute | solution.py:803
  17.8 1.1 %copy-start = (bf16[3,5,5,1,5,1,5,128]{7,0,6,5,4,3,2,1:T(4,128)(2,1)S(1)}, bf16[3,5,5,1,5,1,5,128]{7,0,6,5,4,3,2,1:T(4,128)(2,1)}, u32[]{:S(2)}) copy-start(bf16[3,5,5,1,5,1,5,128]{7,0,6,5,4,3,2,1:T(4,128)(2,1)} %param.15) | copy-start | bytes 1440004
  19.8 7.3 %collective-permute-start.4 = (f32[8,512]{1,0:T(8,128)S(1)}, f32[8,512]{1,0:T(8,128)S(1)}, u32[]{:S(2)}, u32[]{:S(2)}) collective-permute-start(f32[8,512]{1,0:T(8,128)S(1)} %get-tuple-element.60), channel_id=1, source_target_pairs={{1,2},{2,1},{3,4},{4,3},{5,6},{6,5},{7,8},{8,7},{9,10},{10,9},{11,... | collective-permute-start | bytes 49160 | tf_op jit(solution)/shard_map/ppermute | solution.py:799
  19.9 7.2 %collective-permute-start.5 = (f32[8,512]{1,0:T(8,128)S(1)}, f32[8,512]{1,0:T(8,128)S(1)}, u32[]{:S(2)}, u32[]{:S(2)}) collective-permute-start(f32[8,512]{1,0:T(8,128)S(1)} %get-tuple-element.61), channel_id=1, source_target_pairs={{0,32},{32,0},{64,96},{96,64},{128,160},{160,128},{192,224},{224,1... | collective-permute-start | bytes 49160 | tf_op jit(solution)/shard_map/ppermute | solution.py:799
  20.0 7.1 %collective-permute-start.6 = (f32[8,512]{1,0:T(8,128)S(1)}, f32[8,512]{1,0:T(8,128)S(1)}, u32[]{:S(2)}, u32[]{:S(2)}) collective-permute-start(f32[8,512]{1,0:T(8,128)S(1)} %get-tuple-element.62), channel_id=1, source_target_pairs={{32,64},{64,32},{96,128},{128,96},{160,192},{192,160},{224,0},{0,2... | collective-permute-start | bytes 49160 | tf_op jit(solution)/shard_map/ppermute | solution.py:799
  20.2 6.9 %collective-permute-start.7 = (f32[8,512]{1,0:T(8,128)S(1)}, f32[8,512]{1,0:T(8,128)S(1)}, u32[]{:S(2)}, u32[]{:S(2)}) collective-permute-start(f32[8,512]{1,0:T(8,128)S(1)} %get-tuple-element.63), channel_id=1, source_target_pairs={{0,1},{1,0},{2,3},{3,2},{4,5},{5,4},{6,7},{7,6},{8,9},{9,8},{10,11... | collective-permute-start | bytes 49160 | tf_op jit(solution)/shard_map/ppermute | solution.py:799
  27.1 36.7 %copy-start.1 = (f32[3,4,4,512]{3,2,1,0:T(4,128)S(1)}, f32[3,4,4,512]{3,2,1,0:T(4,128)}, u32[]{:S(2)}) copy-start(f32[3,4,4,512]{3,2,1,0:T(4,128)} %vel.1) | copy-start | bytes 294916
  27.1 36.7 %copy-start.2 = (f32[3,4,4,512]{3,2,1,0:T(4,128)S(1)}, f32[3,4,4,512]{3,2,1,0:T(4,128)}, u32[]{:S(2)}) copy-start(f32[3,4,4,512]{3,2,1,0:T(4,128)} %acc.1) | copy-start | bytes 294916
  27.4 4.8 %collective-permute-start.12 = (f32[24,512]{1,0:T(8,128)S(1)}, f32[24,512]{1,0:T(8,128)S(1)}, u32[]{:S(2)}, u32[]{:S(2)}) collective-permute-start(f32[24,512]{1,0:T(8,128)S(1)} %get-tuple-element.74), channel_id=1, source_target_pairs={{0,1},{1,0},{2,3},{3,2},{4,5},{5,4},{6,7},{7,6},{8,9},{9,8},{10,11... | collective-permute-start | bytes 147464 | tf_op jit(solution)/shard_map/ppermute | solution.py:799
  28.1 4.1 %collective-permute-start.9 = (f32[24,512]{1,0:T(8,128)S(1)}, f32[24,512]{1,0:T(8,128)S(1)}, u32[]{:S(2)}, u32[]{:S(2)}) collective-permute-start(f32[24,512]{1,0:T(8,128)S(1)} %get-tuple-element.71), channel_id=1, source_target_pairs={{1,2},{2,1},{3,4},{4,3},{5,6},{6,5},{7,8},{8,7},{9,10},{10,9},{11,... | collective-permute-start | bytes 147464 | tf_op jit(solution)/shard_map/ppermute | solution.py:799
  28.1 3.6 %collective-permute-start.10 = (f32[8,512]{1,0:T(8,128)S(1)}, f32[8,512]{1,0:T(8,128)S(1)}, u32[]{:S(2)}, u32[]{:S(2)}) collective-permute-start(f32[8,512]{1,0:T(8,128)S(1)} %get-tuple-element.72), channel_id=1, source_target_pairs={{0,32},{32,0},{64,96},{96,64},{128,160},{160,128},{192,224},{224,1... | collective-permute-start | bytes 49160 | tf_op jit(solution)/shard_map/ppermute | solution.py:799
  28.4 3.8 %collective-permute-start.11 = (f32[8,512]{1,0:T(8,128)S(1)}, f32[8,512]{1,0:T(8,128)S(1)}, u32[]{:S(2)}, u32[]{:S(2)}) collective-permute-start(f32[8,512]{1,0:T(8,128)S(1)} %get-tuple-element.73), channel_id=1, source_target_pairs={{32,64},{64,32},{96,128},{128,96},{160,192},{192,160},{224,0},{0,2... | collective-permute-start | bytes 49160 | tf_op jit(solution)/shard_map/ppermute | solution.py:799
  32.5 8.9 %collective-permute-start.13 = (f32[32,512]{1,0:T(8,128)S(1)}, f32[32,512]{1,0:T(8,128)S(1)}, u32[]{:S(2)}, u32[]{:S(2)}) collective-permute-start(f32[32,512]{1,0:T(8,128)S(1)} %get-tuple-element.81), channel_id=1, source_target_pairs={{1,2},{2,1},{3,4},{4,3},{5,6},{6,5},{7,8},{8,7},{9,10},{10,9},{11,... | collective-permute-start | bytes 196616 | tf_op jit(solution)/shard_map/ppermute | solution.py:799
  35.9 5.5 %collective-permute-start.14 = (f32[24,512]{1,0:T(8,128)S(1)}, f32[24,512]{1,0:T(8,128)S(1)}, u32[]{:S(2)}, u32[]{:S(2)}) collective-permute-start(f32[24,512]{1,0:T(8,128)S(1)} %get-tuple-element.78._), channel_id=1, source_target_pairs={{0,32},{32,0},{64,96},{96,64},{128,160},{160,128},{192,224},{224,1... | collective-permute-start | bytes 147464 | tf_op jit(solution)/shard_map/ppermute | solution.py:799
  35.9 5.5 %collective-permute-start.15 = (f32[24,512]{1,0:T(8,128)S(1)}, f32[24,512]{1,0:T(8,128)S(1)}, u32[]{:S(2)}, u32[]{:S(2)}) collective-permute-start(f32[24,512]{1,0:T(8,128)S(1)} %get-tuple-element.82), channel_id=1, source_target_pairs={{32,64},{64,32},{96,128},{128,96},{160,192},{192,160},{224,0},{0,2... | collective-permute-start | bytes 147464 | tf_op jit(solution)/shard_map/ppermute | solution.py:799
  38.0 3.4 %collective-permute-start.16 = (f32[8,512]{1,0:T(8,128)S(1)}, f32[8,512]{1,0:T(8,128)S(1)}, u32[]{:S(2)}, u32[]{:S(2)}) collective-permute-start(f32[8,512]{1,0:T(8,128)S(1)} %get-tuple-element.83), channel_id=1, source_target_pairs={{0,1},{1,0},{2,3},{3,2},{4,5},{5,4},{6,7},{7,6},{8,9},{9,8},{10,11... | collective-permute-start | bytes 49160 | tf_op jit(solution)/shard_map/ppermute | solution.py:799

commit v7 on v6

--- a/solution.py
+++ b/solution.py
@@ -290,7 +290,7 @@
 
 
 def residual_kernel(
-    disp_new, phi, own_info, lon_second, lat_below, lat_above, lon_first, _,
+    disp_new, phi, own_info, lon_second, lat_below, lat_above, lon_first,
     coef, precond_out, w0_out, lat0, lat1, lon0, lon1,
 ):
     following, before = has_next(), has_before()
@@ -867,13 +867,13 @@
     corner = ring(lat_a[1], "lat", LAT, -1)
     memory = memory_vars.reshape(3, 5, 5, 5, 5, 128).transpose(1, 2, 3, 4, 0, 5)
     every = ((375, 8, 128), F32)
-    decayed, unpacked = call(
-        unpack_kernel, "unpack", [every, info], [VMEM] * 3, (memory, tables[1], lat_a[0]),
+    coef, precond, w0, *sent = call(
+        residual_kernel, "residual", [r40, field, field, r8, r8, r8, r8], [VMEM] * 7,
+        (disp, phi, own_info, *halo_a),
+    )
+    decayed, _ = call(
+        unpack_kernel, "unpack", [every, info], [VMEM] * 3, (memory, tables[1], sent[0]),
         [pltpu.VMEM((160, 128), F32)],
-    )
-    coef, precond, w0, *sent = call(
-        residual_kernel, "residual", [r40, field, field, r8, r8, r8, r8], [VMEM] * 8,
-        (disp, phi, own_info, *halo_a, unpacked),
     )
     lon_b = swap_lon(*sent[2:])
     halo_b = (lon_b[1], *swap_lat(*sent[:2]), lon_b[0])

time: 65.2 us -> 67.4 us (1.034)
  blocking collectives: 22 us -> 23.6 us
  starting transfers between devices: 31.1 us -> 30.1 us
  waiting for transfers between devices: 0.72 us -> 1.69 us
    all_to_all x1, blocking collectives: 22 us -> 23.6 us  [per_device(): moments = lax.all_to_all(line, AXES, 0, 0, tiled=True)]
    ppermute x3, waiting for transfers between devices: 0.01 us -> 1.3 us  [ring(): lax.ppermute(array, axis, [(i, (i + by) % size) for i in range(size)])]
    ppermute x14, starting transfers between devices: 22.7 us -> 21.8 us  [swap(): return lax.ppermute(array, axis, pairs)]
  transfers between devices with their start and end apart: 17 -> 17, of which waited for: 2 -> 3; matrix products, arithmetic and copies ran while one was open for 0% -> 0% of each run, Pallas kernels for 9% -> 10%
where the time goes in v7:
time: 67.4 us; the launch traced here: 67.1 us
  starting transfers between devices  30.1 us (45%)
  blocking collectives  23.6 us (35%)
  Pallas kernels  9.81 us (15%)
  waiting for transfers between devices  1.69 us (3%)
  local copies, waits for them, and re-layouts  1.09 us (2%)
  between operations  0.82 us (1%)
    all_to_all x1, blocking collectives, per_device(): moments = lax.all_to_all(line, AXES, 0, 0, tiled=True)  23.6 us
    ppermute x14, starting transfers between devices, swap(): return lax.ppermute(array, axis, pairs)  21.8 us
    pallas_call x12, Pallas kernels, call(): pl.pallas_call(kernel, name=name, out_shape=[jax.ShapeDtypeStruct(s, d) f...  9.81 us
    ppermute x3, starting transfers between devices, ring(): lax.ppermute(array, axis, [(i, (i + by) % size) for i in range(size)])  8.32 us
  transfers between devices with their start and end apart: 17, of which 3 were waited for; matrix products, arithmetic and copies ran while one was open for 0% of the time, Pallas kernels for 10%

profile of v7, /device:TPU:1, one launch (start us, length us, event | category | flops | bytes accessed | tf_op | source)
XLA Modules:
  0.0 67.1 jit_solution(4854990430124049596)
XLA Ops:
  0.6 1.2 %start.1 = (f32[3,4,4,512]{3,2,1,0:T(4,128)S(1)}, f32[4,4,512]{2,1,0:T(4,128)S(1)}, f32[8,128]{1,0:T(8,128)S(1)}, f32[16,512]{1,0:T(8,128)S(1)}, f32[16,512]{1,0:T(8,128)S(1)}, /*index=5*/f32[16,512]{1,0:T(8,128)S(1)}) custom-call(f32[3,4,4,512]{3,2,1,0:T(4,128)} %disp_h.1, f32[3,4,4,512]{3,2,1,0:T(4,128)} %vel.1, f32[3,4,4,512]{3,2,1,0:T(4,128)} %acc.1, ...), custom_call_target="tpu_custom_call" | custom-call | flops 1000000 | bytes 500000 | tf_op jit(solution)/shard_map/start/pallas_call | solution.py:782
  1.8 2.8 %collective-permute-start = (f32[16,512]{1,0:T(8,128)S(1)}, f32[16,512]{1,0:T(8,128)S(1)}, u32[]{:S(2)}, u32[]{:S(2)}) collective-permute-start(f32[16,512]{1,0:T(8,128)S(1)} %get-tuple-element.50), channel_id=1, source_target_pairs={{1,2},{2,1},{3,4},{4,3},{5,6},{6,5},{7,8},{8,7},{9,10},{10,9},{11,... | collective-permute-start | bytes 98312 | tf_op jit(solution)/shard_map/ppermute | solution.py:799
  4.6 3.5 %collective-permute-start.1 = (f32[16,512]{1,0:T(8,128)S(1)}, f32[16,512]{1,0:T(8,128)S(1)}, u32[]{:S(2)}, u32[]{:S(2)}) collective-permute-start(f32[16,512]{1,0:T(8,128)S(1)} %get-tuple-element.51), channel_id=1, source_target_pairs={{0,1},{1,0},{2,3},{3,2},{4,5},{5,4},{6,7},{7,6},{8,9},{9,8},{10,11... | collective-permute-start | bytes 98312 | tf_op jit(solution)/shard_map/ppermute | solution.py:799
  8.1 5.6 %collective-permute-start.3 = (f32[16,512]{1,0:T(8,128)S(1)}, f32[16,512]{1,0:T(8,128)S(1)}, u32[]{:S(2)}, u32[]{:S(2)}) collective-permute-start(f32[16,512]{1,0:T(8,128)S(1)} %get-tuple-element.54), channel_id=1, source_target_pairs={{0,224},{32,0},{64,32},{96,64},{128,96},{160,128},{192,160},{224,1... | collective-permute-start | bytes 98312 | tf_op jit(solution)/shard_map/ppermute | solution.py:803
  13.7 1.3 %prepare.1 = (f32[40,128]{1,0:T(8,128)S(1)}, f32[8,128]{1,0:T(8,128)S(1)}, bf16[512,512]{1,0:T(8,128)(2,1)S(1)}, f32[5,96,128]{2,1,0:T(8,128)S(1)}) custom-call(f32[3,4,4,512]{3,2,1,0:T(4,128)S(1)} %get-tuple-element.47.disp.disp_new, s32[1,1,128]{2,1,0:T(1,128)} %mat_h.3, f32[6,8,6]{2,1,0:T(8,128)} %bitcast.16, f32[3]{0:T(128)} %decay_h.1, f32[3]{0:T(128)} %strength_h.1), custom_call_target="tpu_custom_call" | custom-call | flops 1000000 | bytes 500000 | tf_op jit(solution)/shard_map/prepare/pallas_call | solution.py:782
  15.2 2.7 %collective-permute-start.8 = (f32[8,512]{1,0:T(8,128)S(1)}, f32[8,512]{1,0:T(8,128)S(1)}, u32[]{:S(2)}, u32[]{:S(2)}) collective-permute-start(f32[8,512]{1,0:T(8,128)S(1)} %get-tuple-element.62), channel_id=1, source_target_pairs={{0,224},{32,0},{64,32},{96,64},{128,96},{160,128},{192,160},{224,1... | collective-permute-start | bytes 49160 | tf_op jit(solution)/shard_map/ppermute | solution.py:803
  17.8 1.3 %collective-permute-done.2.lat_below.a1 = f32[16,512]{1,0:T(8,128)S(1)} collective-permute-done((f32[16,512]{1,0:T(8,128)S(1)}, f32[16,512]{1,0:T(8,128)S(1)}, u32[]{:S(2)}, u32[]{:S(2)}) %collective-permute-start.2) | collective-permute-done | bytes 32800 | tf_op jit(solution)/shard_map/ppermute | solution.py:803
  19.1 0.6 residual.1
  19.9 4.5 %collective-permute-start.7 = (f32[8,512]{1,0:T(8,128)S(1)}, f32[8,512]{1,0:T(8,128)S(1)}, u32[]{:S(2)}, u32[]{:S(2)}) collective-permute-start(f32[8,512]{1,0:T(8,128)S(1)} %get-tuple-element.61), channel_id=1, source_target_pairs={{0,1},{1,0},{2,3},{3,2},{4,5},{5,4},{6,7},{7,6},{8,9},{9,8},{10,11... | collective-permute-start | bytes 49160 | tf_op jit(solution)/shard_map/ppermute | solution.py:799
  24.4 1.1 %copy-done = bf16[3,5,5,1,5,1,5,128]{7,0,6,5,4,3,2,1:T(4,128)(2,1)S(1)} copy-done((bf16[3,5,5,1,5,1,5,128]{7,0,6,5,4,3,2,1:T(4,128)(2,1)S(1)}, bf16[3,5,5,1,5,1,5,128]{7,0,6,5,4,3,2,1:T(4,128)(2,1)}, u32[]{:S(2)}) %copy-start) | copy-done | bytes 480024
  25.5 0.8 %unpack.1 = (f32[375,8,128]{2,1,0:T(8,128)S(1)}, f32[8,128]{1,0:T(8,128)}) custom-call(bf16[5,5,5,5,3,128]{5,4,3,2,1,0:T(4,128)(2,1)S(1)} %bitcast.13, f32[8,128]{1,0:T(8,128)S(1)} %get-tuple-element.52._.rates, f32[8,512]{1,0:T(8,128)S(1)} %get-tuple-element.59._), custom_call_target="tpu_custom_call" | custom-call | flops 1000000 | bytes 500000 | tf_op jit(solution)/shard_map/unpack/pallas_call | solution.py:782
  26.4 1.8 %elastic.1 = (f32[375,8,128]{2,1,0:T(8,128)S(1)}, f32[3,4,4,512]{3,2,1,0:T(4,128)S(1)}, f32[16,512]{1,0:T(8,128)S(1)}, f32[16,512]{1,0:T(8,128)S(1)}) custom-call(f32[16,512]{1,0:T(8,128)S(1)} %collective-permute-done.lon_second.a0, f32[8,512]{1,0:T(8,128)S(1)} %collective-permute-done.8.corner, f32[16,512]{1,0:T(8,128)S(1)} %collective-permute-done.3.lat_above.a2, ...), custom_call_target="tpu_custom_call" | custom-call | flops 20000000 | bytes 2000000 | tf_op jit(solution)/shard_map/elastic/pallas_call | solution.py:782
  28.6 1.9 %collective-permute-start.12 = (f32[24,512]{1,0:T(8,128)S(1)}, f32[24,512]{1,0:T(8,128)S(1)}, u32[]{:S(2)}, u32[]{:S(2)}) collective-permute-start(f32[24,512]{1,0:T(8,128)S(1)} %get-tuple-element.72), channel_id=1, source_target_pairs={{0,1},{1,0},{2,3},{3,2},{4,5},{5,4},{6,7},{7,6},{8,9},{9,8},{10,11... | collective-permute-start | bytes 147464 | tf_op jit(solution)/shard_map/ppermute | solution.py:799
  30.5 1.5 %collective-permute-start.10 = (f32[8,512]{1,0:T(8,128)S(1)}, f32[8,512]{1,0:T(8,128)S(1)}, u32[]{:S(2)}, u32[]{:S(2)}) collective-permute-start(f32[8,512]{1,0:T(8,128)S(1)} %get-tuple-element.70), channel_id=1, source_target_pairs={{0,32},{32,0},{64,96},{96,64},{128,160},{160,128},{192,224},{224,1... | collective-permute-start | bytes 49160 | tf_op jit(solution)/shard_map/ppermute | solution.py:799
  31.9 2.7 %collective-permute-start.11 = (f32[8,512]{1,0:T(8,128)S(1)}, f32[8,512]{1,0:T(8,128)S(1)}, u32[]{:S(2)}, u32[]{:S(2)}) collective-permute-start(f32[8,512]{1,0:T(8,128)S(1)} %get-tuple-element.71), channel_id=1, source_target_pairs={{32,64},{64,32},{96,128},{128,96},{160,192},{192,160},{224,0},{0,2... | collective-permute-start | bytes 49160 | tf_op jit(solution)/shard_map/ppermute | solution.py:799
  34.6 1.3 %repack.1 = (bf16[5,5,5,5,3,128]{5,4,3,2,1,0:T(4,128)(2,1)}, f32[8,128]{1,0:T(8,128)S(1)}) custom-call(f32[375,8,128]{2,1,0:T(8,128)S(1)} %get-tuple-element.74.dense), custom_call_target="tpu_custom_call" | custom-call | flops 1000000 | bytes 500000 | tf_op jit(solution)/shard_map/repack/pallas_call | solution.py:782
  36.0 0.3 third.1
  36.3 1.4 %collective-permute-start.13 = (f32[32,512]{1,0:T(8,128)S(1)}, f32[32,512]{1,0:T(8,128)S(1)}, u32[]{:S(2)}, u32[]{:S(2)}) collective-permute-start(f32[32,512]{1,0:T(8,128)S(1)} %get-tuple-element.79), channel_id=1, source_target_pairs={{1,2},{2,1},{3,4},{4,3},{5,6},{6,5},{7,8},{8,7},{9,10},{10,9},{11,... | collective-permute-start | bytes 196616 | tf_op jit(solution)/shard_map/ppermute | solution.py:799
  37.6 1.5 %collective-permute-start.15 = (f32[24,512]{1,0:T(8,128)S(1)}, f32[24,512]{1,0:T(8,128)S(1)}, u32[]{:S(2)}, u32[]{:S(2)}) collective-permute-start(f32[24,512]{1,0:T(8,128)S(1)} %get-tuple-element.80), channel_id=1, source_target_pairs={{32,64},{64,32},{96,128},{128,96},{160,192},{192,160},{224,0},{0,2... | collective-permute-start | bytes 147464 | tf_op jit(solution)/shard_map/ppermute | solution.py:799
  39.1 1.9 %collective-permute-start.16 = (f32[8,512]{1,0:T(8,128)S(1)}, f32[8,512]{1,0:T(8,128)S(1)}, u32[]{:S(2)}, u32[]{:S(2)}) collective-permute-start(f32[8,512]{1,0:T(8,128)S(1)} %get-tuple-element.81), channel_id=1, source_target_pairs={{0,1},{1,0},{2,3},{3,2},{4,5},{5,4},{6,7},{7,6},{8,9},{9,8},{10,11... | collective-permute-start | bytes 49160 | tf_op jit(solution)/shard_map/ppermute | solution.py:799
  41.0 0.7 density.1
  42.0 0.3 moments.1
  42.4 23.6 %all_to_all.11 = f32[256,1,128]{2,1,0:T(1,128)S(1)} all-to-all(f32[256,1,128]{2,1,0:T(1,128)S(1)} %bitcast.15), channel_id=1, replica_groups=mesh['lat'=8,'lon'=32] {'lat','lon'}, dimensions={0} | all-to-all | bytes 262144 | tf_op jit(solution)/shard_map/all_to_all | solution.py:915
  66.0 1.1 %final.1 = (f32[4,4,512]{2,1,0:T(4,128)}, f32[3,4,4,512]{3,2,1,0:T(4,128)}, f32[3,4,4,512]{3,2,1,0:T(4,128)}) custom-call(f32[256,128]{1,0:T(8,128)S(1)} %bitcast.14, f32[4,4,512]{2,1,0:T(4,128)S(1)} %get-tuple-element.48.phi, f32[4,4,512]{2,1,0:T(4,128)S(1)} %get-tuple-element.56.field.w0, f32[4,4,512]{2,1,0:T(4,128)S(1)} %get-tuple-element.68.field.w1, ...), custom_call_target="tpu_custom_call" | custom-call | flops 1000000 | bytes 500000 | tf_op jit(solution)/shard_map/final/pallas_call | solution.py:782
  (29 shorter events, 1.1 us)
Async XLA Ops:
  1.8 13.2 %collective-permute-start = (f32[16,512]{1,0:T(8,128)S(1)}, f32[16,512]{1,0:T(8,128)S(1)}, u32[]{:S(2)}, u32[]{:S(2)}) collective-permute-start(f32[16,512]{1,0:T(8,128)S(1)} %get-tuple-element.50), channel_id=1, source_target_pairs={{1,2},{2,1},{3,4},{4,3},{5,6},{6,5},{7,8},{8,7},{9,10},{10,9},{11,... | collective-permute-start | bytes 98312 | tf_op jit(solution)/shard_map/ppermute | solution.py:799
  4.6 10.4 %collective-permute-start.1 = (f32[16,512]{1,0:T(8,128)S(1)}, f32[16,512]{1,0:T(8,128)S(1)}, u32[]{:S(2)}, u32[]{:S(2)}) collective-permute-start(f32[16,512]{1,0:T(8,128)S(1)} %get-tuple-element.51), channel_id=1, source_target_pairs={{0,1},{1,0},{2,3},{3,2},{4,5},{5,4},{6,7},{7,6},{8,9},{9,8},{10,11... | collective-permute-start | bytes 98312 | tf_op jit(solution)/shard_map/ppermute | solution.py:799
  8.1 9.7 %collective-permute-start.3 = (f32[16,512]{1,0:T(8,128)S(1)}, f32[16,512]{1,0:T(8,128)S(1)}, u32[]{:S(2)}, u32[]{:S(2)}) collective-permute-start(f32[16,512]{1,0:T(8,128)S(1)} %get-tuple-element.54), channel_id=1, source_target_pairs={{0,224},{32,0},{64,32},{96,64},{128,96},{160,128},{192,160},{224,1... | collective-permute-start | bytes 98312 | tf_op jit(solution)/shard_map/ppermute | solution.py:803
  15.1 4.1 %collective-permute-start.2 = (f32[16,512]{1,0:T(8,128)S(1)}, f32[16,512]{1,0:T(8,128)S(1)}, u32[]{:S(2)}, u32[]{:S(2)}) collective-permute-start(f32[16,512]{1,0:T(8,128)S(1)} %get-tuple-element.53), channel_id=1, source_target_pairs={{0,32},{32,64},{64,96},{96,128},{128,160},{160,192},{192,224},{224... | collective-permute-start | bytes 98312 | tf_op jit(solution)/shard_map/ppermute | solution.py:803
  15.2 11.2 %collective-permute-start.8 = (f32[8,512]{1,0:T(8,128)S(1)}, f32[8,512]{1,0:T(8,128)S(1)}, u32[]{:S(2)}, u32[]{:S(2)}) collective-permute-start(f32[8,512]{1,0:T(8,128)S(1)} %get-tuple-element.62), channel_id=1, source_target_pairs={{0,224},{32,0},{64,32},{96,64},{128,96},{160,128},{192,160},{224,1... | collective-permute-start | bytes 49160 | tf_op jit(solution)/shard_map/ppermute | solution.py:803
  19.7 8.5 %collective-permute-start.4 = (f32[8,512]{1,0:T(8,128)S(1)}, f32[8,512]{1,0:T(8,128)S(1)}, u32[]{:S(2)}, u32[]{:S(2)}) collective-permute-start(f32[8,512]{1,0:T(8,128)S(1)} %get-tuple-element.58), channel_id=1, source_target_pairs={{1,2},{2,1},{3,4},{4,3},{5,6},{6,5},{7,8},{8,7},{9,10},{10,9},{11,... | collective-permute-start | bytes 49160 | tf_op jit(solution)/shard_map/ppermute | solution.py:799
  19.8 8.4 %collective-permute-start.6 = (f32[8,512]{1,0:T(8,128)S(1)}, f32[8,512]{1,0:T(8,128)S(1)}, u32[]{:S(2)}, u32[]{:S(2)}) collective-permute-start(f32[8,512]{1,0:T(8,128)S(1)} %get-tuple-element.60), channel_id=1, source_target_pairs={{32,64},{64,32},{96,128},{128,96},{160,192},{192,160},{224,0},{0,2... | collective-permute-start | bytes 49160 | tf_op jit(solution)/shard_map/ppermute | solution.py:799
  19.9 8.3 %collective-permute-start.7 = (f32[8,512]{1,0:T(8,128)S(1)}, f32[8,512]{1,0:T(8,128)S(1)}, u32[]{:S(2)}, u32[]{:S(2)}) collective-permute-start(f32[8,512]{1,0:T(8,128)S(1)} %get-tuple-element.61), channel_id=1, source_target_pairs={{0,1},{1,0},{2,3},{3,2},{4,5},{5,4},{6,7},{7,6},{8,9},{9,8},{10,11... | collective-permute-start | bytes 49160 | tf_op jit(solution)/shard_map/ppermute | solution.py:799
  24.4 3.8 %collective-permute-start.5 = (f32[8,512]{1,0:T(8,128)S(1)}, f32[8,512]{1,0:T(8,128)S(1)}, u32[]{:S(2)}, u32[]{:S(2)}) collective-permute-start(f32[8,512]{1,0:T(8,128)S(1)} %get-tuple-element.59._), channel_id=1, source_target_pairs={{0,32},{32,0},{64,96},{96,64},{128,160},{160,128},{192,224},{224,1... | collective-permute-start | bytes 49160 | tf_op jit(solution)/shard_map/ppermute | solution.py:799
  24.4 1.1 %copy-start = (bf16[3,5,5,1,5,1,5,128]{7,0,6,5,4,3,2,1:T(4,128)(2,1)S(1)}, bf16[3,5,5,1,5,1,5,128]{7,0,6,5,4,3,2,1:T(4,128)(2,1)}, u32[]{:S(2)}) copy-start(bf16[3,5,5,1,5,1,5,128]{7,0,6,5,4,3,2,1:T(4,128)(2,1)} %param.15) | copy-start | bytes 1440004
  28.2 37.7 %copy-start.1 = (f32[3,4,4,512]{3,2,1,0:T(4,128)S(1)}, f32[3,4,4,512]{3,2,1,0:T(4,128)}, u32[]{:S(2)}) copy-start(f32[3,4,4,512]{3,2,1,0:T(4,128)} %vel.1) | copy-start | bytes 294916
  28.2 37.7 %copy-start.2 = (f32[3,4,4,512]{3,2,1,0:T(4,128)S(1)}, f32[3,4,4,512]{3,2,1,0:T(4,128)}, u32[]{:S(2)}) copy-start(f32[3,4,4,512]{3,2,1,0:T(4,128)} %acc.1) | copy-start | bytes 294916
  28.5 7.4 %collective-permute-start.9 = (f32[24,512]{1,0:T(8,128)S(1)}, f32[24,512]{1,0:T(8,128)S(1)}, u32[]{:S(2)}, u32[]{:S(2)}) collective-permute-start(f32[24,512]{1,0:T(8,128)S(1)} %get-tuple-element.69), channel_id=1, source_target_pairs={{1,2},{2,1},{3,4},{4,3},{5,6},{6,5},{7,8},{8,7},{9,10},{10,9},{11,... | collective-permute-start | bytes 147464 | tf_op jit(solution)/shard_map/ppermute | solution.py:799
  28.6 7.3 %collective-permute-start.12 = (f32[24,512]{1,0:T(8,128)S(1)}, f32[24,512]{1,0:T(8,128)S(1)}, u32[]{:S(2)}, u32[]{:S(2)}) collective-permute-start(f32[24,512]{1,0:T(8,128)S(1)} %get-tuple-element.72), channel_id=1, source_target_pairs={{0,1},{1,0},{2,3},{3,2},{4,5},{5,4},{6,7},{7,6},{8,9},{9,8},{10,11... | collective-permute-start | bytes 147464 | tf_op jit(solution)/shard_map/ppermute | solution.py:799
  30.5 5.5 %collective-permute-start.10 = (f32[8,512]{1,0:T(8,128)S(1)}, f32[8,512]{1,0:T(8,128)S(1)}, u32[]{:S(2)}, u32[]{:S(2)}) collective-permute-start(f32[8,512]{1,0:T(8,128)S(1)} %get-tuple-element.70), channel_id=1, source_target_pairs={{0,32},{32,0},{64,96},{96,64},{128,160},{160,128},{192,224},{224,1... | collective-permute-start | bytes 49160 | tf_op jit(solution)/shard_map/ppermute | solution.py:799
  31.9 4.0 %collective-permute-start.11 = (f32[8,512]{1,0:T(8,128)S(1)}, f32[8,512]{1,0:T(8,128)S(1)}, u32[]{:S(2)}, u32[]{:S(2)}) collective-permute-start(f32[8,512]{1,0:T(8,128)S(1)} %get-tuple-element.71), channel_id=1, source_target_pairs={{32,64},{64,32},{96,128},{128,96},{160,192},{192,160},{224,0},{0,2... | collective-permute-start | bytes 49160 | tf_op jit(solution)/shard_map/ppermute | solution.py:799
  36.3 5.8 %collective-permute-start.13 = (f32[32,512]{1,0:T(8,128)S(1)}, f32[32,512]{1,0:T(8,128)S(1)}, u32[]{:S(2)}, u32[]{:S(2)}) collective-permute-start(f32[32,512]{1,0:T(8,128)S(1)} %get-tuple-element.79), channel_id=1, source_target_pairs={{1,2},{2,1},{3,4},{4,3},{5,6},{6,5},{7,8},{8,7},{9,10},{10,9},{11,... | collective-permute-start | bytes 196616 | tf_op jit(solution)/shard_map/ppermute | solution.py:799
  37.6 4.2 %collective-permute-start.15 = (f32[24,512]{1,0:T(8,128)S(1)}, f32[24,512]{1,0:T(8,128)S(1)}, u32[]{:S(2)}, u32[]{:S(2)}) collective-permute-start(f32[24,512]{1,0:T(8,128)S(1)} %get-tuple-element.80), channel_id=1, source_target_pairs={{32,64},{64,32},{96,128},{128,96},{160,192},{192,160},{224,0},{0,2... | collective-permute-start | bytes 147464 | tf_op jit(solution)/shard_map/ppermute | solution.py:799
  39.1 2.9 %collective-permute-start.14 = (f32[24,512]{1,0:T(8,128)S(1)}, f32[24,512]{1,0:T(8,128)S(1)}, u32[]{:S(2)}, u32[]{:S(2)}) collective-permute-start(f32[24,512]{1,0:T(8,128)S(1)} %get-tuple-element.76._), channel_id=1, source_target_pairs={{0,32},{32,0},{64,96},{96,64},{128,160},{160,128},{192,224},{224,1... | collective-permute-start | bytes 147464 | tf_op jit(solution)/shard_map/ppermute | solution.py:799
  39.1 2.8 %collective-permute-start.16 = (f32[8,512]{1,0:T(8,128)S(1)}, f32[8,512]{1,0:T(8,128)S(1)}, u32[]{:S(2)}, u32[]{:S(2)}) collective-permute-start(f32[8,512]{1,0:T(8,128)S(1)} %get-tuple-element.81), channel_id=1, source_target_pairs={{0,1},{1,0},{2,3},{3,2},{4,5},{5,4},{6,7},{7,6},{8,9},{9,8},{10,11... | collective-permute-start | bytes 49160 | tf_op jit(solution)/shard_map/ppermute | solution.py:799
